TPU v7x, 768 devices: a whole 4x8x12 slice. The times are simulated.
768 devices in a mesh: gx: 32 (over x, z_hi, core), gy: 24 (over z_lo, y).
Axes of the slice: x: 4, y: 8, z: 12 (z_hi: 4, z_lo: 3; z = z_hi * 3 + z_lo), core: 2. Of those that a mesh axis runs over, the one named last changes fastest.
Arguments:
- fine_residual: float32 [5, 1536, 12288], P(None, 'gx', 'gy'), may hold values from -0.6 to 0.6
- owner_map: int32 [1536, 12288], P('gx', 'gy'), may hold values from 0 to 6143, as said below
- boundary_flags: int32 [768, 6144], P('gx', 'gy'), may hold values from 0 to 2
- jacobian: float32 [5, 5, 768, 6144], P(None, None, 'gx', 'gy'), may hold values from -0.6 to 20
- line_coef: float32 [5, 192, 1536], P(None, 'gx', 'gy'), may hold values from 2.0001 to 2.003
Outputs:
- correction: float32 [5, 768, 6144], P(None, 'gx', 'gy')
- level_residual: float32 [5, 768, 6144], P(None, 'gx', 'gy')
Inputs may be any that keep to these rules, and one draw needn't show every extreme that they name: `owner_map`: each level-0 cell names a level-1 cell of its own device's tile of 24 x 256 cells, numbered row by row, at most one cell away in each direction from the cell covering its own position.
All inputs are finite; a program needn't handle non-finite values.
Results may differ from a plain program's by a relative error of at most 0.0003.
Values sent between devices are 32-bit elements; how exact they have to be, the bound alone decides.
No kernel may reach another device: no remote copies, remote signals or barrier semaphores. Data moves between devices by JAX's collectives and lax.ppermute only.
A program may use at most 64 MiB of HBM per device.

v0:
```python
import jax
import jax.numpy as jnp
from jax import lax
from jax.experimental import pallas as pl
from jax.experimental.pallas import tpu as pltpu
from jax.sharding import PartitionSpec as P

F = 5
TX = 24
TY = 256
EX = 40
EY = 384
ROWS = 6
PLANES = 31
HIGH = lax.Precision.HIGHEST
F32 = jnp.float32


def iota(shape, dim):
    return lax.broadcasted_iota(jnp.int32, shape, dim)


def dot(a, b):
    return jnp.dot(a, b, precision=HIGH, preferred_element_type=F32)


def roll(x, shift, axis):
    shift = shift % x.shape[axis]
    return x if shift == 0 else pltpu.roll(x, shift, axis)


def restrict_kernel(fine, owner, flags, jac, coef, rhs, top, bottom, left, right, tiles, owners):
    def halves(source, tile):
        for j in range(4):
            tile[j] = source[:, 128 * j : 128 * (j + 1)]
        return [
            jnp.concatenate([tile[j, pl.ds(start, TX, 2), :] for j in range(4)], axis=1)
            for start in (0, 1)
        ]

    shape = (TX, 2 * TY)
    row = iota(shape, 0)
    col = iota(shape, 1) // 2
    codes = [
        ((o // TY) - row + 1) * 3 + (o % TY) - col + 1
        for o in halves(owner, owners)
    ]
    masks = [[code == k for code in codes] for k in range(9)]
    gathered = []
    for f in range(F):
        values = halves(fine.at[f], tiles.at[f])
        total = None
        for dy in (-1, 0, 1):
            part = None
            for dx in (-1, 0, 1):
                mask = masks[(dx + 1) * 3 + dy + 1]
                moved = jnp.where(mask[0], values[0], 0.0) + jnp.where(mask[1], values[1], 0.0)
                moved = roll(moved, dx, 0)
                part = moved if part is None else part + moved
            part = roll(part, 2 * dy, 1)
            total = part if total is None else total + part
        gathered.append(total)
    pairs = (iota((2 * TY, TY), 0) // 2 == iota((2 * TY, TY), 1)).astype(F32)
    summed = dot(jnp.concatenate(gathered, axis=0), pairs)
    planes = [summed[TX * f : TX * (f + 1)] for f in range(F)]
    for f in range(F):
        rhs[f] = planes[f]
    planes.append((flags[...] + 1).astype(F32))
    for p in range(F + 1):
        for j in range(2):
            lanes = slice(128 * j, 128 * (j + 1))
            top[2 * p + j] = planes[p][0:8, lanes]
            bottom[2 * p + j] = planes[p][TX - 8 : TX, lanes]
    slot = iota((TX, 128), 1) // 8
    for a in range(2):
        first = jnp.zeros((TX, 128), F32)
        last = jnp.zeros((TX, 128), F32)
        for t in range(16):
            p = 16 * a + t
            if p >= PLANES:
                continue
            if p < F * F:
                head, tail = jac[p // F, p % F, :, 0:128], jac[p // F, p % F, :, TY - 128 : TY]
            else:
                head, tail = planes[p - F * F][:, 0:128], planes[p - F * F][:, TY - 128 : TY]
            first = jnp.where(slot == t, roll(head, 8 * t, 1), first)
            last = jnp.where(slot == t, roll(tail, 8 * t - 120, 1), last)
        left[a] = first
        right[a] = last
    lane = iota((ROWS, 128), 1)
    first = left[1, 0:ROWS, :]
    last = right[1, 0:ROWS, :]
    for f in range(F):
        wide = jnp.concatenate([coef[f], coef[f]], axis=1)
        first = jnp.where(lane == 120 + f, roll(wide, 120 + f, 1), first)
        last = jnp.where(lane == 120 + f, roll(wide, 120 + f - 63, 1), last)
    left[1, 0:ROWS, :] = first
    right[1, 0:ROWS, :] = last


def extended_planes(jac, jac_up, jac_down, rhs, flags, up, down, beside):
    def whole(upper, own, lower, aside):
        return jnp.concatenate([jnp.concatenate([upper, own, lower], axis=0), aside], axis=1)

    def strip(ref, p):
        return jnp.concatenate([ref[2 * p], ref[2 * p + 1]], axis=1)

    def jac_plane(f, g):
        return whole(jac_up[f, g], jac[f, g], jac_down[f, g], beside[f * F + g])

    def rhs_plane(f):
        return whole(strip(up, f), rhs[f], strip(down, f), beside[F * F + f])

    def code_plane():
        return whole(strip(up, F), (flags[...] + 1).astype(F32), strip(down, F), beside[F * F + F])

    return jac_plane, rhs_plane, code_plane


def scaled_planes(code, jac_plane):
    plain = (code == 1.0) | (code == 3.0)
    interior = code == 1.0
    kept = [interior if f in (1, 2) else plain for f in range(F)]
    return kept, [jnp.where(kept[f], 0.8 / jac_plane(f, f), 0.0) for f in range(F)]


def residual(f, state, rhs_plane, jac_plane):
    own = state[f]
    beside = roll(own, 1, 0) + roll(own, -1, 0) + roll(own, 1, 1) + roll(own, -1, 1)
    total = rhs_plane(f) + beside
    for g in range(F):
        total = total - jac_plane(f, g) * state[g]
    return total


def sweep(old, new, scaled, rhs_plane, jac_plane):
    for f in range(F):
        new[f] = old[f] + scaled[f] * residual(f, old, rhs_plane, jac_plane)


def columns(shape, fine_dim, coarse_dim):
    fine = iota(shape, fine_dim)
    coarse = iota(shape, coarse_dim)
    here = (coarse <= 64) & (fine // 4 == coarse)
    return (here | ((coarse == 65) & (fine >= EY - 4))).astype(F32)


def before_kernel(
    jac, jac_up, jac_down, rhs, flags, up, down, from_right, from_left, coef,
    state, beside, scaled, lines, sent, other, block, diag,
):
    lane = iota((EX, 128), 1)
    for a in range(2):
        right = jnp.concatenate([up[12 + a], from_right[a], down[12 + a]], axis=0)
        left = jnp.concatenate([up[14 + a], from_left[a], down[14 + a]], axis=0)
        for t in range(16):
            p = 16 * a + t
            if p < PLANES:
                beside[p] = jnp.where(
                    lane < 8,
                    roll(right, -8 * t, 1),
                    jnp.where(lane >= 120, roll(left, 120 - 8 * t, 1), 0.0),
                )
    jac_plane, rhs_plane, code_plane = extended_planes(
        jac, jac_up, jac_down, rhs, flags, up, down, beside
    )
    _, scale = scaled_planes(code_plane(), jac_plane)
    for f in range(F):
        scaled[f] = scale[f]
        state[f] = scale[f] * rhs_plane(f)
    sweep(state, other, scaled, rhs_plane, jac_plane)
    sweep(other, state, scaled, rhs_plane, jac_plane)
    left_over = jnp.concatenate(
        [residual(f, state, rhs_plane, jac_plane)[8 : 8 + TX] for f in range(F)], axis=0
    )
    by_column = dot(left_over, columns((EY, 128), 0, 1))
    shape = (8 * ROWS, F * TX)
    to, of = iota(shape, 0), iota(shape, 1)
    of_field = (of * 2731) >> 16
    chosen = (to % 8 == of_field) & (to // 8 == (of - TX * of_field) // 4)
    mean = dot(jnp.where(chosen, 0.0625, 0.0), by_column)

    row_lane = iota((ROWS, 128), 1)
    near, far = from_right[1, 0:ROWS, :], from_left[1, 0:ROWS, :]
    diag[...] = jnp.full((8 * ROWS, 128), 4.0, F32)
    for f in range(F):
        wide = jnp.concatenate([coef[f], coef[f]], axis=1)
        wide = jnp.where(row_lane == 64, roll(near, 64 - 120 - f, 1), wide)
        wide = jnp.where(row_lane == 65, roll(far, 65 - 120 - f, 1), wide)
        wide = jnp.where((row_lane <= 65) & (wide > 0.0), wide, 4.0)
        for k in range(ROWS):
            diag[8 * k + f : 8 * k + f + 1, :] = wide[k : k + 1, :]

    value, low, high = [], [], []
    for k in range(ROWS):
        here = mean[8 * k : 8 * k + 8]
        d = diag[8 * k : 8 * k + 8, :]
        if k == 0:
            inverse = 1.0 / d
            value.append(here * inverse)
            low.append(inverse)
        else:
            inverse = 1.0 / (d - high[-1])
            value.append((here + value[-1]) * inverse)
            low.append(low[-1] * inverse)
        high.append(inverse)
    for k in range(ROWS):
        lines[0, 8 * k : 8 * k + 8] = value[k]
        lines[1, 8 * k : 8 * k + 8] = low[k]
        lines[2, 8 * k : 8 * k + 8] = high[k]
    first, first_low = value[-1], low[-1]
    for k in range(ROWS - 2, -1, -1):
        first = value[k] + high[k] * first
        first_low = low[k] + high[k] * first_low
    parts = [first, value[-1], first_low, low[-1], high[-1]]
    lane = iota((8, 128), 1)
    ends = parts[0]
    for q in range(1, 5):
        ends = jnp.where(lane // 2 == 32 + q, roll(parts[q], 2 * q, 1), ends)
    block[...] = jnp.zeros((16, 128), F32)
    block[0:F] = jnp.where(lane < 64, parts[0], roll(parts[1], 64, 1))[0:F]
    block[F : 2 * F] = jnp.where(lane < 64, parts[2], roll(parts[3], 64, 1))[0:F]
    block[2 * F : 3 * F] = jnp.where(lane < 64, parts[4], ends)[0:F]
    whole = block[...]
    for k in range(sent.shape[0]):
        sent[k] = whole


def after_kernel(
    jac, jac_up, jac_down, rhs, flags, up, down, state_in, beside, scaled, lines, got, place,
    correction, level_residual, state, other, ends,
):
    count = got.shape[0]
    me = place[0]
    lane = iota((F, 128), 1)

    def segment(k):
        one, two, three = got[k, 0:F, :], got[k, F : 2 * F, :], got[k, 2 * F : 3 * F, :]
        main = [one, roll(one, 64, 1), two, roll(two, 64, 1), three]
        return [jnp.where(lane < 64, main[q], roll(three, -2 * q, 1)) for q in range(5)]

    def step(p, q, near, far, turn, through, back):
        w = q / (1.0 - turn * q)
        return far + through * (p + w * (near + turn * p)), back + through * through * w

    zero = jnp.zeros((F, 128), F32)
    p_low = q_low = p_high = q_high = zero
    for k in range(count - 1):
        a0, a1, b0, c, c1 = segment(k)
        p, q = step(p_low, q_low, a0, a1, b0, c, c1)
        p_low, q_low = jnp.where(k < me, p, p_low), jnp.where(k < me, q, q_low)
        j = count - 1 - k
        a0, a1, b0, c, c1 = segment(j)
        p, q = step(p_high, q_high, a1, a0, c1, c, b0)
        p_high, q_high = jnp.where(j > me, p, p_high), jnp.where(j > me, q, q_high)
    a0, a1, b0, c, c1 = segment(me)
    p, q = step(p_low, q_low, a0, a1, b0, c, c1)
    last = (p + q * p_high) / (1.0 - q * q_high)
    above = p_high + q_high * last
    first = (a0 + b0 * p_low + c * above) / (1.0 - b0 * q_low)
    below = p_low + q_low * first

    ends[...] = jnp.zeros((64, 128), F32)
    used = lane <= 65
    ends[0:F] = jnp.where(used, below, 0.0)
    ends[8 * (ROWS + 1) : 8 * (ROWS + 1) + F] = jnp.where(used, above, 0.0)
    here = above
    for k in range(ROWS - 1, -1, -1):
        rows = slice(8 * k, 8 * k + F)
        here = lines[0, rows] + lines[1, rows] * below + lines[2, rows] * here
        ends[8 * (k + 1) : 8 * (k + 1) + F] = jnp.where(used, here, 0.0)

    shape = (F * EX, 64)
    to, of = iota(shape, 0), iota(shape, 1)
    to_field = (to * 1639) >> 16
    to_row = to - EX * to_field
    chosen = (to_field == of % 8) & (to_row >= 4) & (to_row < EX - 4)
    chosen = chosen & ((to_row - 4) // 4 == of // 8)
    spread = dot(dot(chosen.astype(F32), ends[...]), columns((128, EY), 1, 0))

    jac_plane, rhs_plane, code_plane = extended_planes(
        jac, jac_up, jac_down, rhs, flags, up, down, beside
    )
    code = code_plane()
    plain = (code == 1.0) | (code == 3.0)
    interior = code == 1.0
    for f in range(F):
        kept = interior if f in (1, 2) else plain
        state[f] = state_in[f] + jnp.where(kept, spread[EX * f : EX * (f + 1)], 0.0)
    sweep(state, other, scaled, rhs_plane, jac_plane)
    sweep(other, state, scaled, rhs_plane, jac_plane)
    for f in range(F):
        correction[f] = state[f, 8 : 8 + TX, 0:TY]
        left_over = residual(f, state, rhs_plane, jac_plane)
        level_residual[f] = left_over[8 : 8 + TX, 0:TY]


def shape_of(*dims):
    return jax.ShapeDtypeStruct(dims, F32)


def call(kernel, outs, scratch, *args, scalars=0):
    vmem = pl.BlockSpec(memory_space=pltpu.VMEM)
    specs = [vmem] * (len(args) - scalars) + [pl.BlockSpec(memory_space=pltpu.SMEM)] * scalars
    return pl.pallas_call(
        kernel,
        out_shape=outs,
        in_specs=specs,
        out_specs=[vmem] * len(outs),
        scratch_shapes=scratch,
        compiler_params=pltpu.CompilerParams(vmem_limit_bytes=48 * 1024 * 1024),
    )(*args)


def shift(value, axis, step):
    count = lax.axis_size(axis)
    pairs = [(i, i + step) for i in range(count) if 0 <= i + step < count]
    return lax.ppermute(value, axis, pairs)


def local(fine, owner, flags, jac, coef):
    jac_up = shift(jac[:, :, TX - 8 :], "gx", 1)
    jac_down = shift(jac[:, :, :8], "gx", -1)
    rhs, top, bottom, left, right = call(
        restrict_kernel,
        [shape_of(F, TX, TY), shape_of(12, 8, 128), shape_of(12, 8, 128), shape_of(2, TX, 128), shape_of(2, TX, 128)],
        [pltpu.VMEM((F, 4, 2 * TX, 128), F32), pltpu.VMEM((4, 2 * TX, 128), jnp.int32)],
        fine, owner, flags, jac, coef,
    )
    from_left = shift(right, "gy", 1)
    from_right = shift(left, "gy", -1)
    top = jnp.concatenate([top, from_right[:, :8], from_left[:, :8]], axis=0)
    bottom = jnp.concatenate([bottom, from_right[:, TX - 8 :], from_left[:, TX - 8 :]], axis=0)
    up = shift(bottom, "gx", 1)
    down = shift(top, "gx", -1)
    count = lax.axis_size("gx")
    state, beside, scaled, lines, sent = call(
        before_kernel,
        [shape_of(F, EX, EY), shape_of(PLANES, EX, 128), shape_of(F, EX, EY), shape_of(3, 8 * ROWS, 128), shape_of(count, 16, 128)],
        [pltpu.VMEM((F, EX, EY), F32), pltpu.VMEM((16, 128), F32), pltpu.VMEM((8 * ROWS, 128), F32)],
        jac, jac_up, jac_down, rhs, flags, up, down, from_right, from_left, coef,
    )
    got = lax.all_to_all(sent, "gx", 0, 0, tiled=True)
    place = lax.axis_index("gx").astype(jnp.int32).reshape(1)
    return tuple(
        call(
            after_kernel,
            [shape_of(F, TX, TY), shape_of(F, TX, TY)],
            [pltpu.VMEM((F, EX, EY), F32), pltpu.VMEM((F, EX, EY), F32), pltpu.VMEM((64, 128), F32)],
            jac, jac_up, jac_down, rhs, flags, up, down, state, beside, scaled, lines, got, place,
            scalars=1,
        )
    )


def solution(mesh):
    in_specs = (
        P(None, "gx", "gy"),
        P("gx", "gy"),
        P("gx", "gy"),
        P(None, None, "gx", "gy"),
        P(None, "gx", "gy"),
    )
    out_specs = (P(None, "gx", "gy"), P(None, "gx", "gy"))
    return jax.shard_map(local, mesh=mesh, in_specs=in_specs, out_specs=out_specs, check_vma=False)
```

profile of v0, /device:TPU:25, one launch (start us, length us, event | category | flops | bytes accessed | tf_op | source)
XLA Modules:
  0.0 79.7 jit_solution(11373011354153207492)
XLA Ops:
  0.6 0.0 copy-start
  0.6 1.1 %copy-done = f32[5,5,24,256]{3,2,1,0:T(8,128)S(1)} copy-done((f32[5,5,24,256]{3,2,1,0:T(8,128)S(1)}, f32[5,5,24,256]{3,2,1,0:T(8,128)}, u32[]{:S(2)}) %copy-start) | copy-done | bytes 614424
  1.7 0.0 copy-start.2
  1.7 1.0 %copy-done.2 = f32[5,48,512]{2,1,0:T(8,128)S(1)} copy-done((f32[5,48,512]{2,1,0:T(8,128)S(1)}, f32[5,48,512]{2,1,0:T(8,128)}, u32[]{:S(2)}) %copy-start.2) | copy-done | bytes 491544
  2.7 0.0 copy-start.3
  2.7 0.7 copy-done.3
  3.5 0.0 copy-start.5
  3.5 0.9 %copy-done.5 = s32[48,512]{1,0:T(8,128)S(1)} copy-done((s32[48,512]{1,0:T(8,128)S(1)}, s32[48,512]{1,0:T(8,128)}, u32[]{:S(2)}) %copy-start.5) | copy-done | bytes 98328
  4.4 0.0 copy-start.6
  4.4 0.7 copy-done.6
  5.1 1.2 %shard_map.68 = (f32[5,24,256]{2,1,0:T(8,128)S(1)}, f32[12,8,128]{2,1,0:T(8,128)S(1)}, f32[12,8,128]{2,1,0:T(8,128)S(1)}, f32[2,24,128]{2,1,0:T(8,128)S(1)}, f32[2,24,128]{2,1,0:T(8,128)S(1)}) custom-call(f32[5,48,512]{2,1,0:T(8,128)S(1)} %copy-done.2, s32[48,512]{1,0:T(8,128)S(1)} %copy-done.5, s32[24,256]{1,0:T(8,128)S(1)} %copy-done.3, ...), custom_call_target="tpu_custom_call" | custom-call | tf_op jit(solution)/shard_map/pallas_call | solution.py:305
  6.3 0.0 copy-start.1
  6.4 4.5 %collective-permute-start.3 = (f32[2,24,128]{2,1,0:T(8,128)S(1)}, f32[2,24,128]{2,1,0:T(8,128)S(1)}, u32[]{:S(2)}, u32[]{:S(2)}) collective-permute-start(f32[2,24,128]{2,1,0:T(8,128)S(1)} %get-tuple-element.15), channel_id=1, source_target_pairs={{0,1},{1,2},{2,3},{3,4},{4,5},{5,6},{6,7},{7,8},{8,9},{9,10},{10,1... | collective-permute-start | bytes 73736 | tf_op jit(solution)/shard_map/ppermute | solution.py:318
  10.9 8.5 %collective-permute-start = (f32[5,5,8,256]{3,2,1,0:T(8,128)S(1)}, f32[5,5,8,256]{3,2,1,0:T(8,128)S(1)}, u32[]{:S(2)}, u32[]{:S(2)}) collective-permute-start(f32[5,5,8,256]{3,2,1,0:T(8,128)S(1)} %get-tuple-element.23), channel_id=1, source_target_pairs={{0,24},{24,48},{48,72},{72,96},{96,120},{120,144},{144,168},{168,1... | collective-permute-start | bytes 614408 | tf_op jit(solution)/shard_map/ppermute | solution.py:318
  19.4 1.9 %collective-permute-start.1 = (f32[5,5,8,256]{3,2,1,0:T(8,128)S(1)}, f32[5,5,8,256]{3,2,1,0:T(8,128)S(1)}, u32[]{:S(2)}, u32[]{:S(2)}) collective-permute-start(f32[5,5,8,256]{3,2,1,0:T(8,128)S(1)} %get-tuple-element.22), channel_id=1, source_target_pairs={{24,0},{48,24},{72,48},{96,72},{120,96},{144,120},{168,144},{192,1... | collective-permute-start | bytes 614408 | tf_op jit(solution)/shard_map/ppermute | solution.py:318
  21.3 1.9 %collective-permute-start.2 = (f32[2,24,128]{2,1,0:T(8,128)S(1)}, f32[2,24,128]{2,1,0:T(8,128)S(1)}, u32[]{:S(2)}, u32[]{:S(2)}) collective-permute-start(f32[2,24,128]{2,1,0:T(8,128)S(1)} %get-tuple-element.14), channel_id=1, source_target_pairs={{1,0},{2,1},{3,2},{4,3},{5,4},{6,5},{7,6},{8,7},{9,8},{10,9},{11,1... | collective-permute-start | bytes 73736 | tf_op jit(solution)/shard_map/ppermute | solution.py:318
  23.3 0.0 collective-permute-done.3.from_left
  23.3 3.8 %collective-permute-done.2.from_right = f32[2,24,128]{2,1,0:T(8,128)S(1)} collective-permute-done((f32[2,24,128]{2,1,0:T(8,128)S(1)}, f32[2,24,128]{2,1,0:T(8,128)S(1)}, u32[]{:S(2)}, u32[]{:S(2)}) %collective-permute-start.2) | collective-permute-done | bytes 24608 | tf_op jit(solution)/shard_map/ppermute | solution.py:318
  27.1 6.6 %collective-permute-start.4 = (f32[16,8,128]{2,1,0:T(8,128)S(1)}, f32[16,8,128]{2,1,0:T(8,128)S(1)}, u32[]{:S(2)}, u32[]{:S(2)}) collective-permute-start(f32[16,8,128]{2,1,0:T(8,128)S(1)} %pad_maximum_fusion), channel_id=1, source_target_pairs={{0,24},{24,48},{48,72},{72,96},{96,120},{120,144},{144,168},{168,1... | collective-permute-start | bytes 196616 | tf_op jit(solution)/shard_map/ppermute | solution.py:318
  33.7 1.9 %collective-permute-start.5 = (f32[16,8,128]{2,1,0:T(8,128)S(1)}, f32[16,8,128]{2,1,0:T(8,128)S(1)}, u32[]{:S(2)}, u32[]{:S(2)}) collective-permute-start(f32[16,8,128]{2,1,0:T(8,128)S(1)} %pad_maximum_fusion.1), channel_id=1, source_target_pairs={{24,0},{48,24},{72,48},{96,72},{120,96},{144,120},{168,144},{192,1... | collective-permute-start | bytes 196616 | tf_op jit(solution)/shard_map/ppermute | solution.py:318
  35.7 0.0 collective-permute-done.4.up
  35.7 5.4 %collective-permute-done.5.down = f32[16,8,128]{2,1,0:T(8,128)S(1)} collective-permute-done((f32[16,8,128]{2,1,0:T(8,128)S(1)}, f32[16,8,128]{2,1,0:T(8,128)S(1)}, u32[]{:S(2)}, u32[]{:S(2)}) %collective-permute-start.5) | collective-permute-done | bytes 65568 | tf_op jit(solution)/shard_map/ppermute | solution.py:318
  41.1 0.0 collective-permute-done.jac_up
  41.1 0.0 collective-permute-done.1.jac_down
  41.1 0.0 copy-done.1
  41.1 2.5 %shard_map.69 = (f32[5,40,384]{2,1,0:T(8,128)S(1)}, f32[31,40,128]{2,1,0:T(8,128)S(1)}, f32[5,40,384]{2,1,0:T(8,128)S(1)}, f32[3,48,128]{2,1,0:T(8,128)S(1)}, f32[32,16,128]{2,1,0:T(8,128)}) custom-call(f32[5,5,24,256]{3,2,1,0:T(8,128)S(1)} %copy-done.1, f32[5,5,8,256]{3,2,1,0:T(8,128)S(1)} %collective-permute-done.jac_up, ...), custom_call_target="tpu_custom_call" | custom-call | tf_op jit(solution)/shard_map/pallas_call | solution.py:305
  43.7 0.0 copy-start.4
  43.7 17.8 %all-to-all-start = ((f32[32,16,128]{2,1,0:T(8,128)}), f32[32,16,128]{2,1,0:T(8,128)S(1)}, u32[]{:S(2)}, u32[]{:S(2)}) async-start(f32[32,16,128]{2,1,0:T(8,128)} %get-tuple-element.21), calls=%async_computation | async-start | bytes 524288 | tf_op jit(solution)/shard_map/all_to_all | solution.py:343
  61.5 15.6 %all-to-all-done.got = f32[32,16,128]{2,1,0:T(8,128)S(1)} async-done(((f32[32,16,128]{2,1,0:T(8,128)}), f32[32,16,128]{2,1,0:T(8,128)S(1)}, u32[]{:S(2)}, u32[]{:S(2)}) %all-to-all-start) | async-done | bytes 262176 | tf_op jit(solution)/shard_map/all_to_all | solution.py:343
  77.1 0.0 copy-done.4
  77.1 2.5 %shard_map.70 = (f32[5,24,256]{2,1,0:T(8,128)}, f32[5,24,256]{2,1,0:T(8,128)}) custom-call(f32[5,5,24,256]{3,2,1,0:T(8,128)S(1)} %copy-done.1, f32[5,5,8,256]{3,2,1,0:T(8,128)S(1)} %collective-permute-done.jac_up, f32[5,5,8,256]{3,2,1,0:T(8,128)S(1)} %collective-permute-done.1.jac_down, f32[5,24,256]{2,1,0:T(8,128)S(1)} %get-tuple-element.12.rhs, ...), custom_call_target="tpu_custom_call" | custom-call | tf_op jit(solution)/shard_map/pallas_call | solution.py:305
  (5 shorter events, 0.0 us)
Async XLA Ops:
  0.6 1.1 %copy-start = (f32[5,5,24,256]{3,2,1,0:T(8,128)S(1)}, f32[5,5,24,256]{3,2,1,0:T(8,128)}, u32[]{:S(2)}) copy-start(f32[5,5,24,256]{3,2,1,0:T(8,128)} %jac.5) | copy-start | bytes 1843204
  1.7 1.0 %copy-start.2 = (f32[5,48,512]{2,1,0:T(8,128)S(1)}, f32[5,48,512]{2,1,0:T(8,128)}, u32[]{:S(2)}) copy-start(f32[5,48,512]{2,1,0:T(8,128)} %fine.1) | copy-start | bytes 1474564
  2.7 0.7 copy-start.3
  3.5 0.9 %copy-start.5 = (s32[48,512]{1,0:T(8,128)S(1)}, s32[48,512]{1,0:T(8,128)}, u32[]{:S(2)}) copy-start(s32[48,512]{1,0:T(8,128)} %owner.1) | copy-start | bytes 294916
  4.4 0.7 copy-start.6
  6.3 34.8 %copy-start.1 = (f32[5,5,24,256]{3,2,1,0:T(8,128)S(1)}, f32[5,5,24,256]{3,2,1,0:T(8,128)}, u32[]{:S(2)}) copy-start(f32[5,5,24,256]{3,2,1,0:T(8,128)} %jac.5) | copy-start | bytes 1843204
  6.4 16.9 %collective-permute-start.3 = (f32[2,24,128]{2,1,0:T(8,128)S(1)}, f32[2,24,128]{2,1,0:T(8,128)S(1)}, u32[]{:S(2)}, u32[]{:S(2)}) collective-permute-start(f32[2,24,128]{2,1,0:T(8,128)S(1)} %get-tuple-element.15), channel_id=1, source_target_pairs={{0,1},{1,2},{2,3},{3,4},{4,5},{5,6},{6,7},{7,8},{8,9},{9,10},{10,1... | collective-permute-start | bytes 73736 | tf_op jit(solution)/shard_map/ppermute | solution.py:318
  10.9 30.2 %collective-permute-start = (f32[5,5,8,256]{3,2,1,0:T(8,128)S(1)}, f32[5,5,8,256]{3,2,1,0:T(8,128)S(1)}, u32[]{:S(2)}, u32[]{:S(2)}) collective-permute-start(f32[5,5,8,256]{3,2,1,0:T(8,128)S(1)} %get-tuple-element.23), channel_id=1, source_target_pairs={{0,24},{24,48},{48,72},{72,96},{96,120},{120,144},{144,168},{168,1... | collective-permute-start | bytes 614408 | tf_op jit(solution)/shard_map/ppermute | solution.py:318
  19.4 21.7 %collective-permute-start.1 = (f32[5,5,8,256]{3,2,1,0:T(8,128)S(1)}, f32[5,5,8,256]{3,2,1,0:T(8,128)S(1)}, u32[]{:S(2)}, u32[]{:S(2)}) collective-permute-start(f32[5,5,8,256]{3,2,1,0:T(8,128)S(1)} %get-tuple-element.22), channel_id=1, source_target_pairs={{24,0},{48,24},{72,48},{96,72},{120,96},{144,120},{168,144},{192,1... | collective-permute-start | bytes 614408 | tf_op jit(solution)/shard_map/ppermute | solution.py:318
  21.3 5.8 %collective-permute-start.2 = (f32[2,24,128]{2,1,0:T(8,128)S(1)}, f32[2,24,128]{2,1,0:T(8,128)S(1)}, u32[]{:S(2)}, u32[]{:S(2)}) collective-permute-start(f32[2,24,128]{2,1,0:T(8,128)S(1)} %get-tuple-element.14), channel_id=1, source_target_pairs={{1,0},{2,1},{3,2},{4,3},{5,4},{6,5},{7,6},{8,7},{9,8},{10,9},{11,1... | collective-permute-start | bytes 73736 | tf_op jit(solution)/shard_map/ppermute | solution.py:318
  27.1 8.5 %collective-permute-start.4 = (f32[16,8,128]{2,1,0:T(8,128)S(1)}, f32[16,8,128]{2,1,0:T(8,128)S(1)}, u32[]{:S(2)}, u32[]{:S(2)}) collective-permute-start(f32[16,8,128]{2,1,0:T(8,128)S(1)} %pad_maximum_fusion), channel_id=1, source_target_pairs={{0,24},{24,48},{48,72},{72,96},{96,120},{120,144},{144,168},{168,1... | collective-permute-start | bytes 196616 | tf_op jit(solution)/shard_map/ppermute | solution.py:318
  33.7 7.4 %collective-permute-start.5 = (f32[16,8,128]{2,1,0:T(8,128)S(1)}, f32[16,8,128]{2,1,0:T(8,128)S(1)}, u32[]{:S(2)}, u32[]{:S(2)}) collective-permute-start(f32[16,8,128]{2,1,0:T(8,128)S(1)} %pad_maximum_fusion.1), channel_id=1, source_target_pairs={{24,0},{48,24},{72,48},{96,72},{120,96},{144,120},{168,144},{192,1... | collective-permute-start | bytes 196616 | tf_op jit(solution)/shard_map/ppermute | solution.py:318
  43.7 33.5 %copy-start.4 = (s32[24,256]{1,0:T(8,128)S(1)}, s32[24,256]{1,0:T(8,128)}, u32[]{:S(2)}) copy-start(s32[24,256]{1,0:T(8,128)} %flags.5) | copy-start | bytes 73732
  43.7 33.5 %all-to-all-start = ((f32[32,16,128]{2,1,0:T(8,128)}), f32[32,16,128]{2,1,0:T(8,128)S(1)}, u32[]{:S(2)}, u32[]{:S(2)}) async-start(f32[32,16,128]{2,1,0:T(8,128)} %get-tuple-element.21), calls=%async_computation | async-start | bytes 524288 | tf_op jit(solution)/shard_map/all_to_all | solution.py:343
where the time goes:
time: 80.3 us; the launch traced here: 79.7 us
  starting transfers between devices  43.2 us (54%)
  waiting for transfers between devices  24.9 us (31%)
  Pallas kernels  6.32 us (8%)
  local copies, waits for them, and re-layouts  4.5 us (6%)
    ppermute x6, starting transfers between devices, shift(): return lax.ppermute(value, axis, pairs)  25.4 us
    all_to_all x1, starting transfers between devices, local(): got = lax.all_to_all(sent, 'gx', 0, 0, tiled=True)  17.8 us
    all_to_all x1, waiting for transfers between devices, local(): got = lax.all_to_all(sent, 'gx', 0, 0, tiled=True)  15.6 us
    ppermute x6, waiting for transfers between devices, shift(): return lax.ppermute(value, axis, pairs)  9.29 us
    pallas_call x3, Pallas kernels, call(): pl.pallas_call(kernel, out_shape=outs, in_specs=specs, out_specs=[vmem] *...  6.32 us
    unnamed x14, local copies, waits for them, and re-layouts  4.46 us
  transfers between devices with their start and end apart: 7, of which 3 were waited for; matrix products, arithmetic and copies ran while one was open for 0% of the time, Pallas kernels for 0%

commit v1 on v0

v1 whole, which is shorter than its diff:
```python
import jax
import jax.numpy as jnp
from jax import lax
from jax.experimental import pallas as pl
from jax.experimental.pallas import tpu as pltpu
from jax.sharding import PartitionSpec as P

F = 5
TX = 24
TY = 256
EX = 40
EY = 384
ROWS = 6
PLANES = 31
HIGH = lax.Precision.HIGHEST
F32 = jnp.float32


def iota(shape, dim):
    return lax.broadcasted_iota(jnp.int32, shape, dim)


def dot(a, b):
    return jnp.dot(a, b, precision=HIGH, preferred_element_type=F32)


def roll(x, shift, axis):
    shift = shift % x.shape[axis]
    return x if shift == 0 else pltpu.roll(x, shift, axis)


def parity(axis):
    return lax.rem(lax.axis_index(axis), 2) == 1


def restrict_kernel(
    fine_in, owner_in, flags_in, jac_in, coef_in, rhs, top, bottom, near, far,
    fine, owner, flags, jac, coef, sems,
):
    copies = [
        pltpu.make_async_copy(owner_in.at[:, 128 * j : 128 * (j + 1)], owner.at[j], sems.at[j])
        for j in range(4)
    ]
    copies += [
        pltpu.make_async_copy(
            fine_in.at[:, :, 128 * j : 128 * (j + 1)], fine.at[j], sems.at[4 + j]
        )
        for j in range(4)
    ]
    late = [
        pltpu.make_async_copy(flags_in, flags, sems.at[8]),
        pltpu.make_async_copy(coef_in, coef, sems.at[9]),
        pltpu.make_async_copy(jac_in, jac, sems.at[10]),
    ]
    for copy in copies + late:
        copy.start()
    for copy in copies:
        copy.wait()

    def halves(load):
        return [
            jnp.concatenate([load(j, pl.ds(start, TX, 2)) for j in range(4)], axis=1)
            for start in (0, 1)
        ]

    shape = (TX, 2 * TY)
    row = iota(shape, 0)
    col = iota(shape, 1) // 2
    codes = [
        (o // TY - row + 1) * 3 + (o % TY) - col + 1
        for o in halves(lambda j, rows: owner[j, rows, :])
    ]
    masks = [[code == k for code in codes] for k in range(9)]
    gathered = []
    for f in range(F):
        values = halves(lambda j, rows: fine[j, f, rows, :])
        total = None
        for dy in (-1, 0, 1):
            part = None
            for dx in (-1, 0, 1):
                mask = masks[(dx + 1) * 3 + dy + 1]
                moved = jnp.where(mask[0], values[0], 0.0) + jnp.where(mask[1], values[1], 0.0)
                moved = roll(moved, dx, 0)
                part = moved if part is None else part + moved
            part = roll(part, 2 * dy, 1)
            total = part if total is None else total + part
        gathered.append(total)
    pairs = (iota((2 * TY, TY), 0) // 2 == iota((2 * TY, TY), 1)).astype(F32)
    summed = dot(jnp.concatenate(gathered, axis=0), pairs)
    planes = [summed[TX * f : TX * (f + 1)] for f in range(F)]
    for f in range(F):
        rhs[f] = planes[f]
    for copy in late:
        copy.wait()
    planes.append((flags[...] + 1).astype(F32))

    for p in range(F * F):
        top[4 * p : 4 * p + 4] = jac[p // F, p % F, 0:4, :]
        bottom[4 * p : 4 * p + 4] = jac[p // F, p % F, TX - 4 : TX, :]
    for p in range(F + 1):
        top[100 + 5 * p : 105 + 5 * p] = planes[p][0:5]
        bottom[100 + 5 * p : 105 + 5 * p] = planes[p][TX - 5 : TX]
    for f in range(F):
        top[130 + f : 131 + f] = jac[f, f, 4:5, :]
        bottom[130 + f : 131 + f] = jac[f, f, TX - 5 : TX - 4, :]
    top[135:136] = jnp.zeros((1, TY), F32)
    bottom[135:136] = jnp.zeros((1, TY), F32)

    odd = parity("gy")
    slot = iota((TX, 128), 1) // 8
    lane = iota((8, 128), 1)
    for a in range(2):
        first = jnp.zeros((TX, 128), F32)
        last = jnp.zeros((TX, 128), F32)
        for t in range(16):
            p = 16 * a + t
            if p >= PLANES:
                continue
            if p < F * F:
                head, tail = jac[p // F, p % F, :, 0:128], jac[p // F, p % F, :, TY - 128 : TY]
            else:
                head, tail = planes[p - F * F][:, 0:128], planes[p - F * F][:, TY - 128 : TY]
            first = jnp.where(slot == t, roll(head, 8 * t, 1), first)
            last = jnp.where(slot == t, roll(tail, 8 * t - 120, 1), last)
        near[a] = jnp.where(odd, first, last)
        far[a] = jnp.where(odd, last, first)
    lane = iota((ROWS, 128), 1)
    first, last = near[1, 0:ROWS, :], far[1, 0:ROWS, :]
    for f in range(F):
        wide = jnp.concatenate([coef[f], coef[f]], axis=1)
        head, tail = roll(wide, 120 + f, 1), roll(wide, 120 + f - 63, 1)
        first = jnp.where(lane == 120 + f, jnp.where(odd, head, tail), first)
        last = jnp.where(lane == 120 + f, jnp.where(odd, tail, head), last)
    near[1, 0:ROWS, :] = first
    far[1, 0:ROWS, :] = last


def extend(jac, rhs, flags, near_x, far_x, near_y, far_y, jac_all, rhs_all, scaled, sides):
    odd_x, odd_y = parity("gx"), parity("gy")
    upper, lower = (jnp.where(odd_x, near_x[...], far_x[...]), jnp.where(odd_x, far_x[...], near_x[...]))
    sides[0] = upper
    sides[1] = lower
    none = jnp.zeros((8, TY), F32)

    lane = iota((EX, 128), 1)

    def aside(p):
        return jnp.where(
            lane < 8,
            roll(right[p // 16], -8 * (p % 16), 1),
            jnp.where(lane >= 120, roll(left[p // 16], 120 - 8 * (p % 16), 1), 0.0),
        )

    right, left = [], []
    for a in range(2):
        near = jnp.concatenate(
            [sides[0, 136:144, 128 * a : 128 * (a + 1)], near_y[a], sides[1, 136:144, 128 * a : 128 * (a + 1)]],
            axis=0,
        )
        far = jnp.concatenate(
            [sides[0, 144:152, 128 * a : 128 * (a + 1)], far_y[a], sides[1, 144:152, 128 * a : 128 * (a + 1)]],
            axis=0,
        )
        right.append(jnp.where(odd_y, far, near))
        left.append(jnp.where(odd_y, near, far))

    for p in range(F * F):
        f, g = p // F, p % F
        jac_all[p, 8 : 8 + TX, 0:TY] = jac[f, g]
        jac_all[p, 0:8, 0:TY] = none
        jac_all[p, 8 + TX : EX, 0:TY] = none
        jac_all[p, 4:8, 0:TY] = sides[0, 4 * p : 4 * p + 4]
        jac_all[p, 8 + TX : 12 + TX, 0:TY] = sides[1, 4 * p : 4 * p + 4]
        if f == g:
            jac_all[p, 3:4, 0:TY] = sides[0, 130 + f : 131 + f]
            jac_all[p, 12 + TX : 13 + TX, 0:TY] = sides[1, 130 + f : 131 + f]
        jac_all[p, :, TY:EY] = aside(p)
    for f in range(F):
        rhs_all[f, 8 : 8 + TX, 0:TY] = rhs[f]
        rhs_all[f, 0:8, 0:TY] = none
        rhs_all[f, 8 + TX : EX, 0:TY] = none
        rhs_all[f, 3:8, 0:TY] = sides[0, 100 + 5 * f : 105 + 5 * f]
        rhs_all[f, 8 + TX : 13 + TX, 0:TY] = sides[1, 100 + 5 * f : 105 + 5 * f]
        rhs_all[f, :, TY:EY] = aside(F * F + f)
    code = scaled.at[0]
    code[8 : 8 + TX, 0:TY] = (flags[...] + 1).astype(F32)
    code[0:8, 0:TY] = none
    code[8 + TX : EX, 0:TY] = none
    code[3:8, 0:TY] = sides[0, 125:130]
    code[8 + TX : 13 + TX, 0:TY] = sides[1, 125:130]
    code[:, TY:EY] = aside(F * F + F)
    kinds = code[...]
    plain = (kinds == 1.0) | (kinds == 3.0)
    interior = kinds == 1.0
    for f in range(F):
        kept = interior if f in (1, 2) else plain
        scaled[f] = jnp.where(kept, 0.8 / jac_all[F * f + f], 0.0)
    return right[1][8 : 8 + ROWS], left[1][8 : 8 + ROWS]


def residual(f, state, rhs, jac):
    own = state[f]
    beside = roll(own, 1, 0) + roll(own, -1, 0) + roll(own, 1, 1) + roll(own, -1, 1)
    total = rhs[f] + beside
    for g in range(F):
        total = total - jac[F * f + g] * state[g]
    return total


def sweep(old, new, scaled, rhs, jac):
    for f in range(F):
        new[f] = old[f] + scaled[f] * residual(f, old, rhs, jac)


def columns(shape, fine_dim, coarse_dim):
    fine = iota(shape, fine_dim)
    coarse = iota(shape, coarse_dim)
    here = (coarse <= 64) & (fine // 4 == coarse)
    return (here | ((coarse == 65) & (fine >= EY - 4))).astype(F32)


def before_kernel(
    jac_in, rhs_in, flags, near_x, far_x, near_y, far_y, coef,
    state, jac, rhs, scaled, lines, sent, other, sides, block, diag,
):
    near, far = extend(
        jac_in, rhs_in, flags, near_x, far_x, near_y, far_y, jac, rhs, scaled, sides
    )
    for f in range(F):
        state[f] = scaled[f] * rhs[f]
    sweep(state, other, scaled, rhs, jac)
    sweep(other, state, scaled, rhs, jac)
    left_over = jnp.concatenate(
        [residual(f, state, rhs, jac)[8 : 8 + TX] for f in range(F)], axis=0
    )
    by_column = dot(left_over, columns((EY, 128), 0, 1))
    shape = (8 * ROWS, F * TX)
    to, of = iota(shape, 0), iota(shape, 1)
    of_field = (of * 2731) >> 16
    chosen = (to % 8 == of_field) & (to // 8 == (of - TX * of_field) // 4)
    mean = dot(jnp.where(chosen, 0.0625, 0.0), by_column)

    row_lane = iota((ROWS, 128), 1)
    diag[...] = jnp.full((8 * ROWS, 128), 4.0, F32)
    for f in range(F):
        wide = jnp.concatenate([coef[f], coef[f]], axis=1)
        wide = jnp.where(row_lane == 64, roll(near, 64 - 120 - f, 1), wide)
        wide = jnp.where(row_lane == 65, roll(far, 65 - 120 - f, 1), wide)
        wide = jnp.where((row_lane <= 65) & (wide > 0.0), wide, 4.0)
        for k in range(ROWS):
            diag[8 * k + f : 8 * k + f + 1, :] = wide[k : k + 1, :]

    value, low, high = [], [], []
    for k in range(ROWS):
        here = mean[8 * k : 8 * k + 8]
        d = diag[8 * k : 8 * k + 8, :]
        if k == 0:
            inverse = 1.0 / d
            value.append(here * inverse)
            low.append(inverse)
        else:
            inverse = 1.0 / (d - high[-1])
            value.append((here + value[-1]) * inverse)
            low.append(low[-1] * inverse)
        high.append(inverse)
    for k in range(ROWS):
        lines[0, 8 * k : 8 * k + 8] = value[k]
        lines[1, 8 * k : 8 * k + 8] = low[k]
        lines[2, 8 * k : 8 * k + 8] = high[k]
    first, first_low = value[-1], low[-1]
    for k in range(ROWS - 2, -1, -1):
        first = value[k] + high[k] * first
        first_low = low[k] + high[k] * first_low
    parts = [first, value[-1], first_low, low[-1], high[-1]]
    lane = iota((8, 128), 1)
    ends = parts[0]
    for q in range(1, 5):
        ends = jnp.where(lane // 2 == 32 + q, roll(parts[q], 2 * q, 1), ends)
    block[...] = jnp.zeros((16, 128), F32)
    block[0:F] = jnp.where(lane < 64, parts[0], roll(parts[1], 64, 1))[0:F]
    block[F : 2 * F] = jnp.where(lane < 64, parts[2], roll(parts[3], 64, 1))[0:F]
    block[2 * F : 3 * F] = jnp.where(lane < 64, parts[4], ends)[0:F]
    whole = block[...]
    for k in range(sent.shape[0]):
        sent[k] = whole


def after_kernel(
    jac, rhs, scaled, state_in, lines, got, correction, level_residual, state, other, ends
):
    count = got.shape[0]
    me = lax.axis_index("gx")
    lane = iota((F, 128), 1)

    def segment(k):
        one, two, three = got[k, 0:F, :], got[k, F : 2 * F, :], got[k, 2 * F : 3 * F, :]
        main = [one, roll(one, 64, 1), two, roll(two, 64, 1), three]
        return [jnp.where(lane < 64, main[q], roll(three, -2 * q, 1)) for q in range(5)]

    def step(p, q, near, far, turn, through, back):
        w = q / (1.0 - turn * q)
        return far + through * (p + w * (near + turn * p)), back + through * through * w

    zero = jnp.zeros((F, 128), F32)
    p_low = q_low = p_high = q_high = zero
    for k in range(count - 1):
        a0, a1, b0, c, c1 = segment(k)
        p, q = step(p_low, q_low, a0, a1, b0, c, c1)
        p_low, q_low = jnp.where(k < me, p, p_low), jnp.where(k < me, q, q_low)
        j = count - 1 - k
        a0, a1, b0, c, c1 = segment(j)
        p, q = step(p_high, q_high, a1, a0, c1, c, b0)
        p_high, q_high = jnp.where(j > me, p, p_high), jnp.where(j > me, q, q_high)
    a0, a1, b0, c, c1 = segment(me)
    p, q = step(p_low, q_low, a0, a1, b0, c, c1)
    last = (p + q * p_high) / (1.0 - q * q_high)
    above = p_high + q_high * last
    first = (a0 + b0 * p_low + c * above) / (1.0 - b0 * q_low)
    below = p_low + q_low * first

    ends[...] = jnp.zeros((64, 128), F32)
    used = lane <= 65
    ends[0:F] = jnp.where(used, below, 0.0)
    ends[8 * (ROWS + 1) : 8 * (ROWS + 1) + F] = jnp.where(used, above, 0.0)
    here = above
    for k in range(ROWS - 1, -1, -1):
        rows = slice(8 * k, 8 * k + F)
        here = lines[0, rows] + lines[1, rows] * below + lines[2, rows] * here
        ends[8 * (k + 1) : 8 * (k + 1) + F] = jnp.where(used, here, 0.0)

    shape = (F * EX, 64)
    to, of = iota(shape, 0), iota(shape, 1)
    to_field = (to * 1639) >> 16
    to_row = to - EX * to_field
    chosen = (to_field == of % 8) & (to_row >= 4) & (to_row < EX - 4)
    chosen = chosen & ((to_row - 4) // 4 == of // 8)
    spread = dot(dot(chosen.astype(F32), ends[...]), columns((128, EY), 1, 0))

    for f in range(F):
        added = jnp.where(scaled[f] != 0.0, spread[EX * f : EX * (f + 1)], 0.0)
        state[f] = state_in[f] + added
    sweep(state, other, scaled, rhs, jac)
    sweep(other, state, scaled, rhs, jac)
    for f in range(F):
        correction[f] = state[f, 8 : 8 + TX, 0:TY]
        level_residual[f] = residual(f, state, rhs, jac)[8 : 8 + TX, 0:TY]


def shape_of(*dims):
    return jax.ShapeDtypeStruct(dims, F32)


def call(kernel, outs, scratch, *args, space=pltpu.VMEM):
    return pl.pallas_call(
        kernel,
        out_shape=outs,
        in_specs=[pl.BlockSpec(memory_space=space)] * len(args),
        out_specs=[pl.BlockSpec(memory_space=pltpu.VMEM)] * len(outs),
        scratch_shapes=scratch,
        compiler_params=pltpu.CompilerParams(vmem_limit_bytes=48 * 1024 * 1024),
    )(*args)


def swap(value, axis, start):
    count = lax.axis_size(axis)
    firsts = range(start, count - 1, 2)
    return lax.ppermute(value, axis, [(i, i + 1) for i in firsts] + [(i + 1, i) for i in firsts])


def local(fine, owner, flags, jac, coef):
    strip = shape_of(2, TX, 128)
    rows = shape_of(136, TY)
    rhs, top, bottom, near, far = call(
        restrict_kernel,
        [shape_of(F, TX, TY), rows, rows, strip, strip],
        [
            pltpu.VMEM((4, F, 2 * TX, 128), F32),
            pltpu.VMEM((4, 2 * TX, 128), jnp.int32),
            pltpu.VMEM((TX, TY), jnp.int32),
            pltpu.VMEM((F, F, TX, TY), F32),
            pltpu.VMEM((F, ROWS, TY // 4), F32),
            pltpu.SemaphoreType.DMA((11,)),
        ],
        fine, owner, flags, jac, coef,
        space=pl.ANY,
    )
    near_y = swap(near, "gy", 0)
    far_y = swap(far, "gy", 1)

    def with_corners(own, rows):
        corners = [jnp.concatenate([side[0, rows], side[1, rows]], axis=1) for side in (near_y, far_y)]
        return jnp.concatenate([own, *corners], axis=0)

    top = with_corners(top, slice(0, 8))
    bottom = with_corners(bottom, slice(TX - 8, TX))
    odd = parity("gx")
    near_x = swap(jnp.where(odd, top, bottom), "gx", 0)
    far_x = swap(jnp.where(odd, bottom, top), "gx", 1)
    count = lax.axis_size("gx")
    tile = shape_of(F, EX, EY)
    state, jac_all, rhs_all, scaled, lines, sent = call(
        before_kernel,
        [tile, shape_of(F * F, EX, EY), tile, tile, shape_of(3, 8 * ROWS, 128), shape_of(count, 16, 128)],
        [
            pltpu.VMEM((F, EX, EY), F32),
            pltpu.VMEM((2, 152, TY), F32),
            pltpu.VMEM((16, 128), F32),
            pltpu.VMEM((8 * ROWS, 128), F32),
        ],
        jac, rhs, flags, near_x, far_x, near_y, far_y, coef,
    )
    got = lax.all_to_all(sent, "gx", 0, 0, tiled=True)
    tile = pltpu.VMEM((F, EX, EY), F32)
    return tuple(
        call(
            after_kernel,
            [shape_of(F, TX, TY), shape_of(F, TX, TY)],
            [tile, tile, pltpu.VMEM((64, 128), F32)],
            jac_all, rhs_all, scaled, state, lines, got,
        )
    )


def solution(mesh):
    in_specs = (
        P(None, "gx", "gy"),
        P("gx", "gy"),
        P("gx", "gy"),
        P(None, None, "gx", "gy"),
        P(None, "gx", "gy"),
    )
    out_specs = (P(None, "gx", "gy"), P(None, "gx", "gy"))
    return jax.shard_map(local, mesh=mesh, in_specs=in_specs, out_specs=out_specs, check_vma=False)
```

time: 80.3 us -> 70.6 us (0.88)
  the two profiles are of different devices: /device:TPU:25 before, /device:TPU:33 now
where the time goes in v1:
time: 70.6 us; the launch traced here: 70.2 us
  blocking collectives  36 us (51%)
  starting transfers between devices  15.8 us (22%)
  waiting for transfers between devices  6.74 us (10%)
  Pallas kernels  6.39 us (9%)
  local copies, waits for them, and re-layouts  4.47 us (6%)
  between operations  0.71 us (1%)
    all_to_all x1, blocking collectives, local(): got = lax.all_to_all(sent, 'gx', 0, 0, tiled=True)  36 us
    ppermute x4, starting transfers between devices, swap(): lax.ppermute(value, axis, [(i, i + 1) for i in firsts] + [(i + 1, i) for...  15.8 us
    ppermute x4, waiting for transfers between devices, swap(): lax.ppermute(value, axis, [(i, i + 1) for i in firsts] + [(i + 1, i) for...  6.74 us
    pallas_call x3, Pallas kernels, call(): pl.pallas_call(kernel, out_shape=outs, in_specs=[pl.BlockSpec(memory_spac...  6.39 us
    unnamed x16, local copies, waits for them, and re-layouts  4.46 us
  transfers between devices with their start and end apart: 4, of which 3 were waited for; matrix products, arithmetic and copies ran while one was open for 0% of the time, Pallas kernels for 0%

profile of v1, /device:TPU:33, one launch (start us, length us, event | category | flops | bytes accessed | tf_op | source)
XLA Modules:
  0.0 70.2 jit_solution(4901567965746746479)
XLA Ops:
  0.6 0.0 copy-start
  0.6 1.1 %copy-done = f32[5,5,24,256]{3,2,1,0:T(8,128)S(1)} copy-done((f32[5,5,24,256]{3,2,1,0:T(8,128)S(1)}, f32[5,5,24,256]{3,2,1,0:T(8,128)}, u32[]{:S(2)}) %copy-start) | copy-done | bytes 614424
  1.7 0.0 copy-start.2
  1.7 1.0 %copy-done.2 = f32[5,48,512]{2,1,0:T(8,128)S(1)} copy-done((f32[5,48,512]{2,1,0:T(8,128)S(1)}, f32[5,48,512]{2,1,0:T(8,128)}, u32[]{:S(2)}) %copy-start.2) | copy-done | bytes 491544
  2.7 0.0 copy-start.3
  2.7 0.9 %copy-done.3 = s32[48,512]{1,0:T(8,128)S(1)} copy-done((s32[48,512]{1,0:T(8,128)S(1)}, s32[48,512]{1,0:T(8,128)}, u32[]{:S(2)}) %copy-start.3) | copy-done | bytes 98328
  3.6 0.0 copy-start.4
  3.6 0.7 %copy-done.4 = s32[24,256]{1,0:T(8,128)S(1)} copy-done((s32[24,256]{1,0:T(8,128)S(1)}, s32[24,256]{1,0:T(8,128)}, u32[]{:S(2)}) %copy-start.4) | copy-done | bytes 24600
  4.4 0.0 copy-start.6
  4.4 0.7 %copy-done.6 = f32[5,6,64]{2,1,0:T(8,128)S(1)} copy-done((f32[5,6,64]{2,1,0:T(8,128)S(1)}, f32[5,6,64]{2,1,0:T(8,128)}, u32[]{:S(2)}) %copy-start.6) | copy-done | bytes 7704
  5.1 0.0 copy-start.1
  5.1 0.0 copy-start.5
  5.1 0.0 copy-start.7
  5.1 1.9 %shard_map.68 = (f32[5,24,256]{2,1,0:T(8,128)S(1)}, f32[136,256]{1,0:T(8,128)S(1)}, f32[136,256]{1,0:T(8,128)S(1)}, f32[2,24,128]{2,1,0:T(8,128)S(1)}, f32[2,24,128]{2,1,0:T(8,128)S(1)}) custom-call(f32[5,48,512]{2,1,0:T(8,128)S(1)} %copy-done.2, s32[48,512]{1,0:T(8,128)S(1)} %copy-done.3, s32[24,256]{1,0:T(8,128)S(1)} %copy-done.4, ...), custom_call_target="tpu_custom_call" | custom-call | tf_op jit(solution)/shard_map/pallas_call | solution.py:354
  7.0 2.3 %collective-permute-start = (f32[2,24,128]{2,1,0:T(8,128)S(1)}, f32[2,24,128]{2,1,0:T(8,128)S(1)}, u32[]{:S(2)}, u32[]{:S(2)}) collective-permute-start(f32[2,24,128]{2,1,0:T(8,128)S(1)} %get-tuple-element.15), channel_id=1, source_target_pairs={{0,1},{2,3},{4,5},{6,7},{8,9},{10,11},{12,13},{14,15},{16,17},{18,... | collective-permute-start | bytes 73736 | tf_op jit(solution)/shard_map/ppermute | solution.py:367
  9.3 1.9 %collective-permute-start.1 = (f32[2,24,128]{2,1,0:T(8,128)S(1)}, f32[2,24,128]{2,1,0:T(8,128)S(1)}, u32[]{:S(2)}, u32[]{:S(2)}) collective-permute-start(f32[2,24,128]{2,1,0:T(8,128)S(1)} %get-tuple-element.16), channel_id=1, source_target_pairs={{1,2},{3,4},{5,6},{7,8},{9,10},{11,12},{13,14},{15,16},{17,18},{19... | collective-permute-start | bytes 73736 | tf_op jit(solution)/shard_map/ppermute | solution.py:367
  11.2 0.3 collective-permute-done.near_y
  11.5 3.5 %collective-permute-done.1.far_y = f32[2,24,128]{2,1,0:T(8,128)S(1)} collective-permute-done((f32[2,24,128]{2,1,0:T(8,128)S(1)}, f32[2,24,128]{2,1,0:T(8,128)S(1)}, u32[]{:S(2)}, u32[]{:S(2)}) %collective-permute-start.1) | collective-permute-done | bytes 24608 | tf_op jit(solution)/shard_map/ppermute | solution.py:367
  15.1 4.0 %collective-permute-start.2 = (f32[152,256]{1,0:T(8,128)S(1)}, f32[152,256]{1,0:T(8,128)S(1)}, u32[]{:S(2)}, u32[]{:S(2)}) collective-permute-start(f32[152,256]{1,0:T(8,128)S(1)} %broadcast_select_fusion.1), channel_id=1, source_target_pairs={{0,24},{48,72},{96,120},{144,168},{192,216},{240,264},{288,312},{3... | collective-permute-start | bytes 466952 | tf_op jit(solution)/shard_map/ppermute | solution.py:367
  19.1 7.5 %collective-permute-start.3 = (f32[152,256]{1,0:T(8,128)S(1)}, f32[152,256]{1,0:T(8,128)S(1)}, u32[]{:S(2)}, u32[]{:S(2)}) collective-permute-start(f32[152,256]{1,0:T(8,128)S(1)} %broadcast_select_fusion), channel_id=1, source_target_pairs={{24,48},{72,96},{120,144},{168,192},{216,240},{264,288},{312,336},... | collective-permute-start | bytes 466952 | tf_op jit(solution)/shard_map/ppermute | solution.py:367
  26.7 0.0 collective-permute-done.2.near_x
  26.7 2.9 %collective-permute-done.3.far_x = f32[152,256]{1,0:T(8,128)S(1)} collective-permute-done((f32[152,256]{1,0:T(8,128)S(1)}, f32[152,256]{1,0:T(8,128)S(1)}, u32[]{:S(2)}, u32[]{:S(2)}) %collective-permute-start.3) | collective-permute-done | bytes 155680 | tf_op jit(solution)/shard_map/ppermute | solution.py:367
  29.6 0.0 copy-done.1
  29.6 0.0 copy-done.5
  29.6 0.0 copy-done.7
  29.6 2.0 %shard_map.69 = (f32[5,40,384]{2,1,0:T(8,128)S(1)}, f32[25,40,384]{2,1,0:T(8,128)S(1)}, f32[5,40,384]{2,1,0:T(8,128)S(1)}, f32[5,40,384]{2,1,0:T(8,128)S(1)}, f3...) custom-call(f32[5,5,24,256]{3,2,1,0:T(8,128)S(1)} %copy-done.1, f32[5,24,256]{2,1,0:T(8,128)S(1)} %get-tuple-element.13.rhs_in, ...), custom_call_target="tpu_custom_call" | custom-call | tf_op jit(solution)/shard_map/pallas_call | solution.py:354
  31.6 36.0 %all_to_all.5.got = f32[32,16,128]{2,1,0:T(8,128)S(1)} all-to-all(f32[32,16,128]{2,1,0:T(8,128)S(1)} %get-tuple-element.23), channel_id=1, replica_groups=mesh['gx'=32,'gy'=24] {'gx'}, dimensions={0} | all-to-all | bytes 524288 | tf_op jit(solution)/shard_map/all_to_all | solution.py:412
  67.6 2.6 %shard_map.70 = (f32[5,24,256]{2,1,0:T(8,128)}, f32[5,24,256]{2,1,0:T(8,128)}) custom-call(f32[25,40,384]{2,1,0:T(8,128)S(1)} %get-tuple-element.18.jac, f32[5,40,384]{2,1,0:T(8,128)S(1)} %get-tuple-element.19.rhs, f32[5,40,384]{2,1,0:T(8,128)S(1)} %get-tuple-element.20.scaled, f32[5,40,384]{2,1,0:T(8,128)S(1)} %get-tuple-element.21.state_in, ...), custom_call_target="tpu_custom_call" | custom-call | tf_op jit(solution)/shard_map/pallas_call | solution.py:354
  (4 shorter events, 0.1 us)
Async XLA Ops:
  0.6 1.1 %copy-start = (f32[5,5,24,256]{3,2,1,0:T(8,128)S(1)}, f32[5,5,24,256]{3,2,1,0:T(8,128)}, u32[]{:S(2)}) copy-start(f32[5,5,24,256]{3,2,1,0:T(8,128)} %jac_in.3) | copy-start | bytes 1843204
  1.7 1.0 %copy-start.2 = (f32[5,48,512]{2,1,0:T(8,128)S(1)}, f32[5,48,512]{2,1,0:T(8,128)}, u32[]{:S(2)}) copy-start(f32[5,48,512]{2,1,0:T(8,128)} %fine_in.1) | copy-start | bytes 1474564
  2.7 0.9 %copy-start.3 = (s32[48,512]{1,0:T(8,128)S(1)}, s32[48,512]{1,0:T(8,128)}, u32[]{:S(2)}) copy-start(s32[48,512]{1,0:T(8,128)} %owner_in.1) | copy-start | bytes 294916
  3.6 0.7 %copy-start.4 = (s32[24,256]{1,0:T(8,128)S(1)}, s32[24,256]{1,0:T(8,128)}, u32[]{:S(2)}) copy-start(s32[24,256]{1,0:T(8,128)} %flags.1) | copy-start | bytes 73732
  4.4 0.7 %copy-start.6 = (f32[5,6,64]{2,1,0:T(8,128)S(1)}, f32[5,6,64]{2,1,0:T(8,128)}, u32[]{:S(2)}) copy-start(f32[5,6,64]{2,1,0:T(8,128)} %coef.1) | copy-start | bytes 23044
  5.1 24.5 %copy-start.1 = (f32[5,5,24,256]{3,2,1,0:T(8,128)S(1)}, f32[5,5,24,256]{3,2,1,0:T(8,128)}, u32[]{:S(2)}) copy-start(f32[5,5,24,256]{3,2,1,0:T(8,128)} %jac_in.3) | copy-start | bytes 1843204
  5.1 24.5 %copy-start.5 = (s32[24,256]{1,0:T(8,128)S(1)}, s32[24,256]{1,0:T(8,128)}, u32[]{:S(2)}) copy-start(s32[24,256]{1,0:T(8,128)} %flags.1) | copy-start | bytes 73732
  5.1 24.5 %copy-start.7 = (f32[5,6,64]{2,1,0:T(8,128)S(1)}, f32[5,6,64]{2,1,0:T(8,128)}, u32[]{:S(2)}) copy-start(f32[5,6,64]{2,1,0:T(8,128)} %coef.1) | copy-start | bytes 23044
  7.0 4.6 %collective-permute-start = (f32[2,24,128]{2,1,0:T(8,128)S(1)}, f32[2,24,128]{2,1,0:T(8,128)S(1)}, u32[]{:S(2)}, u32[]{:S(2)}) collective-permute-start(f32[2,24,128]{2,1,0:T(8,128)S(1)} %get-tuple-element.15), channel_id=1, source_target_pairs={{0,1},{2,3},{4,5},{6,7},{8,9},{10,11},{12,13},{14,15},{16,17},{18,... | collective-permute-start | bytes 73736 | tf_op jit(solution)/shard_map/ppermute | solution.py:367
  9.3 5.8 %collective-permute-start.1 = (f32[2,24,128]{2,1,0:T(8,128)S(1)}, f32[2,24,128]{2,1,0:T(8,128)S(1)}, u32[]{:S(2)}, u32[]{:S(2)}) collective-permute-start(f32[2,24,128]{2,1,0:T(8,128)S(1)} %get-tuple-element.16), channel_id=1, source_target_pairs={{1,2},{3,4},{5,6},{7,8},{9,10},{11,12},{13,14},{15,16},{17,18},{19... | collective-permute-start | bytes 73736 | tf_op jit(solution)/shard_map/ppermute | solution.py:367
  15.1 11.5 %collective-permute-start.2 = (f32[152,256]{1,0:T(8,128)S(1)}, f32[152,256]{1,0:T(8,128)S(1)}, u32[]{:S(2)}, u32[]{:S(2)}) collective-permute-start(f32[152,256]{1,0:T(8,128)S(1)} %broadcast_select_fusion.1), channel_id=1, source_target_pairs={{0,24},{48,72},{96,120},{144,168},{192,216},{240,264},{288,312},{3... | collective-permute-start | bytes 466952 | tf_op jit(solution)/shard_map/ppermute | solution.py:367
  19.1 10.4 %collective-permute-start.3 = (f32[152,256]{1,0:T(8,128)S(1)}, f32[152,256]{1,0:T(8,128)S(1)}, u32[]{:S(2)}, u32[]{:S(2)}) collective-permute-start(f32[152,256]{1,0:T(8,128)S(1)} %broadcast_select_fusion), channel_id=1, source_target_pairs={{24,48},{72,96},{120,144},{168,192},{216,240},{264,288},{312,336},... | collective-permute-start | bytes 466952 | tf_op jit(solution)/shard_map/ppermute | solution.py:367

commit v2 on v1

--- a/solution.py
+++ b/solution.py
@@ -154,11 +154,11 @@
     right, left = [], []
     for a in range(2):
         near = jnp.concatenate(
-            [sides[0, 136:144, 128 * a : 128 * (a + 1)], near_y[a], sides[1, 136:144, 128 * a : 128 * (a + 1)]],
+            [sides[0, 144:152, 128 * a : 128 * (a + 1)], near_y[a], sides[1, 144:152, 128 * a : 128 * (a + 1)]],
             axis=0,
         )
         far = jnp.concatenate(
-            [sides[0, 144:152, 128 * a : 128 * (a + 1)], far_y[a], sides[1, 144:152, 128 * a : 128 * (a + 1)]],
+            [sides[0, 136:144, 128 * a : 128 * (a + 1)], far_y[a], sides[1, 136:144, 128 * a : 128 * (a + 1)]],
             axis=0,
         )
         right.append(jnp.where(odd_y, far, near))
@@ -220,7 +220,7 @@
 
 
 def before_kernel(
-    jac_in, rhs_in, flags, near_x, far_x, near_y, far_y, coef,
+    jac_in, rhs_in, flags, far_x, near_x, far_y, near_y, coef,
     state, jac, rhs, scaled, lines, sent, other, sides, block, diag,
 ):
     near, far = extend(
@@ -350,14 +350,14 @@
     return jax.ShapeDtypeStruct(dims, F32)
 
 
-def call(kernel, outs, scratch, *args, space=pltpu.VMEM):
+def call(kernel, outs, scratch, *args, space=pltpu.VMEM, limit=32 * 1024 * 1024):
     return pl.pallas_call(
         kernel,
         out_shape=outs,
         in_specs=[pl.BlockSpec(memory_space=space)] * len(args),
         out_specs=[pl.BlockSpec(memory_space=pltpu.VMEM)] * len(outs),
         scratch_shapes=scratch,
-        compiler_params=pltpu.CompilerParams(vmem_limit_bytes=48 * 1024 * 1024),
+        compiler_params=pltpu.CompilerParams(vmem_limit_bytes=limit),
     )(*args)
 
 
@@ -381,21 +381,21 @@
             pltpu.VMEM((F, ROWS, TY // 4), F32),
             pltpu.SemaphoreType.DMA((11,)),
         ],
-        fine, owner, flags, jac, coef,
-        space=pl.ANY,
-    )
+        *[pltpu.with_memory_space_constraint(x, pltpu.HBM) for x in (fine, owner, flags, jac, coef)],
+        space=pltpu.HBM,
+    )
+    far_y = swap(far, "gy", 1)
     near_y = swap(near, "gy", 0)
-    far_y = swap(far, "gy", 1)
 
     def with_corners(own, rows):
-        corners = [jnp.concatenate([side[0, rows], side[1, rows]], axis=1) for side in (near_y, far_y)]
+        corners = [jnp.concatenate([side[0, rows], side[1, rows]], axis=1) for side in (far_y, near_y)]
         return jnp.concatenate([own, *corners], axis=0)
 
     top = with_corners(top, slice(0, 8))
     bottom = with_corners(bottom, slice(TX - 8, TX))
     odd = parity("gx")
+    far_x = swap(jnp.where(odd, bottom, top), "gx", 1)
     near_x = swap(jnp.where(odd, top, bottom), "gx", 0)
-    far_x = swap(jnp.where(odd, bottom, top), "gx", 1)
     count = lax.axis_size("gx")
     tile = shape_of(F, EX, EY)
     state, jac_all, rhs_all, scaled, lines, sent = call(
@@ -407,7 +407,7 @@
             pltpu.VMEM((16, 128), F32),
             pltpu.VMEM((8 * ROWS, 128), F32),
         ],
-        jac, rhs, flags, near_x, far_x, near_y, far_y, coef,
+        jac, rhs, flags, far_x, near_x, far_y, near_y, coef,
     )
     got = lax.all_to_all(sent, "gx", 0, 0, tiled=True)
     tile = pltpu.VMEM((F, EX, EY), F32)

time: 70.6 us -> 65.5 us (0.928)
  the two profiles are of different devices: /device:TPU:33 before, /device:TPU:89 now
where the time goes in v2:
time: 65.5 us; the launch traced here: 65.3 us
  blocking collectives  34.1 us (52%)
  starting transfers between devices  19.1 us (29%)
  Pallas kernels  7.33 us (11%)
  waiting for transfers between devices  3.96 us (6%)
  between operations  0.73 us (1%)
    all_to_all x1, blocking collectives, local(): got = lax.all_to_all(sent, 'gx', 0, 0, tiled=True)  34.1 us
    ppermute x4, starting transfers between devices, swap(): lax.ppermute(value, axis, [(i, i + 1) for i in firsts] + [(i + 1, i) for...  19.1 us
    pallas_call x3, Pallas kernels, call(): pl.pallas_call(kernel, out_shape=outs, in_specs=[pl.BlockSpec(memory_spac...  7.33 us
    ppermute x4, waiting for transfers between devices, swap(): lax.ppermute(value, axis, [(i, i + 1) for i in firsts] + [(i + 1, i) for...  3.96 us
  transfers between devices with their start and end apart: 4, of which 3 were waited for; matrix products, arithmetic and copies ran while one was open for 0% of the time, Pallas kernels for 0%

profile of v2, /device:TPU:89, one launch (start us, length us, event | category | flops | bytes accessed | tf_op | source)
XLA Modules:
  0.0 65.3 jit_solution(6085256159152819371)
XLA Ops:
  0.6 0.0 copy-start.2
  0.6 0.0 copy-start
  0.7 0.0 copy-start.1
  0.7 2.8 %shard_map.68 = (f32[5,24,256]{2,1,0:T(8,128)S(1)}, f32[136,256]{1,0:T(8,128)S(1)}, f32[136,256]{1,0:T(8,128)S(1)}, f32[2,24,128]{2,1,0:T(8,128)S(1)}, f32[2,24,128]{2,1,0:T(8,128)S(1)}) custom-call(f32[5,48,512]{2,1,0:T(8,128)} %fine_in.1, s32[48,512]{1,0:T(8,128)} %owner_in.1, s32[24,256]{1,0:T(8,128)} %flags.1, f32[5,5,24,256]{3,2,1,0:T(8,128)} %jac_in.3, ...), custom_call_target="tpu_custom_call" | custom-call | tf_op jit(solution)/shard_map/pallas_call | solution.py:354
  3.5 4.4 %collective-permute-start = (f32[2,24,128]{2,1,0:T(8,128)S(1)}, f32[2,24,128]{2,1,0:T(8,128)S(1)}, u32[]{:S(2)}, u32[]{:S(2)}) collective-permute-start(f32[2,24,128]{2,1,0:T(8,128)S(1)} %get-tuple-element.15), channel_id=1, source_target_pairs={{1,2},{3,4},{5,6},{7,8},{9,10},{11,12},{13,14},{15,16},{17,18},{19... | collective-permute-start | bytes 73736 | tf_op jit(solution)/shard_map/ppermute | solution.py:367
  7.9 1.9 %collective-permute-start.1 = (f32[2,24,128]{2,1,0:T(8,128)S(1)}, f32[2,24,128]{2,1,0:T(8,128)S(1)}, u32[]{:S(2)}, u32[]{:S(2)}) collective-permute-start(f32[2,24,128]{2,1,0:T(8,128)S(1)} %get-tuple-element.16), channel_id=1, source_target_pairs={{0,1},{2,3},{4,5},{6,7},{8,9},{10,11},{12,13},{14,15},{16,17},{18,... | collective-permute-start | bytes 73736 | tf_op jit(solution)/shard_map/ppermute | solution.py:367
  9.8 0.0 collective-permute-done.far_y
  9.8 2.6 %collective-permute-done.1.near_y = f32[2,24,128]{2,1,0:T(8,128)S(1)} collective-permute-done((f32[2,24,128]{2,1,0:T(8,128)S(1)}, f32[2,24,128]{2,1,0:T(8,128)S(1)}, u32[]{:S(2)}, u32[]{:S(2)}) %collective-permute-start.1) | collective-permute-done | bytes 24608 | tf_op jit(solution)/shard_map/ppermute | solution.py:367
  12.5 10.8 %collective-permute-start.2 = (f32[152,256]{1,0:T(8,128)S(1)}, f32[152,256]{1,0:T(8,128)S(1)}, u32[]{:S(2)}, u32[]{:S(2)}) collective-permute-start(f32[152,256]{1,0:T(8,128)S(1)} %broadcast_select_fusion.1), channel_id=1, source_target_pairs={{24,48},{72,96},{120,144},{168,192},{216,240},{264,288},{312,336},... | collective-permute-start | bytes 466952 | tf_op jit(solution)/shard_map/ppermute | solution.py:367
  23.3 1.9 %collective-permute-start.3 = (f32[152,256]{1,0:T(8,128)S(1)}, f32[152,256]{1,0:T(8,128)S(1)}, u32[]{:S(2)}, u32[]{:S(2)}) collective-permute-start(f32[152,256]{1,0:T(8,128)S(1)} %broadcast_select_fusion), channel_id=1, source_target_pairs={{0,24},{48,72},{96,120},{144,168},{192,216},{240,264},{288,312},{3... | collective-permute-start | bytes 466952 | tf_op jit(solution)/shard_map/ppermute | solution.py:367
  25.3 1.0 %collective-permute-done.2.far_x = f32[152,256]{1,0:T(8,128)S(1)} collective-permute-done((f32[152,256]{1,0:T(8,128)S(1)}, f32[152,256]{1,0:T(8,128)S(1)}, u32[]{:S(2)}, u32[]{:S(2)}) %collective-permute-start.2) | collective-permute-done | bytes 155680 | tf_op jit(solution)/shard_map/ppermute | solution.py:367
  26.2 0.4 collective-permute-done.3.near_x
  26.6 0.0 copy-done.2
  26.6 0.0 copy-done
  26.6 0.0 copy-done.1
  26.6 2.0 %shard_map.69 = (f32[5,40,384]{2,1,0:T(8,128)S(1)}, f32[25,40,384]{2,1,0:T(8,128)S(1)}, f32[5,40,384]{2,1,0:T(8,128)S(1)}, f32[5,40,384]{2,1,0:T(8,128)S(1)}, f3...) custom-call(f32[5,5,24,256]{3,2,1,0:T(8,128)S(1)} %copy-done, f32[5,24,256]{2,1,0:T(8,128)S(1)} %get-tuple-element.13.rhs_in, ...), custom_call_target="tpu_custom_call" | custom-call | tf_op jit(solution)/shard_map/pallas_call | solution.py:354
  28.6 34.1 %all_to_all.5.got = f32[32,16,128]{2,1,0:T(8,128)S(1)} all-to-all(f32[32,16,128]{2,1,0:T(8,128)S(1)} %get-tuple-element.23), channel_id=1, replica_groups=mesh['gx'=32,'gy'=24] {'gx'}, dimensions={0} | all-to-all | bytes 524288 | tf_op jit(solution)/shard_map/all_to_all | solution.py:412
  62.7 2.6 %shard_map.70 = (f32[5,24,256]{2,1,0:T(8,128)}, f32[5,24,256]{2,1,0:T(8,128)}) custom-call(f32[25,40,384]{2,1,0:T(8,128)S(1)} %get-tuple-element.18.jac, f32[5,40,384]{2,1,0:T(8,128)S(1)} %get-tuple-element.19.rhs, f32[5,40,384]{2,1,0:T(8,128)S(1)} %get-tuple-element.20.scaled, f32[5,40,384]{2,1,0:T(8,128)S(1)} %get-tuple-element.21.state_in, ...), custom_call_target="tpu_custom_call" | custom-call | tf_op jit(solution)/shard_map/pallas_call | solution.py:354
  (4 shorter events, 0.1 us)
Async XLA Ops:
  0.6 26.0 %copy-start.2 = (f32[5,6,64]{2,1,0:T(8,128)S(1)}, f32[5,6,64]{2,1,0:T(8,128)}, u32[]{:S(2)}) copy-start(f32[5,6,64]{2,1,0:T(8,128)} %coef.1) | copy-start | bytes 23044
  0.6 26.0 %copy-start = (f32[5,5,24,256]{3,2,1,0:T(8,128)S(1)}, f32[5,5,24,256]{3,2,1,0:T(8,128)}, u32[]{:S(2)}) copy-start(f32[5,5,24,256]{3,2,1,0:T(8,128)} %jac_in.3) | copy-start | bytes 1843204
  0.7 26.0 %copy-start.1 = (s32[24,256]{1,0:T(8,128)S(1)}, s32[24,256]{1,0:T(8,128)}, u32[]{:S(2)}) copy-start(s32[24,256]{1,0:T(8,128)} %flags.1) | copy-start | bytes 73732
  3.5 6.4 %collective-permute-start = (f32[2,24,128]{2,1,0:T(8,128)S(1)}, f32[2,24,128]{2,1,0:T(8,128)S(1)}, u32[]{:S(2)}, u32[]{:S(2)}) collective-permute-start(f32[2,24,128]{2,1,0:T(8,128)S(1)} %get-tuple-element.15), channel_id=1, source_target_pairs={{1,2},{3,4},{5,6},{7,8},{9,10},{11,12},{13,14},{15,16},{17,18},{19... | collective-permute-start | bytes 73736 | tf_op jit(solution)/shard_map/ppermute | solution.py:367
  7.9 4.6 %collective-permute-start.1 = (f32[2,24,128]{2,1,0:T(8,128)S(1)}, f32[2,24,128]{2,1,0:T(8,128)S(1)}, u32[]{:S(2)}, u32[]{:S(2)}) collective-permute-start(f32[2,24,128]{2,1,0:T(8,128)S(1)} %get-tuple-element.16), channel_id=1, source_target_pairs={{0,1},{2,3},{4,5},{6,7},{8,9},{10,11},{12,13},{14,15},{16,17},{18,... | collective-permute-start | bytes 73736 | tf_op jit(solution)/shard_map/ppermute | solution.py:367
  12.5 13.7 %collective-permute-start.2 = (f32[152,256]{1,0:T(8,128)S(1)}, f32[152,256]{1,0:T(8,128)S(1)}, u32[]{:S(2)}, u32[]{:S(2)}) collective-permute-start(f32[152,256]{1,0:T(8,128)S(1)} %broadcast_select_fusion.1), channel_id=1, source_target_pairs={{24,48},{72,96},{120,144},{168,192},{216,240},{264,288},{312,336},... | collective-permute-start | bytes 466952 | tf_op jit(solution)/shard_map/ppermute | solution.py:367
  23.3 3.3 %collective-permute-start.3 = (f32[152,256]{1,0:T(8,128)S(1)}, f32[152,256]{1,0:T(8,128)S(1)}, u32[]{:S(2)}, u32[]{:S(2)}) collective-permute-start(f32[152,256]{1,0:T(8,128)S(1)} %broadcast_select_fusion), channel_id=1, source_target_pairs={{0,24},{48,72},{96,120},{144,168},{192,216},{240,264},{288,312},{3... | collective-permute-start | bytes 466952 | tf_op jit(solution)/shard_map/ppermute | solution.py:367

commit v3 on v2

v3 whole, which is shorter than its diff:
```python
import jax
import jax.numpy as jnp
from jax import lax
from jax.experimental import pallas as pl
from jax.experimental.pallas import tpu as pltpu
from jax.sharding import PartitionSpec as P

F = 5
TX = 24
TY = 256
EX = 40
EY = 384
ROWS = 6
PLANES = 31
F32 = jnp.float32


def iota(shape, dim):
    return lax.broadcasted_iota(jnp.int32, shape, dim)


def parts_of(x):
    head = x.astype(jnp.bfloat16)
    rest = x - head.astype(F32)
    middle = rest.astype(jnp.bfloat16)
    return head, middle, (rest - middle.astype(F32)).astype(jnp.bfloat16)


def select_columns(x, chosen):
    rows = x.shape[0]
    whole = jnp.concatenate(parts_of(x), axis=0)
    out = jnp.dot(whole, chosen.astype(jnp.bfloat16), preferred_element_type=F32)
    return out[0:rows] + out[rows : 2 * rows] + out[2 * rows :]


def roll(x, shift, axis):
    shift = shift % x.shape[axis]
    return x if shift == 0 else pltpu.roll(x, shift, axis)


def parity(axis):
    return lax.rem(lax.axis_index(axis), 2) == 1


def restrict_kernel(
    fine_in, owner_in, flags_in, jac_in, coef_in, rhs, top, bottom, near, far,
    fine, owner, flags, jac, coef, sems,
):
    def tile_copy(source, target, sem, j):
        return pltpu.make_async_copy(source.at[:, 128 * j : 128 * (j + 1)], target.at[j], sem)

    owners = [tile_copy(owner_in, owner, sems.at[0, j], j) for j in range(4)]
    fines = [
        [tile_copy(fine_in.at[f], fine.at[f], sems.at[1 + f, j], j) for j in range(4)]
        for f in range(F)
    ]
    late = [
        pltpu.make_async_copy(flags_in, flags, sems.at[F + 1, 0]),
        pltpu.make_async_copy(coef_in, coef, sems.at[F + 1, 1]),
        pltpu.make_async_copy(jac_in, jac, sems.at[F + 1, 2]),
    ]
    for copy in owners + sum(fines, []) + late:
        copy.start()
    for copy in owners:
        copy.wait()

    def halves(load):
        return [
            jnp.concatenate([load(j, pl.ds(start, TX, 2)) for j in range(4)], axis=1)
            for start in (0, 1)
        ]

    shape = (TX, 2 * TY)
    row = iota(shape, 0)
    col = iota(shape, 1) >> 1
    codes = [
        ((o >> 8) - row + 1) * 3 + (o & (TY - 1)) - col + 1
        for o in halves(lambda j, rows: owner[j, rows, :])
    ]
    masks = [[code == k for code in codes] for k in range(9)]
    gathered = []
    for f in range(F):
        for copy in fines[f]:
            copy.wait()
        values = halves(lambda j, rows: fine[f, j, rows, :])
        total = None
        for dy in (-1, 0, 1):
            part = None
            for dx in (-1, 0, 1):
                mask = masks[(dx + 1) * 3 + dy + 1]
                moved = jnp.where(mask[0], values[0], 0.0) + jnp.where(mask[1], values[1], 0.0)
                moved = roll(moved, dx, 0)
                part = moved if part is None else part + moved
            part = roll(part, 2 * dy, 1)
            total = part if total is None else total + part
        gathered.append(total)
    pairs = ((iota((2 * TY, TY), 0) >> 1) == iota((2 * TY, TY), 1)).astype(F32)
    gathered.append(jnp.zeros((8, 2 * TY), F32))
    summed = select_columns(jnp.concatenate(gathered, axis=0), pairs)
    planes = [summed[TX * f : TX * (f + 1)] for f in range(F)]
    for f in range(F):
        rhs[f] = planes[f]
    for copy in late:
        copy.wait()
    planes.append((flags[...] + 1).astype(F32))

    for p in range(F * F):
        top[4 * p : 4 * p + 4] = jac[p // F, p % F, 0:4, :]
        bottom[4 * p : 4 * p + 4] = jac[p // F, p % F, TX - 4 : TX, :]
    for p in range(F + 1):
        top[100 + 5 * p : 105 + 5 * p] = planes[p][0:5]
        bottom[100 + 5 * p : 105 + 5 * p] = planes[p][TX - 5 : TX]
    for f in range(F):
        top[130 + f : 131 + f] = jac[f, f, 4:5, :]
        bottom[130 + f : 131 + f] = jac[f, f, TX - 5 : TX - 4, :]
    top[135:136] = jnp.zeros((1, TY), F32)
    bottom[135:136] = jnp.zeros((1, TY), F32)

    odd = parity("gy")
    slot = iota((TX, 128), 1) >> 3
    for a in range(2):
        first = jnp.zeros((TX, 128), F32)
        last = jnp.zeros((TX, 128), F32)
        for t in range(16):
            p = 16 * a + t
            if p >= PLANES:
                continue
            if p < F * F:
                head, tail = jac[p // F, p % F, :, 0:128], jac[p // F, p % F, :, TY - 128 : TY]
            else:
                head, tail = planes[p - F * F][:, 0:128], planes[p - F * F][:, TY - 128 : TY]
            first = jnp.where(slot == t, roll(head, 8 * t, 1), first)
            last = jnp.where(slot == t, roll(tail, 8 * t - 120, 1), last)
        near[a] = jnp.where(odd, first, last)
        far[a] = jnp.where(odd, last, first)
    lane = iota((ROWS, 128), 1)
    first, last = near[1, 0:ROWS, :], far[1, 0:ROWS, :]
    for f in range(F):
        wide = jnp.concatenate([coef[f], coef[f]], axis=1)
        head, tail = roll(wide, 120 + f, 1), roll(wide, 120 + f - 63, 1)
        first = jnp.where(lane == 120 + f, jnp.where(odd, head, tail), first)
        last = jnp.where(lane == 120 + f, jnp.where(odd, tail, head), last)
    near[1, 0:ROWS, :] = first
    far[1, 0:ROWS, :] = last


def unpack(near, far, p):
    odd = parity("gy")
    right = jnp.where(odd, far, near)
    left = jnp.where(odd, near, far)
    lane = iota(near.shape, 1)
    return jnp.where(
        lane < 8,
        roll(right, -8 * (p % 16), 1),
        jnp.where(lane >= 120, roll(left, 120 - 8 * (p % 16), 1), 0.0),
    )


def scale(code, jac, scaled):
    plain = (code == 1.0) | (code == 3.0)
    interior = code == 1.0
    for f in range(F):
        kept = interior if f in (1, 2) else plain
        scaled[f] = jnp.where(kept, 0.8 / jac[F * f + f], 0.0)


def own_kernel(
    jac_in, rhs_in, flags, far_y, near_y, coef, jac, rhs, scaled, low, high, block, diag
):
    near, far = [near_y[0], near_y[1]], [far_y[0], far_y[1]]
    for p in range(F * F):
        jac[p, :, 0:TY] = jac_in[p // F, p % F]
        jac[p, :, TY:EY] = unpack(near[p // 16], far[p // 16], p)
    for f in range(F):
        rhs[f, :, 0:TY] = rhs_in[f]
        rhs[f, :, TY:EY] = unpack(near[1], far[1], F * F + f)
    aside = unpack(near[1], far[1], F * F + F)
    code = jnp.concatenate([(flags[...] + 1).astype(F32), aside], axis=1)
    scale(code, jac, scaled)

    lane = iota((ROWS, 128), 1)
    odd = parity("gy")
    right = jnp.where(odd, far[1], near[1])[0:ROWS]
    left = jnp.where(odd, near[1], far[1])[0:ROWS]
    diag[...] = jnp.full((8 * ROWS, 128), 4.0, F32)
    for f in range(F):
        wide = jnp.concatenate([coef[f], coef[f]], axis=1)
        wide = jnp.where(lane == 64, roll(right, 64 - 120 - f, 1), wide)
        wide = jnp.where(lane == 65, roll(left, 65 - 120 - f, 1), wide)
        wide = jnp.where((lane <= 65) & (wide > 0.0), wide, 4.0)
        for k in range(ROWS):
            diag[8 * k + f : 8 * k + f + 1, :] = wide[k : k + 1, :]
    lows, highs = [], []
    for k in range(ROWS):
        d = diag[8 * k : 8 * k + 8, :]
        inverse = 1.0 / (d - highs[-1] if k else d)
        lows.append(lows[-1] * inverse if k else inverse)
        highs.append(inverse)
        low[8 * k : 8 * k + 8] = lows[k]
        high[8 * k : 8 * k + 8] = highs[k]
    first_low = lows[-1]
    for k in range(ROWS - 2, -1, -1):
        first_low = lows[k] + highs[k] * first_low
    lane = iota((8, 128), 1)
    last = highs[-1]
    for q, part in ((2, first_low), (3, lows[-1]), (4, highs[-1])):
        last = jnp.where(lane >> 1 == 32 + q, roll(part, 2 * q, 1), last)
    block[...] = jnp.zeros((16, 128), F32)
    block[F : 2 * F] = jnp.where(lane < 64, first_low, roll(lows[-1], 64, 1))[0:F]
    block[2 * F : 3 * F] = last[0:F]


def residual(f, state, rhs, jac):
    own = state[f]
    beside = roll(own, 1, 0) + roll(own, -1, 0) + roll(own, 1, 1) + roll(own, -1, 1)
    total = rhs(f) + beside
    for g in range(F):
        total = total - jac(F * f + g) * state[g]
    return total


def sweep(old, new, scaled, rhs, jac):
    for f in range(F):
        new[f] = old[f] + scaled(f) * residual(f, old, rhs, jac)


def planes_of(own, beyond):
    return lambda p: jnp.concatenate([beyond[p, 0:8], own[p], beyond[p, 8:16]], axis=0)


def columns(shape, fine_dim, coarse_dim):
    fine = iota(shape, fine_dim)
    coarse = iota(shape, coarse_dim)
    here = (coarse <= 64) & (fine >> 2 == coarse)
    return (here | ((coarse == 65) & (fine >= EY - 4))).astype(F32)


def before_kernel(
    jac_own, rhs_own, scaled_own, high, block, far_x, near_x,
    state, jac, rhs, scaled, value, sent, other, sides, means, whole_block,
):
    odd = parity("gx")
    sides[0] = jnp.where(odd, near_x[...], far_x[...])
    sides[1] = jnp.where(odd, far_x[...], near_x[...])
    none = jnp.zeros((16, TY), F32)

    def corners(start, a):
        lanes = slice(128 * a, 128 * (a + 1))
        return jnp.concatenate([sides[s, start : start + 8, lanes] for s in range(2)], axis=0)

    far = [corners(136, a) for a in range(2)]
    near = [corners(144, a) for a in range(2)]
    for p in range(F * F):
        jac[p, :, 0:TY] = none
        jac[p, 4:8, 0:TY] = sides[0, 4 * p : 4 * p + 4]
        jac[p, 8:12, 0:TY] = sides[1, 4 * p : 4 * p + 4]
        if p % (F + 1) == 0:
            f = p // (F + 1)
            jac[p, 3:4, 0:TY] = sides[0, 130 + f : 131 + f]
            jac[p, 12:13, 0:TY] = sides[1, 130 + f : 131 + f]
        jac[p, :, TY:EY] = unpack(near[p // 16], far[p // 16], p)
    for f in range(F):
        rhs[f, :, 0:TY] = none
        rhs[f, 3:8, 0:TY] = sides[0, 100 + 5 * f : 105 + 5 * f]
        rhs[f, 8:13, 0:TY] = sides[1, 100 + 5 * f : 105 + 5 * f]
        rhs[f, :, TY:EY] = unpack(near[1], far[1], F * F + f)
    code = scaled.at[F - 1]
    code[:, 0:TY] = none
    code[3:8, 0:TY] = sides[0, 125:130]
    code[8:13, 0:TY] = sides[1, 125:130]
    code[:, TY:EY] = unpack(near[1], far[1], F * F + F)
    scale(code[...], jac, scaled)

    jac_plane, rhs_plane = planes_of(jac_own, jac), planes_of(rhs_own, rhs)
    scaled_plane = planes_of(scaled_own, scaled)
    for f in range(F):
        state[f] = scaled_plane(f) * rhs_plane(f)
    sweep(state, other, scaled_plane, rhs_plane, jac_plane)
    sweep(other, state, scaled_plane, rhs_plane, jac_plane)
    means[...] = jnp.zeros((8 * ROWS, EY), F32)
    for f in range(F):
        left_over = residual(f, state, rhs_plane, jac_plane)[8 : 8 + TX]
        left_over = left_over + roll(left_over, -1, 0)
        left_over = left_over + roll(left_over, -2, 0)
        for k in range(ROWS):
            means[8 * k + f : 8 * k + f + 1, :] = left_over[4 * k : 4 * k + 1]
    mean = select_columns(means[...] * 0.0625, columns((EY, 128), 0, 1))
    values = []
    for k in range(ROWS):
        rows = slice(8 * k, 8 * k + 8)
        here = mean[rows] + values[-1] if k else mean[rows]
        values.append(here * high[rows, :])
        value[rows] = values[k]
    first, last = values[-1], values[-1]
    for k in range(ROWS - 2, -1, -1):
        first = values[k] + high[8 * k : 8 * k + 8, :] * first
    lane = iota((8, 128), 1)
    ends = jnp.where(lane >> 1 == 32, first, roll(last, 2, 1))[0:F]
    whole_block[...] = block[...]
    whole_block[0:F] = jnp.where(lane < 64, first, roll(last, 64, 1))[0:F]
    kept = whole_block[2 * F : 3 * F]
    pair = lane[0:F] >> 1
    whole_block[2 * F : 3 * F] = jnp.where((pair == 32) | (pair == 33), ends, kept)
    whole = whole_block[...]
    for k in range(sent.shape[0]):
        sent[k] = whole


def merge(one, two):
    a0, a1, b0, c, c1 = one
    d0, d1, e0, g, g1 = two
    w = 1.0 / (1.0 - c1 * e0)
    cw, gw = c * w, g * w
    return (
        a0 + cw * (d0 + e0 * a1),
        d1 + gw * (a1 + c1 * d0),
        b0 + c * cw * e0,
        cw * g,
        g1 + g * gw * c1,
    )


def between(one, two, below, above):
    a0, a1, b0, c, c1 = one
    d0, d1, e0, g, g1 = two
    outer = d0 + g * above
    last = (a1 + c * below + c1 * outer) / (1.0 - c1 * e0)
    return last, outer + e0 * last


def after_kernel(
    jac_own, rhs_own, scaled_own, low, high, jac_beyond, rhs_beyond, scaled_beyond, state_in, value, got,
    correction_out, level_residual_out,
    state, other, ends, spread, tree, correction, level_residual, sems,
):
    count = got.shape[0]
    me = lax.axis_index("gx")
    lane = iota((F, 128), 1)

    def segment(k):
        one, two, three = got[k, 0:F, :], got[k, F : 2 * F, :], got[k, 2 * F : 3 * F, :]
        main = [one, roll(one, 64, 1), two, roll(two, 64, 1), three]
        return [jnp.where(lane < 64, main[q], roll(three, -2 * q, 1)) for q in range(5)]

    level, starts, total = [segment(k) for k in range(count)], [], 0
    while len(level) > 2:
        level = [merge(level[2 * k], level[2 * k + 1]) for k in range(len(level) // 2)]
        starts.append(total)
        for parts in level:
            for q in range(5):
                tree[total, q, 0:F] = parts[q]
            total += 1
    below = above = jnp.zeros((F, 128), F32)
    for size in range(len(starts), -1, -1):
        pair = me >> (size + 1)
        if size:
            at = starts[size - 1] + 2 * pair
            one = [tree[at, q, 0:F] for q in range(5)]
            two = [tree[at + 1, q, 0:F] for q in range(5)]
        else:
            one, two = segment(2 * pair), segment(2 * pair + 1)
        last, first = between(one, two, below, above)
        second = (me >> size) & 1 == 1
        below, above = jnp.where(second, last, below), jnp.where(second, above, first)

    used = lane <= 65
    ends[...] = jnp.zeros((64, 128), F32)
    ends[0:F] = jnp.where(used, below, 0.0)
    ends[8 * (ROWS + 1) : 8 * (ROWS + 1) + F] = jnp.where(used, above, 0.0)
    here = above
    for k in range(ROWS - 1, -1, -1):
        rows = slice(8 * k, 8 * k + F)
        here = value[rows] + low[rows] * below + high[rows] * here
        ends[8 * (k + 1) : 8 * (k + 1) + F] = jnp.where(used, here, 0.0)
    spread[...] = select_columns(ends[...], columns((128, EY), 1, 0))

    jac_plane, rhs_plane = planes_of(jac_own, jac_beyond), planes_of(rhs_own, rhs_beyond)
    scaled_plane = planes_of(scaled_own, scaled_beyond)
    upper = iota((8, EY), 0) < 4

    def repeated(row):
        return jnp.broadcast_to(spread[row : row + 1, :], (8, EY))

    for f in range(F):
        tiles = []
        for v in range(EX // 8):
            one = repeated(8 * (2 * v - 1) + f) if v else 0.0
            two = repeated(8 * (2 * v) + f) if v < EX // 8 - 1 else 0.0
            tiles.append(jnp.where(upper, one, two))
        added = jnp.where(scaled_plane(f) != 0.0, jnp.concatenate(tiles, axis=0), 0.0)
        state[f] = state_in[f] + added
    sweep(state, other, scaled_plane, rhs_plane, jac_plane)
    sweep(other, state, scaled_plane, rhs_plane, jac_plane)
    copies = []
    for f in range(F):
        correction[f] = state[f, 8 : 8 + TX, 0:TY]
        copies.append(
            pltpu.make_async_copy(correction.at[f], correction_out.at[f], sems.at[0, f])
        )
        copies[-1].start()
    for f in range(F):
        level_residual[f] = residual(f, state, rhs_plane, jac_plane)[8 : 8 + TX, 0:TY]
        copies.append(
            pltpu.make_async_copy(level_residual.at[f], level_residual_out.at[f], sems.at[1, f])
        )
        copies[-1].start()
    for copy in copies:
        copy.wait()


def shape_of(*dims):
    return jax.ShapeDtypeStruct(dims, F32)


def call(kernel, outs, scratch, *args, space=pltpu.VMEM, out_space=pltpu.VMEM):
    return pl.pallas_call(
        kernel,
        out_shape=outs,
        in_specs=[pl.BlockSpec(memory_space=space)] * len(args),
        out_specs=[pl.BlockSpec(memory_space=out_space)] * len(outs),
        scratch_shapes=scratch,
        compiler_params=pltpu.CompilerParams(vmem_limit_bytes=32 * 1024 * 1024),
    )(*args)


def swap(value, axis, start):
    count = lax.axis_size(axis)
    firsts = range(start, count - 1, 2)
    return lax.ppermute(value, axis, [(i, i + 1) for i in firsts] + [(i + 1, i) for i in firsts])


def local(fine, owner, flags, jac, coef):
    strip = shape_of(2, TX, 128)
    rows = shape_of(136, TY)
    rhs, top, bottom, near, far = call(
        restrict_kernel,
        [shape_of(F, TX, TY), rows, rows, strip, strip],
        [
            pltpu.VMEM((F, 4, 2 * TX, 128), F32),
            pltpu.VMEM((4, 2 * TX, 128), jnp.int32),
            pltpu.VMEM((TX, TY), jnp.int32),
            pltpu.VMEM((F, F, TX, TY), F32),
            pltpu.VMEM((F, ROWS, TY // 4), F32),
            pltpu.SemaphoreType.DMA((F + 2, 4)),
        ],
        *[pltpu.with_memory_space_constraint(x, pltpu.HBM) for x in (fine, owner, flags, jac, coef)],
        space=pltpu.HBM,
    )
    far_y = swap(far, "gy", 1)
    near_y = swap(near, "gy", 0)

    def with_corners(own, rows):
        corners = [jnp.concatenate([side[0, rows], side[1, rows]], axis=1) for side in (far_y, near_y)]
        return jnp.concatenate([own, *corners], axis=0)

    top = with_corners(top, slice(0, 8))
    bottom = with_corners(bottom, slice(TX - 8, TX))
    odd = parity("gx")
    far_x = swap(jnp.where(odd, bottom, top), "gx", 1)
    near_x = swap(jnp.where(odd, top, bottom), "gx", 0)
    count = lax.axis_size("gx")
    lines = shape_of(8 * ROWS, 128)
    own = shape_of(F, TX, EY)
    jac_own, rhs_own, scaled_own, low, high, block = call(
        own_kernel,
        [shape_of(F * F, TX, EY), own, own, lines, lines, shape_of(16, 128)],
        [pltpu.VMEM((8 * ROWS, 128), F32)],
        jac, rhs, flags, far_y, near_y, coef,
    )
    tile = pltpu.VMEM((F, EX, EY), F32)
    beyond = shape_of(F, 16, EY)
    state, jac_beyond, rhs_beyond, scaled_beyond, value, sent = call(
        before_kernel,
        [shape_of(F, EX, EY), shape_of(F * F, 16, EY), beyond, beyond, lines, shape_of(count, 16, 128)],
        [tile, pltpu.VMEM((2, 152, TY), F32), pltpu.VMEM((8 * ROWS, EY), F32), pltpu.VMEM((16, 128), F32)],
        jac_own, rhs_own, scaled_own, high, block, far_x, near_x,
    )
    got = lax.all_to_all(sent, "gx", 0, 0, tiled=True)
    return tuple(
        call(
            after_kernel,
            [shape_of(F, TX, TY), shape_of(F, TX, TY)],
            [
                tile,
                tile,
                pltpu.VMEM((64, 128), F32),
                pltpu.VMEM((64, EY), F32),
                pltpu.VMEM((count, 5, 8, 128), F32),
                pltpu.VMEM((F, TX, TY), F32),
                pltpu.VMEM((F, TX, TY), F32),
                pltpu.SemaphoreType.DMA((2, F)),
            ],
            jac_own, rhs_own, scaled_own, low, high, jac_beyond, rhs_beyond, scaled_beyond, state, value, got,
            out_space=pl.ANY,
        )
    )


def solution(mesh):
    in_specs = (
        P(None, "gx", "gy"),
        P("gx", "gy"),
        P("gx", "gy"),
        P(None, None, "gx", "gy"),
        P(None, "gx", "gy"),
    )
    out_specs = (P(None, "gx", "gy"), P(None, "gx", "gy"))
    return jax.shard_map(local, mesh=mesh, in_specs=in_specs, out_specs=out_specs, check_vma=False)
```

time: 65.5 us -> 64.4 us (0.983)
  Pallas kernels: 7.33 us -> 6.35 us
    pallas_call x3 -> x4, Pallas kernels: 7.33 us -> 6.35 us  [call(): pl.pallas_call(kernel, out_shape=outs, in_specs=[pl.BlockSpec(memory_spac...]
  transfers between devices with their start and end apart: 4 -> 4, of which waited for: 3 -> 3; matrix products, arithmetic and copies ran while one was open for 0% -> 0% of each run, Pallas kernels for 0% -> 1%
where the time goes in v3:
time: 64.4 us; the launch traced here: 64.1 us
  blocking collectives  34.1 us (53%)
  starting transfers between devices  19.2 us (30%)
  Pallas kernels  6.35 us (10%)
  waiting for transfers between devices  3.58 us (6%)
  between operations  0.76 us (1%)
    all_to_all x1, blocking collectives, local(): got = lax.all_to_all(sent, 'gx', 0, 0, tiled=True)  34.1 us
    ppermute x4, starting transfers between devices, swap(): lax.ppermute(value, axis, [(i, i + 1) for i in firsts] + [(i + 1, i) for...  19.2 us
    pallas_call x4, Pallas kernels, call(): pl.pallas_call(kernel, out_shape=outs, in_specs=[pl.BlockSpec(memory_spac...  6.35 us
    ppermute x4, waiting for transfers between devices, swap(): lax.ppermute(value, axis, [(i, i + 1) for i in firsts] + [(i + 1, i) for...  3.58 us
  transfers between devices with their start and end apart: 4, of which 3 were waited for; matrix products, arithmetic and copies ran while one was open for 0% of the time, Pallas kernels for 1%

profile of v3, /device:TPU:89, one launch (start us, length us, event | category | flops | bytes accessed | tf_op | source)
XLA Modules:
  0.0 64.1 jit_solution(9622116363449881957)
XLA Ops:
  0.6 2.4 %shard_map.68 = (f32[5,24,256]{2,1,0:T(8,128)S(1)}, f32[136,256]{1,0:T(8,128)S(1)}, f32[136,256]{1,0:T(8,128)S(1)}, f32[2,24,128]{2,1,0:T(8,128)S(1)}, f32[2,24,128]{2,1,0:T(8,128)S(1)}) custom-call(f32[5,48,512]{2,1,0:T(8,128)} %fine_in.1, s32[48,512]{1,0:T(8,128)} %owner_in.1, s32[24,256]{1,0:T(8,128)} %flags.1, f32[5,5,24,256]{3,2,1,0:T(8,128)} %jac_in.3, ...), custom_call_target="tpu_custom_call" | custom-call | tf_op jit(solution)/shard_map/pallas_call | solution.py:416
  3.1 0.0 copy-start
  3.1 4.5 %collective-permute-start = (f32[2,24,128]{2,1,0:T(8,128)S(1)}, f32[2,24,128]{2,1,0:T(8,128)S(1)}, u32[]{:S(2)}, u32[]{:S(2)}) collective-permute-start(f32[2,24,128]{2,1,0:T(8,128)S(1)} %get-tuple-element.20), channel_id=1, source_target_pairs={{1,2},{3,4},{5,6},{7,8},{9,10},{11,12},{13,14},{15,16},{17,18},{19... | collective-permute-start | bytes 73736 | tf_op jit(solution)/shard_map/ppermute | solution.py:429
  7.6 1.9 %collective-permute-start.1 = (f32[2,24,128]{2,1,0:T(8,128)S(1)}, f32[2,24,128]{2,1,0:T(8,128)S(1)}, u32[]{:S(2)}, u32[]{:S(2)}) collective-permute-start(f32[2,24,128]{2,1,0:T(8,128)S(1)} %get-tuple-element.21), channel_id=1, source_target_pairs={{0,1},{2,3},{4,5},{6,7},{8,9},{10,11},{12,13},{14,15},{16,17},{18,... | collective-permute-start | bytes 73736 | tf_op jit(solution)/shard_map/ppermute | solution.py:429
  9.6 0.0 collective-permute-done.far_y
  9.6 2.6 %collective-permute-done.1.near_y = f32[2,24,128]{2,1,0:T(8,128)S(1)} collective-permute-done((f32[2,24,128]{2,1,0:T(8,128)S(1)}, f32[2,24,128]{2,1,0:T(8,128)S(1)}, u32[]{:S(2)}, u32[]{:S(2)}) %collective-permute-start.1) | collective-permute-done | bytes 24608 | tf_op jit(solution)/shard_map/ppermute | solution.py:429
  12.2 0.0 copy-start.1
  12.2 0.0 copy-start.2
  12.3 10.8 %collective-permute-start.2 = (f32[152,256]{1,0:T(8,128)S(1)}, f32[152,256]{1,0:T(8,128)S(1)}, u32[]{:S(2)}, u32[]{:S(2)}) collective-permute-start(f32[152,256]{1,0:T(8,128)S(1)} %broadcast_select_fusion.1), channel_id=1, source_target_pairs={{24,48},{72,96},{120,144},{168,192},{216,240},{264,288},{312,336},... | collective-permute-start | bytes 466952 | tf_op jit(solution)/shard_map/ppermute | solution.py:429
  23.1 1.9 %collective-permute-start.3 = (f32[152,256]{1,0:T(8,128)S(1)}, f32[152,256]{1,0:T(8,128)S(1)}, u32[]{:S(2)}, u32[]{:S(2)}) collective-permute-start(f32[152,256]{1,0:T(8,128)S(1)} %broadcast_select_fusion), channel_id=1, source_target_pairs={{0,24},{48,72},{96,120},{144,168},{192,216},{240,264},{288,312},{3... | collective-permute-start | bytes 466952 | tf_op jit(solution)/shard_map/ppermute | solution.py:429
  25.0 0.0 copy-done
  25.0 0.0 copy-done.1
  25.1 0.0 copy-done.2
  25.1 0.3 shard_map.69
  25.4 0.6 collective-permute-done.2.far_x
  26.0 0.4 collective-permute-done.3.near_x
  26.4 1.6 %shard_map.70 = (f32[5,40,384]{2,1,0:T(8,128)S(1)}, f32[25,16,384]{2,1,0:T(8,128)S(1)}, f32[5,16,384]{2,1,0:T(8,128)S(1)}, f32[5,16,384]{2,1,0:T(8,128)S(1)}, f3...) custom-call(f32[25,24,384]{2,1,0:T(8,128)S(1)} %get-tuple-element.22.jac_own, ...), custom_call_target="tpu_custom_call" | custom-call | tf_op jit(solution)/shard_map/pallas_call | solution.py:416
  28.0 34.1 %all_to_all.5.got = f32[32,16,128]{2,1,0:T(8,128)S(1)} all-to-all(f32[32,16,128]{2,1,0:T(8,128)S(1)} %get-tuple-element.35), channel_id=1, replica_groups=mesh['gx'=32,'gy'=24] {'gx'}, dimensions={0} | all-to-all | bytes 524288 | tf_op jit(solution)/shard_map/all_to_all | solution.py:478
  62.1 2.0 %shard_map.71 = (f32[5,24,256]{2,1,0:T(8,128)}, f32[5,24,256]{2,1,0:T(8,128)}) custom-call(f32[25,24,384]{2,1,0:T(8,128)S(1)} %get-tuple-element.22.jac_own, f32[5,24,384]{2,1,0:T(8,128)S(1)} %get-tuple-element.23.rhs_own, f32[5,24,384]{2,1,0:T(8,128)S(1)} %get-tuple-element.24.scaled_own, f32[48,128]{1,0:T(8,128)S(1)} %get-tuple-element.25.low, ...), custom_call_target="tpu_custom_call" | custom-call | tf_op jit(solution)/shard_map/pallas_call | solution.py:416
  (4 shorter events, 0.1 us)
Async XLA Ops:
  3.1 22.0 %copy-start = (f32[5,5,24,256]{3,2,1,0:T(8,128)S(1)}, f32[5,5,24,256]{3,2,1,0:T(8,128)}, u32[]{:S(2)}) copy-start(f32[5,5,24,256]{3,2,1,0:T(8,128)} %jac_in.3) | copy-start | bytes 1843204
  3.1 6.5 %collective-permute-start = (f32[2,24,128]{2,1,0:T(8,128)S(1)}, f32[2,24,128]{2,1,0:T(8,128)S(1)}, u32[]{:S(2)}, u32[]{:S(2)}) collective-permute-start(f32[2,24,128]{2,1,0:T(8,128)S(1)} %get-tuple-element.20), channel_id=1, source_target_pairs={{1,2},{3,4},{5,6},{7,8},{9,10},{11,12},{13,14},{15,16},{17,18},{19... | collective-permute-start | bytes 73736 | tf_op jit(solution)/shard_map/ppermute | solution.py:429
  7.6 4.6 %collective-permute-start.1 = (f32[2,24,128]{2,1,0:T(8,128)S(1)}, f32[2,24,128]{2,1,0:T(8,128)S(1)}, u32[]{:S(2)}, u32[]{:S(2)}) collective-permute-start(f32[2,24,128]{2,1,0:T(8,128)S(1)} %get-tuple-element.21), channel_id=1, source_target_pairs={{0,1},{2,3},{4,5},{6,7},{8,9},{10,11},{12,13},{14,15},{16,17},{18,... | collective-permute-start | bytes 73736 | tf_op jit(solution)/shard_map/ppermute | solution.py:429
  12.2 12.8 %copy-start.1 = (s32[24,256]{1,0:T(8,128)S(1)}, s32[24,256]{1,0:T(8,128)}, u32[]{:S(2)}) copy-start(s32[24,256]{1,0:T(8,128)} %flags.1) | copy-start | bytes 73732
  12.2 12.8 %copy-start.2 = (f32[5,6,64]{2,1,0:T(8,128)S(1)}, f32[5,6,64]{2,1,0:T(8,128)}, u32[]{:S(2)}) copy-start(f32[5,6,64]{2,1,0:T(8,128)} %coef.1) | copy-start | bytes 23044
  12.3 13.7 %collective-permute-start.2 = (f32[152,256]{1,0:T(8,128)S(1)}, f32[152,256]{1,0:T(8,128)S(1)}, u32[]{:S(2)}, u32[]{:S(2)}) collective-permute-start(f32[152,256]{1,0:T(8,128)S(1)} %broadcast_select_fusion.1), channel_id=1, source_target_pairs={{24,48},{72,96},{120,144},{168,192},{216,240},{264,288},{312,336},... | collective-permute-start | bytes 466952 | tf_op jit(solution)/shard_map/ppermute | solution.py:429
  23.1 3.3 %collective-permute-start.3 = (f32[152,256]{1,0:T(8,128)S(1)}, f32[152,256]{1,0:T(8,128)S(1)}, u32[]{:S(2)}, u32[]{:S(2)}) collective-permute-start(f32[152,256]{1,0:T(8,128)S(1)} %broadcast_select_fusion), channel_id=1, source_target_pairs={{0,24},{48,72},{96,120},{144,168},{192,216},{240,264},{288,312},{3... | collective-permute-start | bytes 466952 | tf_op jit(solution)/shard_map/ppermute | solution.py:429

commit v4 on v3

--- a/solution.py
+++ b/solution.py
@@ -43,7 +43,7 @@
 
 
 def restrict_kernel(
-    fine_in, owner_in, flags_in, jac_in, coef_in, rhs, top, bottom, near, far,
+    fine_in, owner_in, flags_in, jac_in, coef_in, rhs, near, far,
     fine, owner, flags, jac, coef, sems,
 ):
     def tile_copy(source, target, sem, j):
@@ -61,7 +61,7 @@
     ]
     for copy in owners + sum(fines, []) + late:
         copy.start()
-    for copy in owners:
+    for copy in owners + sum(fines, []) + late:
         copy.wait()
 
     def halves(load):
@@ -80,8 +80,6 @@
     masks = [[code == k for code in codes] for k in range(9)]
     gathered = []
     for f in range(F):
-        for copy in fines[f]:
-            copy.wait()
         values = halves(lambda j, rows: fine[f, j, rows, :])
         total = None
         for dy in (-1, 0, 1):
@@ -100,21 +98,7 @@
     planes = [summed[TX * f : TX * (f + 1)] for f in range(F)]
     for f in range(F):
         rhs[f] = planes[f]
-    for copy in late:
-        copy.wait()
     planes.append((flags[...] + 1).astype(F32))
-
-    for p in range(F * F):
-        top[4 * p : 4 * p + 4] = jac[p // F, p % F, 0:4, :]
-        bottom[4 * p : 4 * p + 4] = jac[p // F, p % F, TX - 4 : TX, :]
-    for p in range(F + 1):
-        top[100 + 5 * p : 105 + 5 * p] = planes[p][0:5]
-        bottom[100 + 5 * p : 105 + 5 * p] = planes[p][TX - 5 : TX]
-    for f in range(F):
-        top[130 + f : 131 + f] = jac[f, f, 4:5, :]
-        bottom[130 + f : 131 + f] = jac[f, f, TX - 5 : TX - 4, :]
-    top[135:136] = jnp.zeros((1, TY), F32)
-    bottom[135:136] = jnp.zeros((1, TY), F32)
 
     odd = parity("gy")
     slot = iota((TX, 128), 1) >> 3
@@ -142,6 +126,49 @@
         last = jnp.where(lane == 120 + f, jnp.where(odd, tail, head), last)
     near[1, 0:ROWS, :] = first
     far[1, 0:ROWS, :] = last
+
+
+JAC_AT, RHS_AT, CODE_AT, DIAG_AT, CORNER_AT, ROWS_SENT = 0, 50, 65, 68, 74, 80
+
+
+def rows_kernel(jac, rhs, flags, near, far):
+    def write(out, first):
+        start = 0 if first else TX - 2
+        wide = 0 if first else TX - 3
+        third = 2 if first else TX - 3
+        for p in range(F * F):
+            out[2 * p : 2 * p + 2] = jac[p // F, p % F, start : start + 2, :]
+        for f in range(F):
+            at = RHS_AT + 3 * f
+            out[at : at + 3] = rhs[f, wide : wide + 3, :]
+            out[DIAG_AT + f : DIAG_AT + f + 1] = jac[f, f, third : third + 1, :]
+        out[CODE_AT : CODE_AT + 3] = (flags[wide : wide + 3, :] + 1).astype(F32)
+        out[73:ROWS_SENT] = jnp.zeros((ROWS_SENT - 73, TY), F32)
+
+    odd = parity("gx")
+
+    @pl.when(odd)
+    def _():
+        write(near, True)
+        write(far, False)
+
+    @pl.when(jnp.logical_not(odd))
+    def _():
+        write(near, False)
+        write(far, True)
+
+
+def corners_kernel(near_rows, far_rows, far_y, near_y, near, far):
+    odd = parity("gx")
+    near[...] = near_rows[...]
+    far[...] = far_rows[...]
+    for side, strip in enumerate((far_y, near_y)):
+        at = CORNER_AT + 3 * side
+        for a in range(2):
+            lanes = slice(128 * a, 128 * (a + 1))
+            first, last = strip[a, 0:3, :], strip[a, TX - 3 : TX, :]
+            near[at : at + 3, lanes] = jnp.where(odd, first, last)
+            far[at : at + 3, lanes] = jnp.where(odd, last, first)
 
 
 def unpack(near, far, p):
@@ -237,37 +264,40 @@
 
 def before_kernel(
     jac_own, rhs_own, scaled_own, high, block, far_x, near_x,
-    state, jac, rhs, scaled, value, sent, other, sides, means, whole_block,
+    state, jac, rhs, scaled, value, sent, near_state, far_state, other, sides, beside, means, whole_block,
 ):
     odd = parity("gx")
     sides[0] = jnp.where(odd, near_x[...], far_x[...])
     sides[1] = jnp.where(odd, far_x[...], near_x[...])
     none = jnp.zeros((16, TY), F32)
 
-    def corners(start, a):
-        lanes = slice(128 * a, 128 * (a + 1))
-        return jnp.concatenate([sides[s, start : start + 8, lanes] for s in range(2)], axis=0)
-
-    far = [corners(136, a) for a in range(2)]
-    near = [corners(144, a) for a in range(2)]
+    def put(out, at, rows):
+        out[8 - rows : 8, 0:TY] = sides[0, at : at + rows]
+        out[8 : 8 + rows, 0:TY] = sides[1, at : at + rows]
+
+    for side in range(2):
+        at = CORNER_AT + 3 * side
+        for a in range(2):
+            lanes = slice(128 * a, 128 * (a + 1))
+            beside[side, a] = jnp.zeros((16, 128), F32)
+            beside[side, a, 5:8] = sides[0, at : at + 3, lanes]
+            beside[side, a, 8:11] = sides[1, at : at + 3, lanes]
+    far, near = [[beside[side, a] for a in range(2)] for side in range(2)]
     for p in range(F * F):
         jac[p, :, 0:TY] = none
-        jac[p, 4:8, 0:TY] = sides[0, 4 * p : 4 * p + 4]
-        jac[p, 8:12, 0:TY] = sides[1, 4 * p : 4 * p + 4]
+        put(jac.at[p], 2 * p, 2)
         if p % (F + 1) == 0:
             f = p // (F + 1)
-            jac[p, 3:4, 0:TY] = sides[0, 130 + f : 131 + f]
-            jac[p, 12:13, 0:TY] = sides[1, 130 + f : 131 + f]
+            jac[p, 5:6, 0:TY] = sides[0, DIAG_AT + f : DIAG_AT + f + 1]
+            jac[p, 10:11, 0:TY] = sides[1, DIAG_AT + f : DIAG_AT + f + 1]
         jac[p, :, TY:EY] = unpack(near[p // 16], far[p // 16], p)
     for f in range(F):
         rhs[f, :, 0:TY] = none
-        rhs[f, 3:8, 0:TY] = sides[0, 100 + 5 * f : 105 + 5 * f]
-        rhs[f, 8:13, 0:TY] = sides[1, 100 + 5 * f : 105 + 5 * f]
+        put(rhs.at[f], RHS_AT + 3 * f, 3)
         rhs[f, :, TY:EY] = unpack(near[1], far[1], F * F + f)
     code = scaled.at[F - 1]
     code[:, 0:TY] = none
-    code[3:8, 0:TY] = sides[0, 125:130]
-    code[8:13, 0:TY] = sides[1, 125:130]
+    put(code, CODE_AT, 3)
     code[:, TY:EY] = unpack(near[1], far[1], F * F + F)
     scale(code[...], jac, scaled)
 
@@ -277,6 +307,12 @@
         state[f] = scaled_plane(f) * rhs_plane(f)
     sweep(state, other, scaled_plane, rhs_plane, jac_plane)
     sweep(other, state, scaled_plane, rhs_plane, jac_plane)
+    near_state[15:16] = jnp.zeros((1, EY), F32)
+    far_state[15:16] = jnp.zeros((1, EY), F32)
+    for f in range(F):
+        first, last = state[f, 8:11], state[f, 5 + TX : 8 + TX]
+        near_state[3 * f : 3 * f + 3] = jnp.where(odd, first, last)
+        far_state[3 * f : 3 * f + 3] = jnp.where(odd, last, first)
     means[...] = jnp.zeros((8 * ROWS, EY), F32)
     for f in range(F):
         left_over = residual(f, state, rhs_plane, jac_plane)[8 : 8 + TX]
@@ -329,7 +365,7 @@
 
 
 def after_kernel(
-    jac_own, rhs_own, scaled_own, low, high, jac_beyond, rhs_beyond, scaled_beyond, state_in, value, got,
+    jac_own, rhs_own, scaled_own, low, high, jac_beyond, rhs_beyond, scaled_beyond, state_in, value, far_state, near_state, got,
     correction_out, level_residual_out,
     state, other, ends, spread, tree, correction, level_residual, sems,
 ):
@@ -377,6 +413,7 @@
     jac_plane, rhs_plane = planes_of(jac_own, jac_beyond), planes_of(rhs_own, rhs_beyond)
     scaled_plane = planes_of(scaled_own, scaled_beyond)
     upper = iota((8, EY), 0) < 4
+    odd = parity("gx")
 
     def repeated(row):
         return jnp.broadcast_to(spread[row : row + 1, :], (8, EY))
@@ -388,7 +425,11 @@
             two = repeated(8 * (2 * v) + f) if v < EX // 8 - 1 else 0.0
             tiles.append(jnp.where(upper, one, two))
         added = jnp.where(scaled_plane(f) != 0.0, jnp.concatenate(tiles, axis=0), 0.0)
-        state[f] = state_in[f] + added
+        other[f] = state_in[f]
+        far, near = far_state[3 * f : 3 * f + 3], near_state[3 * f : 3 * f + 3]
+        other[f, 5:8] = jnp.where(odd, near, far)
+        other[f, 8 + TX : 11 + TX] = jnp.where(odd, far, near)
+        state[f] = other[f] + added
     sweep(state, other, scaled_plane, rhs_plane, jac_plane)
     sweep(other, state, scaled_plane, rhs_plane, jac_plane)
     copies = []
@@ -431,10 +472,9 @@
 
 def local(fine, owner, flags, jac, coef):
     strip = shape_of(2, TX, 128)
-    rows = shape_of(136, TY)
-    rhs, top, bottom, near, far = call(
+    rhs, near, far = call(
         restrict_kernel,
-        [shape_of(F, TX, TY), rows, rows, strip, strip],
+        [shape_of(F, TX, TY), strip, strip],
         [
             pltpu.VMEM((F, 4, 2 * TX, 128), F32),
             pltpu.VMEM((4, 2 * TX, 128), jnp.int32),
@@ -446,18 +486,15 @@
         *[pltpu.with_memory_space_constraint(x, pltpu.HBM) for x in (fine, owner, flags, jac, coef)],
         space=pltpu.HBM,
     )
+    near_rows, far_rows = call(
+        rows_kernel, [shape_of(ROWS_SENT, TY), shape_of(ROWS_SENT, TY)], [], jac, rhs, flags
+    )
     far_y = swap(far, "gy", 1)
     near_y = swap(near, "gy", 0)
-
-    def with_corners(own, rows):
-        corners = [jnp.concatenate([side[0, rows], side[1, rows]], axis=1) for side in (far_y, near_y)]
-        return jnp.concatenate([own, *corners], axis=0)
-
-    top = with_corners(top, slice(0, 8))
-    bottom = with_corners(bottom, slice(TX - 8, TX))
-    odd = parity("gx")
-    far_x = swap(jnp.where(odd, bottom, top), "gx", 1)
-    near_x = swap(jnp.where(odd, top, bottom), "gx", 0)
+    rows = shape_of(ROWS_SENT, TY)
+    near_rows, far_rows = call(corners_kernel, [rows, rows], [], near_rows, far_rows, far_y, near_y)
+    far_x = swap(far_rows, "gx", 1)
+    near_x = swap(near_rows, "gx", 0)
     count = lax.axis_size("gx")
     lines = shape_of(8 * ROWS, 128)
     own = shape_of(F, TX, EY)
@@ -469,13 +506,22 @@
     )
     tile = pltpu.VMEM((F, EX, EY), F32)
     beyond = shape_of(F, 16, EY)
-    state, jac_beyond, rhs_beyond, scaled_beyond, value, sent = call(
+    ends = shape_of(16, EY)
+    state, jac_beyond, rhs_beyond, scaled_beyond, value, sent, near_state, far_state = call(
         before_kernel,
-        [shape_of(F, EX, EY), shape_of(F * F, 16, EY), beyond, beyond, lines, shape_of(count, 16, 128)],
-        [tile, pltpu.VMEM((2, 152, TY), F32), pltpu.VMEM((8 * ROWS, EY), F32), pltpu.VMEM((16, 128), F32)],
+        [shape_of(F, EX, EY), shape_of(F * F, 16, EY), beyond, beyond, lines, shape_of(count, 16, 128), ends, ends],
+        [
+            tile,
+            pltpu.VMEM((2, ROWS_SENT, TY), F32),
+            pltpu.VMEM((2, 2, 16, 128), F32),
+            pltpu.VMEM((8 * ROWS, EY), F32),
+            pltpu.VMEM((16, 128), F32),
+        ],
         jac_own, rhs_own, scaled_own, high, block, far_x, near_x,
     )
     got = lax.all_to_all(sent, "gx", 0, 0, tiled=True)
+    far_state = swap(far_state, "gx", 1)
+    near_state = swap(near_state, "gx", 0)
     return tuple(
         call(
             after_kernel,
@@ -490,7 +536,7 @@
                 pltpu.VMEM((F, TX, TY), F32),
                 pltpu.SemaphoreType.DMA((2, F)),
             ],
-            jac_own, rhs_own, scaled_own, low, high, jac_beyond, rhs_beyond, scaled_beyond, state, value, got,
+            jac_own, rhs_own, scaled_own, low, high, jac_beyond, rhs_beyond, scaled_beyond, state, value, far_state, near_state, got,
             out_space=pl.ANY,
         )
     )

time: 64.4 us -> 63.2 us (0.981)
  blocking collectives: 34.1 us -> 0 us
  starting transfers between devices: 19.2 us -> 41.6 us
  waiting for transfers between devices: 3.58 us -> 13.1 us
  Pallas kernels: 6.35 us -> 7.37 us
    all_to_all x1 -> x0, blocking collectives: 34.1 us -> none  [local(): got = lax.all_to_all(sent, 'gx', 0, 0, tiled=True)]
    all_to_all x0 -> x1, starting transfers between devices: none -> 14 us  [local(): got = lax.all_to_all(sent, 'gx', 0, 0, tiled=True)]
    ppermute x4 -> x6, starting transfers between devices: 19.2 us -> 27.5 us  [swap(): lax.ppermute(value, axis, [(i, i + 1) for i in firsts] + [(i + 1, i) for...]
    all_to_all x0 -> x1, waiting for transfers between devices: none -> 7.93 us  [local(): got = lax.all_to_all(sent, 'gx', 0, 0, tiled=True)]
    ppermute x4 -> x6, waiting for transfers between devices: 3.58 us -> 5.13 us  [swap(): lax.ppermute(value, axis, [(i, i + 1) for i in firsts] + [(i + 1, i) for...]
    pallas_call x4 -> x6, Pallas kernels: 6.35 us -> 7.37 us  [call(): pl.pallas_call(kernel, out_shape=outs, in_specs=[pl.BlockSpec(memory_spac...]
  transfers between devices with their start and end apart: 4 -> 7, of which waited for: 3 -> 4; matrix products, arithmetic and copies ran while one was open for 0% -> 0% of each run, Pallas kernels for 1% -> 1%
where the time goes in v4:
time: 63.2 us; the launch traced here: 62.8 us
  starting transfers between devices  41.6 us (66%)
  waiting for transfers between devices  13.1 us (21%)
  Pallas kernels  7.37 us (12%)
  between operations  0.77 us (1%)
    ppermute x6, starting transfers between devices, swap(): lax.ppermute(value, axis, [(i, i + 1) for i in firsts] + [(i + 1, i) for...  27.5 us
    all_to_all x1, starting transfers between devices, local(): got = lax.all_to_all(sent, 'gx', 0, 0, tiled=True)  14 us
    all_to_all x1, waiting for transfers between devices, local(): got = lax.all_to_all(sent, 'gx', 0, 0, tiled=True)  7.93 us
    pallas_call x6, Pallas kernels, call(): pl.pallas_call(kernel, out_shape=outs, in_specs=[pl.BlockSpec(memory_spac...  7.37 us
    ppermute x6, waiting for transfers between devices, swap(): lax.ppermute(value, axis, [(i, i + 1) for i in firsts] + [(i + 1, i) for...  5.13 us
  transfers between devices with their start and end apart: 7, of which 4 were waited for; matrix products, arithmetic and copies ran while one was open for 0% of the time, Pallas kernels for 1%

profile of v4, /device:TPU:89, one launch (start us, length us, event | category | flops | bytes accessed | tf_op | source)
XLA Modules:
  0.0 62.8 jit_solution(9804320766140347439)
XLA Ops:
  0.6 0.0 copy-start
  0.6 0.0 copy-start.1
  0.7 2.6 %shard_map.68 = (f32[5,24,256]{2,1,0:T(8,128)S(1)}, f32[2,24,128]{2,1,0:T(8,128)S(1)}, f32[2,24,128]{2,1,0:T(8,128)S(1)}) custom-call(f32[5,48,512]{2,1,0:T(8,128)} %fine_in.1, s32[48,512]{1,0:T(8,128)} %owner_in.1, s32[24,256]{1,0:T(8,128)} %flags.3, f32[5,5,24,256]{3,2,1,0:T(8,128)} %jac.1, f32[5,6,64]{2,1,0:T(8,128)} %coef.1), custom_call_target="tpu_custom_call" | custom-call | tf_op jit(solution)/shard_map/pallas_call | solution.py:457
  3.3 4.4 %collective-permute-start = (f32[2,24,128]{2,1,0:T(8,128)S(1)}, f32[2,24,128]{2,1,0:T(8,128)S(1)}, u32[]{:S(2)}, u32[]{:S(2)}) collective-permute-start(f32[2,24,128]{2,1,0:T(8,128)S(1)} %get-tuple-element.24), channel_id=1, source_target_pairs={{1,2},{3,4},{5,6},{7,8},{9,10},{11,12},{13,14},{15,16},{17,18},{19... | collective-permute-start | bytes 73736 | tf_op jit(solution)/shard_map/ppermute | solution.py:470
  7.7 1.9 %collective-permute-start.1 = (f32[2,24,128]{2,1,0:T(8,128)S(1)}, f32[2,24,128]{2,1,0:T(8,128)S(1)}, u32[]{:S(2)}, u32[]{:S(2)}) collective-permute-start(f32[2,24,128]{2,1,0:T(8,128)S(1)} %get-tuple-element.25), channel_id=1, source_target_pairs={{0,1},{2,3},{4,5},{6,7},{8,9},{10,11},{12,13},{14,15},{16,17},{18,... | collective-permute-start | bytes 73736 | tf_op jit(solution)/shard_map/ppermute | solution.py:470
  9.6 0.0 copy-done
  9.6 0.0 copy-done.1
  9.6 0.1 shard_map.70
  9.7 0.0 collective-permute-done.far_y
  9.7 2.5 %collective-permute-done.1.near_y = f32[2,24,128]{2,1,0:T(8,128)S(1)} collective-permute-done((f32[2,24,128]{2,1,0:T(8,128)S(1)}, f32[2,24,128]{2,1,0:T(8,128)S(1)}, u32[]{:S(2)}, u32[]{:S(2)}) %collective-permute-start.1) | collective-permute-done | bytes 24608 | tf_op jit(solution)/shard_map/ppermute | solution.py:470
  12.3 0.0 copy-start.2
  12.3 10.8 %collective-permute-start.2 = (f32[80,256]{1,0:T(8,128)S(1)}, f32[80,256]{1,0:T(8,128)S(1)}, u32[]{:S(2)}, u32[]{:S(2)}) collective-permute-start(f32[80,256]{1,0:T(8,128)S(1)} %get-tuple-element.34), channel_id=1, source_target_pairs={{24,48},{72,96},{120,144},{168,192},{216,240},{264,288},{312,336},... | collective-permute-start | bytes 245768 | tf_op jit(solution)/shard_map/ppermute | solution.py:470
  23.1 1.9 %collective-permute-start.3 = (f32[80,256]{1,0:T(8,128)S(1)}, f32[80,256]{1,0:T(8,128)S(1)}, u32[]{:S(2)}, u32[]{:S(2)}) collective-permute-start(f32[80,256]{1,0:T(8,128)S(1)} %get-tuple-element.35), channel_id=1, source_target_pairs={{0,24},{48,72},{96,120},{144,168},{192,216},{240,264},{288,312},{3... | collective-permute-start | bytes 245768 | tf_op jit(solution)/shard_map/ppermute | solution.py:470
  25.0 0.0 copy-done.2
  25.1 0.3 shard_map.69
  25.4 0.0 collective-permute-done.2.far_x
  25.4 0.9 %collective-permute-done.3.near_x = f32[80,256]{1,0:T(8,128)S(1)} collective-permute-done((f32[80,256]{1,0:T(8,128)S(1)}, f32[80,256]{1,0:T(8,128)S(1)}, u32[]{:S(2)}, u32[]{:S(2)}) %collective-permute-start.3) | collective-permute-done | bytes 81952 | tf_op jit(solution)/shard_map/ppermute | solution.py:470
  26.3 2.3 %shard_map.72 = (f32[5,40,384]{2,1,0:T(8,128)S(1)}, f32[25,16,384]{2,1,0:T(8,128)S(1)}, f32[5,16,384]{2,1,0:T(8,128)S(1)}, f32[5,16,384]{2,1,0:T(8,128)S(1)}, f3...) custom-call(f32[25,24,384]{2,1,0:T(8,128)S(1)} %get-tuple-element.26.jac_own, ...), custom_call_target="tpu_custom_call" | custom-call | tf_op jit(solution)/shard_map/pallas_call | solution.py:457
  28.6 14.0 %all-to-all-start = ((f32[32,16,128]{2,1,0:T(8,128)}), f32[32,16,128]{2,1,0:T(8,128)S(1)}, u32[]{:S(2)}, u32[]{:S(2)}) async-start(f32[32,16,128]{2,1,0:T(8,128)} %get-tuple-element.43), calls=%async_computation | async-start | bytes 524288 | tf_op jit(solution)/shard_map/all_to_all | solution.py:522
  42.6 6.5 %collective-permute-start.4 = (f32[16,384]{1,0:T(8,128)S(1)}, f32[16,384]{1,0:T(8,128)S(1)}, u32[]{:S(2)}, u32[]{:S(2)}) collective-permute-start(f32[16,384]{1,0:T(8,128)S(1)} %get-tuple-element.41), channel_id=1, source_target_pairs={{24,48},{72,96},{120,144},{168,192},{216,240},{264,288},{312,336},... | collective-permute-start | bytes 73736 | tf_op jit(solution)/shard_map/ppermute | solution.py:470
  49.2 1.9 %collective-permute-start.5 = (f32[16,384]{1,0:T(8,128)S(1)}, f32[16,384]{1,0:T(8,128)S(1)}, u32[]{:S(2)}, u32[]{:S(2)}) collective-permute-start(f32[16,384]{1,0:T(8,128)S(1)} %get-tuple-element.42), channel_id=1, source_target_pairs={{0,24},{48,72},{96,120},{144,168},{192,216},{240,264},{288,312},{3... | collective-permute-start | bytes 73736 | tf_op jit(solution)/shard_map/ppermute | solution.py:470
  51.1 1.7 %collective-permute-done.4.far_state = f32[16,384]{1,0:T(8,128)S(1)} collective-permute-done((f32[16,384]{1,0:T(8,128)S(1)}, f32[16,384]{1,0:T(8,128)S(1)}, u32[]{:S(2)}, u32[]{:S(2)}) %collective-permute-start.4) | collective-permute-done | bytes 24608 | tf_op jit(solution)/shard_map/ppermute | solution.py:470
  52.9 0.0 collective-permute-done.5.near_state
  52.9 7.9 %all-to-all-done.got = f32[32,16,128]{2,1,0:T(8,128)S(1)} async-done(((f32[32,16,128]{2,1,0:T(8,128)}), f32[32,16,128]{2,1,0:T(8,128)S(1)}, u32[]{:S(2)}, u32[]{:S(2)}) %all-to-all-start) | async-done | bytes 262176 | tf_op jit(solution)/shard_map/all_to_all | solution.py:522
  60.8 2.0 %shard_map.73 = (f32[5,24,256]{2,1,0:T(8,128)}, f32[5,24,256]{2,1,0:T(8,128)}) custom-call(f32[25,24,384]{2,1,0:T(8,128)S(1)} %get-tuple-element.26.jac_own, f32[5,24,384]{2,1,0:T(8,128)S(1)} %get-tuple-element.27.rhs_own, f32[5,24,384]{2,1,0:T(8,128)S(1)} %get-tuple-element.28.scaled_own, f32[48,128]{1,0:T(8,128)S(1)} %get-tuple-element.29.low, ...), custom_call_target="tpu_custom_call" | custom-call | tf_op jit(solution)/shard_map/pallas_call | solution.py:457
  (1 shorter events, 0.0 us)
Async XLA Ops:
  0.6 9.0 %copy-start = (f32[5,5,24,256]{3,2,1,0:T(8,128)S(1)}, f32[5,5,24,256]{3,2,1,0:T(8,128)}, u32[]{:S(2)}) copy-start(f32[5,5,24,256]{3,2,1,0:T(8,128)} %jac.1) | copy-start | bytes 1843204
  0.6 9.0 %copy-start.1 = (s32[24,256]{1,0:T(8,128)S(1)}, s32[24,256]{1,0:T(8,128)}, u32[]{:S(2)}) copy-start(s32[24,256]{1,0:T(8,128)} %flags.3) | copy-start | bytes 73732
  3.3 6.5 %collective-permute-start = (f32[2,24,128]{2,1,0:T(8,128)S(1)}, f32[2,24,128]{2,1,0:T(8,128)S(1)}, u32[]{:S(2)}, u32[]{:S(2)}) collective-permute-start(f32[2,24,128]{2,1,0:T(8,128)S(1)} %get-tuple-element.24), channel_id=1, source_target_pairs={{1,2},{3,4},{5,6},{7,8},{9,10},{11,12},{13,14},{15,16},{17,18},{19... | collective-permute-start | bytes 73736 | tf_op jit(solution)/shard_map/ppermute | solution.py:470
  7.7 4.6 %collective-permute-start.1 = (f32[2,24,128]{2,1,0:T(8,128)S(1)}, f32[2,24,128]{2,1,0:T(8,128)S(1)}, u32[]{:S(2)}, u32[]{:S(2)}) collective-permute-start(f32[2,24,128]{2,1,0:T(8,128)S(1)} %get-tuple-element.25), channel_id=1, source_target_pairs={{0,1},{2,3},{4,5},{6,7},{8,9},{10,11},{12,13},{14,15},{16,17},{18,... | collective-permute-start | bytes 73736 | tf_op jit(solution)/shard_map/ppermute | solution.py:470
  12.3 12.8 %copy-start.2 = (f32[5,6,64]{2,1,0:T(8,128)S(1)}, f32[5,6,64]{2,1,0:T(8,128)}, u32[]{:S(2)}) copy-start(f32[5,6,64]{2,1,0:T(8,128)} %coef.1) | copy-start | bytes 23044
  12.3 13.1 %collective-permute-start.2 = (f32[80,256]{1,0:T(8,128)S(1)}, f32[80,256]{1,0:T(8,128)S(1)}, u32[]{:S(2)}, u32[]{:S(2)}) collective-permute-start(f32[80,256]{1,0:T(8,128)S(1)} %get-tuple-element.34), channel_id=1, source_target_pairs={{24,48},{72,96},{120,144},{168,192},{216,240},{264,288},{312,336},... | collective-permute-start | bytes 245768 | tf_op jit(solution)/shard_map/ppermute | solution.py:470
  23.1 3.2 %collective-permute-start.3 = (f32[80,256]{1,0:T(8,128)S(1)}, f32[80,256]{1,0:T(8,128)S(1)}, u32[]{:S(2)}, u32[]{:S(2)}) collective-permute-start(f32[80,256]{1,0:T(8,128)S(1)} %get-tuple-element.35), channel_id=1, source_target_pairs={{0,24},{48,72},{96,120},{144,168},{192,216},{240,264},{288,312},{3... | collective-permute-start | bytes 245768 | tf_op jit(solution)/shard_map/ppermute | solution.py:470
  28.6 32.2 %all-to-all-start = ((f32[32,16,128]{2,1,0:T(8,128)}), f32[32,16,128]{2,1,0:T(8,128)S(1)}, u32[]{:S(2)}, u32[]{:S(2)}) async-start(f32[32,16,128]{2,1,0:T(8,128)} %get-tuple-element.43), calls=%async_computation | async-start | bytes 524288 | tf_op jit(solution)/shard_map/all_to_all | solution.py:522
  42.6 10.2 %collective-permute-start.4 = (f32[16,384]{1,0:T(8,128)S(1)}, f32[16,384]{1,0:T(8,128)S(1)}, u32[]{:S(2)}, u32[]{:S(2)}) collective-permute-start(f32[16,384]{1,0:T(8,128)S(1)} %get-tuple-element.41), channel_id=1, source_target_pairs={{24,48},{72,96},{120,144},{168,192},{216,240},{264,288},{312,336},... | collective-permute-start | bytes 73736 | tf_op jit(solution)/shard_map/ppermute | solution.py:470
  49.2 3.7 %collective-permute-start.5 = (f32[16,384]{1,0:T(8,128)S(1)}, f32[16,384]{1,0:T(8,128)S(1)}, u32[]{:S(2)}, u32[]{:S(2)}) collective-permute-start(f32[16,384]{1,0:T(8,128)S(1)} %get-tuple-element.42), channel_id=1, source_target_pairs={{0,24},{48,72},{96,120},{144,168},{192,216},{240,264},{288,312},{3... | collective-permute-start | bytes 73736 | tf_op jit(solution)/shard_map/ppermute | solution.py:470

commit v5 on v4

--- a/solution.py
+++ b/solution.py
@@ -61,7 +61,7 @@
     ]
     for copy in owners + sum(fines, []) + late:
         copy.start()
-    for copy in owners + sum(fines, []) + late:
+    for copy in owners:
         copy.wait()
 
     def halves(load):
@@ -80,6 +80,8 @@
     masks = [[code == k for code in codes] for k in range(9)]
     gathered = []
     for f in range(F):
+        for copy in fines[f]:
+            copy.wait()
         values = halves(lambda j, rows: fine[f, j, rows, :])
         total = None
         for dy in (-1, 0, 1):
@@ -95,6 +97,8 @@
     pairs = ((iota((2 * TY, TY), 0) >> 1) == iota((2 * TY, TY), 1)).astype(F32)
     gathered.append(jnp.zeros((8, 2 * TY), F32))
     summed = select_columns(jnp.concatenate(gathered, axis=0), pairs)
+    for copy in late:
+        copy.wait()
     planes = [summed[TX * f : TX * (f + 1)] for f in range(F)]
     for f in range(F):
         rhs[f] = planes[f]
@@ -158,10 +162,11 @@
         write(far, True)
 
 
-def corners_kernel(near_rows, far_rows, far_y, near_y, near, far):
+def corners_kernel(near_rows, far_rows, coef, far_y, near_y, near, far, low, high, turn, diag):
     odd = parity("gx")
-    near[...] = near_rows[...]
-    far[...] = far_rows[...]
+    near[0:ROWS_SENT] = near_rows[...]
+    far[0:ROWS_SENT] = far_rows[...]
+    far[ROWS_SENT : ROWS_SENT + 8] = jnp.zeros((8, TY), F32)
     for side, strip in enumerate((far_y, near_y)):
         at = CORNER_AT + 3 * side
         for a in range(2):
@@ -170,45 +175,10 @@
             near[at : at + 3, lanes] = jnp.where(odd, first, last)
             far[at : at + 3, lanes] = jnp.where(odd, last, first)
 
-
-def unpack(near, far, p):
-    odd = parity("gy")
-    right = jnp.where(odd, far, near)
-    left = jnp.where(odd, near, far)
-    lane = iota(near.shape, 1)
-    return jnp.where(
-        lane < 8,
-        roll(right, -8 * (p % 16), 1),
-        jnp.where(lane >= 120, roll(left, 120 - 8 * (p % 16), 1), 0.0),
-    )
-
-
-def scale(code, jac, scaled):
-    plain = (code == 1.0) | (code == 3.0)
-    interior = code == 1.0
-    for f in range(F):
-        kept = interior if f in (1, 2) else plain
-        scaled[f] = jnp.where(kept, 0.8 / jac[F * f + f], 0.0)
-
-
-def own_kernel(
-    jac_in, rhs_in, flags, far_y, near_y, coef, jac, rhs, scaled, low, high, block, diag
-):
-    near, far = [near_y[0], near_y[1]], [far_y[0], far_y[1]]
-    for p in range(F * F):
-        jac[p, :, 0:TY] = jac_in[p // F, p % F]
-        jac[p, :, TY:EY] = unpack(near[p // 16], far[p // 16], p)
-    for f in range(F):
-        rhs[f, :, 0:TY] = rhs_in[f]
-        rhs[f, :, TY:EY] = unpack(near[1], far[1], F * F + f)
-    aside = unpack(near[1], far[1], F * F + F)
-    code = jnp.concatenate([(flags[...] + 1).astype(F32), aside], axis=1)
-    scale(code, jac, scaled)
-
     lane = iota((ROWS, 128), 1)
-    odd = parity("gy")
-    right = jnp.where(odd, far[1], near[1])[0:ROWS]
-    left = jnp.where(odd, near[1], far[1])[0:ROWS]
+    odd_y = parity("gy")
+    right = jnp.where(odd_y, far_y[1, 0:ROWS, :], near_y[1, 0:ROWS, :])
+    left = jnp.where(odd_y, near_y[1, 0:ROWS, :], far_y[1, 0:ROWS, :])
     diag[...] = jnp.full((8 * ROWS, 128), 4.0, F32)
     for f in range(F):
         wide = jnp.concatenate([coef[f], coef[f]], axis=1)
@@ -228,13 +198,48 @@
     first_low = lows[-1]
     for k in range(ROWS - 2, -1, -1):
         first_low = lows[k] + highs[k] * first_low
+    turn[...] = first_low
     lane = iota((8, 128), 1)
-    last = highs[-1]
-    for q, part in ((2, first_low), (3, lows[-1]), (4, highs[-1])):
-        last = jnp.where(lane >> 1 == 32 + q, roll(part, 2 * q, 1), last)
-    block[...] = jnp.zeros((16, 128), F32)
-    block[F : 2 * F] = jnp.where(lane < 64, first_low, roll(lows[-1], 64, 1))[0:F]
-    block[2 * F : 3 * F] = last[0:F]
+    ends = highs[-1]
+    for q, part in enumerate((first_low, lows[-1], highs[-1])):
+        ends = jnp.where(lane >> 1 == 33 + q, roll(part, 2 * (q + 1), 1), ends)
+    near[ROWS_SENT : ROWS_SENT + 8, 0:128] = jnp.where(lane < 64, first_low, roll(lows[-1], 64, 1))
+    near[ROWS_SENT : ROWS_SENT + 8, 128:TY] = ends
+
+
+def unpack(near, far, p):
+    odd = parity("gy")
+    right = jnp.where(odd, far, near)
+    left = jnp.where(odd, near, far)
+    lane = iota(near.shape, 1)
+    return jnp.where(
+        lane < 8,
+        roll(right, -8 * (p % 16), 1),
+        jnp.where(lane >= 120, roll(left, 120 - 8 * (p % 16), 1), 0.0),
+    )
+
+
+def scale(code, jac, scaled):
+    plain = (code == 1.0) | (code == 3.0)
+    interior = code == 1.0
+    for f in range(F):
+        kept = interior if f in (1, 2) else plain
+        scaled[f] = jnp.where(kept, 0.8 / jac[F * f + f], 0.0)
+
+
+def own_kernel(
+    jac_in, rhs_in, flags, far_y, near_y, jac, rhs, scaled
+):
+    near, far = [near_y[0], near_y[1]], [far_y[0], far_y[1]]
+    for p in range(F * F):
+        jac[p, :, 0:TY] = jac_in[p // F, p % F]
+        jac[p, :, TY:EY] = unpack(near[p // 16], far[p // 16], p)
+    for f in range(F):
+        rhs[f, :, 0:TY] = rhs_in[f]
+        rhs[f, :, TY:EY] = unpack(near[1], far[1], F * F + f)
+    aside = unpack(near[1], far[1], F * F + F)
+    code = jnp.concatenate([(flags[...] + 1).astype(F32), aside], axis=1)
+    scale(code, jac, scaled)
 
 
 def residual(f, state, rhs, jac):
@@ -263,12 +268,13 @@
 
 
 def before_kernel(
-    jac_own, rhs_own, scaled_own, high, block, far_x, near_x,
-    state, jac, rhs, scaled, value, sent, near_state, far_state, other, sides, beside, means, whole_block,
+    jac_own, rhs_own, scaled_own, low, high, turn, far_x, near_x,
+    state, jac, rhs, scaled, value, chip, near_state, far_state, sent, other, sides, beside, means, block, sems,
 ):
     odd = parity("gx")
-    sides[0] = jnp.where(odd, near_x[...], far_x[...])
-    sides[1] = jnp.where(odd, far_x[...], near_x[...])
+    near_rows, far_rows = near_x[0:ROWS_SENT, :], far_x[0:ROWS_SENT, :]
+    sides[0] = jnp.where(odd, near_rows, far_rows)
+    sides[1] = jnp.where(odd, far_rows, near_rows)
     none = jnp.zeros((16, TY), F32)
 
     def put(out, at, rows):
@@ -307,12 +313,6 @@
         state[f] = scaled_plane(f) * rhs_plane(f)
     sweep(state, other, scaled_plane, rhs_plane, jac_plane)
     sweep(other, state, scaled_plane, rhs_plane, jac_plane)
-    near_state[15:16] = jnp.zeros((1, EY), F32)
-    far_state[15:16] = jnp.zeros((1, EY), F32)
-    for f in range(F):
-        first, last = state[f, 8:11], state[f, 5 + TX : 8 + TX]
-        near_state[3 * f : 3 * f + 3] = jnp.where(odd, first, last)
-        far_state[3 * f : 3 * f + 3] = jnp.where(odd, last, first)
     means[...] = jnp.zeros((8 * ROWS, EY), F32)
     for f in range(F):
         left_over = residual(f, state, rhs_plane, jac_plane)[8 : 8 + TX]
@@ -331,15 +331,47 @@
     for k in range(ROWS - 2, -1, -1):
         first = values[k] + high[8 * k : 8 * k + 8, :] * first
     lane = iota((8, 128), 1)
-    ends = jnp.where(lane >> 1 == 32, first, roll(last, 2, 1))[0:F]
-    whole_block[...] = block[...]
-    whole_block[0:F] = jnp.where(lane < 64, first, roll(last, 64, 1))[0:F]
-    kept = whole_block[2 * F : 3 * F]
-    pair = lane[0:F] >> 1
-    whole_block[2 * F : 3 * F] = jnp.where((pair == 32) | (pair == 33), ends, kept)
-    whole = whole_block[...]
-    for k in range(sent.shape[0]):
-        sent[k] = whole
+
+    packed = [near_x[ROWS_SENT : ROWS_SENT + 8, 128 * a : 128 * (a + 1)] for a in range(2)]
+    theirs = [packed[0], roll(packed[0], 64, 1), packed[1]]
+    theirs = [jnp.where(lane < 64, theirs[q], roll(packed[1], -2 * (q + 1), 1)) for q in range(3)]
+    own = [turn[...], low[8 * ROWS - 8 :, :], high[8 * ROWS - 8 :, :]]
+    b0, c, c1 = [jnp.where(odd, theirs[q], own[q]) for q in range(3)]
+    e0, g, g1 = [jnp.where(odd, own[q], theirs[q]) for q in range(3)]
+    w = 1.0 / (1.0 - c1 * e0)
+    cw, gw = c * w, g * w
+    x0 = jnp.where(odd, cw * first, first + cw * e0 * last)
+    x1 = jnp.where(odd, last + gw * c1 * first, gw * last)
+    chip[0] = w
+    chip[1] = jnp.where(odd, gw, cw)
+    chip[2] = jnp.where(odd, first, last)
+    chip[3] = jnp.where(odd, c1, e0)
+    chip[4] = c
+    chip[5] = g
+    whole_b0, whole_c, whole_c1 = b0 + c * cw * e0, cw * g, g1 + g * gw * c1
+    middle = roll(whole_c, 64, 1)
+    pair = lane >> 1
+    even_part = jnp.where(lane < 64, whole_b0, middle)
+    for q, part in enumerate((x0, x1, whole_b0, whole_c, whole_c1)):
+        even_part = jnp.where(pair == 48 + q, roll(part, 32 + 2 * q, 1), even_part)
+    odd_part = jnp.where(lane < 64, whole_c1, middle)
+    odd_part = jnp.where(pair == 32, x0, jnp.where(pair == 33, roll(x1, 2, 1), odd_part))
+    main = jnp.where(lane < 64, x0, roll(x1, 64, 1))
+    rest = jnp.where(odd, odd_part, even_part)
+    for f in range(F):
+        block[f, 0:1] = main[f : f + 1]
+        block[f, 1:2] = rest[f : f + 1]
+    copies = [pltpu.make_async_copy(block, sent.at[k], sems.at[k]) for k in range(sent.shape[0])]
+    for copy in copies:
+        copy.start()
+    near_state[15:16] = jnp.zeros((1, EY), F32)
+    far_state[15:16] = jnp.zeros((1, EY), F32)
+    for f in range(F):
+        first, last = state[f, 8:11], state[f, 5 + TX : 8 + TX]
+        near_state[3 * f : 3 * f + 3] = jnp.where(odd, first, last)
+        far_state[3 * f : 3 * f + 3] = jnp.where(odd, last, first)
+    for copy in copies:
+        copy.wait()
 
 
 def merge(one, two):
@@ -365,7 +397,7 @@
 
 
 def after_kernel(
-    jac_own, rhs_own, scaled_own, low, high, jac_beyond, rhs_beyond, scaled_beyond, state_in, value, far_state, near_state, got,
+    jac_own, rhs_own, scaled_own, low, high, jac_beyond, rhs_beyond, scaled_beyond, state_in, value, chip, far_state, near_state, got,
     correction_out, level_residual_out,
     state, other, ends, spread, tree, correction, level_residual, sems,
 ):
@@ -373,31 +405,51 @@
     me = lax.axis_index("gx")
     lane = iota((F, 128), 1)
 
+    odd = parity("gx")
+
+    def stacked(k, part):
+        return jnp.concatenate([got[k, f, part : part + 1, :] for f in range(F)], axis=0)
+
     def segment(k):
-        one, two, three = got[k, 0:F, :], got[k, F : 2 * F, :], got[k, 2 * F : 3 * F, :]
-        main = [one, roll(one, 64, 1), two, roll(two, 64, 1), three]
-        return [jnp.where(lane < 64, main[q], roll(three, -2 * q, 1)) for q in range(5)]
-
-    level, starts, total = [segment(k) for k in range(count)], [], 0
-    while len(level) > 2:
-        level = [merge(level[2 * k], level[2 * k + 1]) for k in range(len(level) // 2)]
+        main = stacked(2 * k, 0) + stacked(2 * k + 1, 0)
+        even, other_core = stacked(2 * k, 1), stacked(2 * k + 1, 1)
+        ends = roll(even, 64 - 96, 1)
+        moving = ends + other_core
+        middle = roll(jnp.where(lane < 96, even, other_core), 64, 1)
+        inner = [main, roll(main, 64, 1), even, middle, other_core]
+        outer = [moving, roll(moving, -2, 1)] + [roll(ends, -2 * q, 1) for q in (2, 3, 4)]
+        return [jnp.where(lane < 64, inner[q], outer[q]) for q in range(5)]
+
+    level, starts, total = [segment(k) for k in range(count // 2)], [], 0
+    while True:
         starts.append(total)
         for parts in level:
             for q in range(5):
                 tree[total, q, 0:F] = parts[q]
             total += 1
+        if len(level) <= 2:
+            break
+        level = [merge(level[2 * k], level[2 * k + 1]) for k in range(len(level) // 2)]
     below = above = jnp.zeros((F, 128), F32)
-    for size in range(len(starts), -1, -1):
-        pair = me >> (size + 1)
-        if size:
-            at = starts[size - 1] + 2 * pair
+    my_chip = me >> 1
+    if count > 2:
+        for size in range(len(starts) - 1, -1, -1):
+            at = starts[size] + 2 * (my_chip >> (size + 1))
             one = [tree[at, q, 0:F] for q in range(5)]
             two = [tree[at + 1, q, 0:F] for q in range(5)]
-        else:
-            one, two = segment(2 * pair), segment(2 * pair + 1)
-        last, first = between(one, two, below, above)
-        second = (me >> size) & 1 == 1
-        below, above = jnp.where(second, last, below), jnp.where(second, above, first)
+            last, first = between(one, two, below, above)
+            second = (my_chip >> size) & 1 == 1
+            below, above = jnp.where(second, last, below), jnp.where(second, above, first)
+    partner = me + 1 - 2 * (me & 1)
+    main, rest = stacked(partner, 0), stacked(partner, 1)
+    from_even = jnp.where(lane < 64, roll(main, 64, 1), roll(rest, 64 - 98, 1))
+    from_odd = jnp.where(lane < 64, main, rest)
+    w, share, own, turn, c, g = [chip[q, 0:F, :] for q in range(6)]
+    theirs = jnp.where(odd, from_even, from_odd) / share
+    lower, upper = c * below, g * above
+    inside = jnp.where(odd, lower, upper) + theirs
+    inside = w * (inside + turn * (own + jnp.where(odd, upper, lower)))
+    below, above = jnp.where(odd, inside, below), jnp.where(odd, above, inside)
 
     used = lane <= 65
     ends[...] = jnp.zeros((64, 128), F32)
@@ -413,7 +465,6 @@
     jac_plane, rhs_plane = planes_of(jac_own, jac_beyond), planes_of(rhs_own, rhs_beyond)
     scaled_plane = planes_of(scaled_own, scaled_beyond)
     upper = iota((8, EY), 0) < 4
-    odd = parity("gx")
 
     def repeated(row):
         return jnp.broadcast_to(spread[row : row + 1, :], (8, EY))
@@ -453,12 +504,12 @@
     return jax.ShapeDtypeStruct(dims, F32)
 
 
-def call(kernel, outs, scratch, *args, space=pltpu.VMEM, out_space=pltpu.VMEM):
+def call(kernel, outs, scratch, *args, space=pltpu.VMEM, out_space=None):
     return pl.pallas_call(
         kernel,
         out_shape=outs,
         in_specs=[pl.BlockSpec(memory_space=space)] * len(args),
-        out_specs=[pl.BlockSpec(memory_space=out_space)] * len(outs),
+        out_specs=[pl.BlockSpec(memory_space=o) for o in out_space or [pltpu.VMEM] * len(outs)],
         scratch_shapes=scratch,
         compiler_params=pltpu.CompilerParams(vmem_limit_bytes=32 * 1024 * 1024),
     )(*args)
@@ -491,33 +542,39 @@
     )
     far_y = swap(far, "gy", 1)
     near_y = swap(near, "gy", 0)
-    rows = shape_of(ROWS_SENT, TY)
-    near_rows, far_rows = call(corners_kernel, [rows, rows], [], near_rows, far_rows, far_y, near_y)
+    rows, lines, line = shape_of(ROWS_SENT, TY), shape_of(8 * ROWS, 128), shape_of(8, 128)
+    near_rows, far_rows, low, high, turn = call(
+        corners_kernel,
+        [shape_of(ROWS_SENT + 8, TY), shape_of(ROWS_SENT + 8, TY), lines, lines, line],
+        [pltpu.VMEM((8 * ROWS, 128), F32)],
+        near_rows, far_rows, coef, far_y, near_y,
+    )
     far_x = swap(far_rows, "gx", 1)
     near_x = swap(near_rows, "gx", 0)
     count = lax.axis_size("gx")
-    lines = shape_of(8 * ROWS, 128)
     own = shape_of(F, TX, EY)
-    jac_own, rhs_own, scaled_own, low, high, block = call(
-        own_kernel,
-        [shape_of(F * F, TX, EY), own, own, lines, lines, shape_of(16, 128)],
-        [pltpu.VMEM((8 * ROWS, 128), F32)],
-        jac, rhs, flags, far_y, near_y, coef,
+    jac_own, rhs_own, scaled_own = call(
+        own_kernel, [shape_of(F * F, TX, EY), own, own], [], jac, rhs, flags, far_y, near_y
     )
     tile = pltpu.VMEM((F, EX, EY), F32)
     beyond = shape_of(F, 16, EY)
     ends = shape_of(16, EY)
-    state, jac_beyond, rhs_beyond, scaled_beyond, value, sent, near_state, far_state = call(
+    state, jac_beyond, rhs_beyond, scaled_beyond, value, chip, near_state, far_state, sent = call(
         before_kernel,
-        [shape_of(F, EX, EY), shape_of(F * F, 16, EY), beyond, beyond, lines, shape_of(count, 16, 128), ends, ends],
+        [
+            shape_of(F, EX, EY), shape_of(F * F, 16, EY), beyond, beyond, lines, shape_of(6, 8, 128), ends, ends,
+            shape_of(count, F, 2, 128),
+        ],
         [
             tile,
             pltpu.VMEM((2, ROWS_SENT, TY), F32),
             pltpu.VMEM((2, 2, 16, 128), F32),
             pltpu.VMEM((8 * ROWS, EY), F32),
-            pltpu.VMEM((16, 128), F32),
+            pltpu.VMEM((F, 2, 128), F32),
+            pltpu.SemaphoreType.DMA((count,)),
         ],
-        jac_own, rhs_own, scaled_own, high, block, far_x, near_x,
+        jac_own, rhs_own, scaled_own, low, high, turn, far_x, near_x,
+        out_space=[pltpu.VMEM] * 8 + [pl.ANY],
     )
     got = lax.all_to_all(sent, "gx", 0, 0, tiled=True)
     far_state = swap(far_state, "gx", 1)
@@ -536,8 +593,9 @@
                 pltpu.VMEM((F, TX, TY), F32),
                 pltpu.SemaphoreType.DMA((2, F)),
             ],
-            jac_own, rhs_own, scaled_own, low, high, jac_beyond, rhs_beyond, scaled_beyond, state, value, far_state, near_state, got,
-            out_space=pl.ANY,
+            jac_own, rhs_own, scaled_own, low, high, jac_beyond, rhs_beyond, scaled_beyond, state, value, chip,
+            far_state, near_state, got,
+            out_space=[pl.ANY] * 2,
         )
     )
 

time: 63.2 us -> 59.9 us (0.948)
  waiting for transfers between devices: 13.1 us -> 9.31 us
    all_to_all x1, waiting for transfers between devices: 7.93 us -> 4.63 us  [local(): got = lax.all_to_all(sent, 'gx', 0, 0, tiled=True)]
where the time goes in v5:
time: 59.9 us; the launch traced here: 59.5 us
  starting transfers between devices  41.9 us (70%)
  waiting for transfers between devices  9.31 us (16%)
  Pallas kernels  7.53 us (13%)
  between operations  0.78 us (1%)
    ppermute x6, starting transfers between devices, swap(): lax.ppermute(value, axis, [(i, i + 1) for i in firsts] + [(i + 1, i) for...  27.6 us
    all_to_all x1, starting transfers between devices, local(): got = lax.all_to_all(sent, 'gx', 0, 0, tiled=True)  14.4 us
    pallas_call x6, Pallas kernels, call(): pl.pallas_call(kernel, out_shape=outs, in_specs=[pl.BlockSpec(memory_spac...  7.53 us
    ppermute x6, waiting for transfers between devices, swap(): lax.ppermute(value, axis, [(i, i + 1) for i in firsts] + [(i + 1, i) for...  4.68 us
    all_to_all x1, waiting for transfers between devices, local(): got = lax.all_to_all(sent, 'gx', 0, 0, tiled=True)  4.63 us
  transfers between devices with their start and end apart: 7, of which 4 were waited for; matrix products, arithmetic and copies ran while one was open for 0% of the time, Pallas kernels for 1%

profile of v5, /device:TPU:89, one launch (start us, length us, event | category | flops | bytes accessed | tf_op | source)
XLA Modules:
  0.0 59.5 jit_solution(836609374245522033)
XLA Ops:
  0.6 0.0 copy-start
  0.6 0.0 copy-start.1
  0.7 2.4 %shard_map.68 = (f32[5,24,256]{2,1,0:T(8,128)S(1)}, f32[2,24,128]{2,1,0:T(8,128)S(1)}, f32[2,24,128]{2,1,0:T(8,128)S(1)}) custom-call(f32[5,48,512]{2,1,0:T(8,128)} %fine_in.1, s32[48,512]{1,0:T(8,128)} %owner_in.1, s32[24,256]{1,0:T(8,128)} %flags.3, f32[5,5,24,256]{3,2,1,0:T(8,128)} %jac.1, f32[5,6,64]{2,1,0:T(8,128)} %coef.1), custom_call_target="tpu_custom_call" | custom-call | tf_op jit(solution)/shard_map/pallas_call | solution.py:508
  3.1 4.4 %collective-permute-start = (f32[2,24,128]{2,1,0:T(8,128)S(1)}, f32[2,24,128]{2,1,0:T(8,128)S(1)}, u32[]{:S(2)}, u32[]{:S(2)}) collective-permute-start(f32[2,24,128]{2,1,0:T(8,128)S(1)} %get-tuple-element.25), channel_id=1, source_target_pairs={{1,2},{3,4},{5,6},{7,8},{9,10},{11,12},{13,14},{15,16},{17,18},{19... | collective-permute-start | bytes 73736 | tf_op jit(solution)/shard_map/ppermute | solution.py:521
  7.5 1.9 %collective-permute-start.1 = (f32[2,24,128]{2,1,0:T(8,128)S(1)}, f32[2,24,128]{2,1,0:T(8,128)S(1)}, u32[]{:S(2)}, u32[]{:S(2)}) collective-permute-start(f32[2,24,128]{2,1,0:T(8,128)S(1)} %get-tuple-element.26), channel_id=1, source_target_pairs={{0,1},{2,3},{4,5},{6,7},{8,9},{10,11},{12,13},{14,15},{16,17},{18,... | collective-permute-start | bytes 73736 | tf_op jit(solution)/shard_map/ppermute | solution.py:521
  9.4 0.0 copy-done
  9.4 0.0 copy-done.1
  9.5 0.0 copy-start.2
  9.5 0.1 shard_map.70
  9.6 0.0 collective-permute-done.far_y
  9.6 2.5 %collective-permute-done.1.near_y = f32[2,24,128]{2,1,0:T(8,128)S(1)} collective-permute-done((f32[2,24,128]{2,1,0:T(8,128)S(1)}, f32[2,24,128]{2,1,0:T(8,128)S(1)}, u32[]{:S(2)}, u32[]{:S(2)}) %collective-permute-start.1) | collective-permute-done | bytes 24608 | tf_op jit(solution)/shard_map/ppermute | solution.py:521
  12.1 0.0 copy-done.2
  12.1 0.2 shard_map.71
  12.3 10.8 %collective-permute-start.2 = (f32[88,256]{1,0:T(8,128)S(1)}, f32[88,256]{1,0:T(8,128)S(1)}, u32[]{:S(2)}, u32[]{:S(2)}) collective-permute-start(f32[88,256]{1,0:T(8,128)S(1)} %get-tuple-element.35), channel_id=1, source_target_pairs={{24,48},{72,96},{120,144},{168,192},{216,240},{264,288},{312,336},... | collective-permute-start | bytes 270344 | tf_op jit(solution)/shard_map/ppermute | solution.py:521
  23.1 1.9 %collective-permute-start.3 = (f32[88,256]{1,0:T(8,128)S(1)}, f32[88,256]{1,0:T(8,128)S(1)}, u32[]{:S(2)}, u32[]{:S(2)}) collective-permute-start(f32[88,256]{1,0:T(8,128)S(1)} %get-tuple-element.36), channel_id=1, source_target_pairs={{0,24},{48,72},{96,120},{144,168},{192,216},{240,264},{288,312},{3... | collective-permute-start | bytes 270344 | tf_op jit(solution)/shard_map/ppermute | solution.py:521
  25.1 0.3 shard_map.69
  25.3 0.0 collective-permute-done.2.far_x
  25.3 1.0 %collective-permute-done.3.near_x = f32[88,256]{1,0:T(8,128)S(1)} collective-permute-done((f32[88,256]{1,0:T(8,128)S(1)}, f32[88,256]{1,0:T(8,128)S(1)}, u32[]{:S(2)}, u32[]{:S(2)}) %collective-permute-start.3) | collective-permute-done | bytes 90144 | tf_op jit(solution)/shard_map/ppermute | solution.py:521
  26.3 2.6 %shard_map.72 = (f32[5,40,384]{2,1,0:T(8,128)S(1)}, f32[25,16,384]{2,1,0:T(8,128)S(1)}, f32[5,16,384]{2,1,0:T(8,128)S(1)}, f32[5,16,384]{2,1,0:T(8,128)S(1)}, f3...) custom-call(f32[25,24,384]{2,1,0:T(8,128)S(1)} %get-tuple-element.27, ...), custom_call_target="tpu_custom_call" | custom-call | tf_op jit(solution)/shard_map/pallas_call | solution.py:508
  28.9 14.4 %all-to-all-start = ((f32[32,5,2,128]{3,2,1,0:T(2,128)}), f32[32,5,2,128]{3,2,1,0:T(2,128)S(1)}, u32[]{:S(2)}, u32[]{:S(2)}) async-start(f32[32,5,2,128]{3,2,1,0:T(2,128)} %get-tuple-element.45), calls=%async_computation | async-start | bytes 327680 | tf_op jit(solution)/shard_map/all_to_all | solution.py:579
  43.3 6.5 %collective-permute-start.4 = (f32[16,384]{1,0:T(8,128)S(1)}, f32[16,384]{1,0:T(8,128)S(1)}, u32[]{:S(2)}, u32[]{:S(2)}) collective-permute-start(f32[16,384]{1,0:T(8,128)S(1)} %get-tuple-element.43), channel_id=1, source_target_pairs={{24,48},{72,96},{120,144},{168,192},{216,240},{264,288},{312,336},... | collective-permute-start | bytes 73736 | tf_op jit(solution)/shard_map/ppermute | solution.py:521
  49.8 1.9 %collective-permute-start.5 = (f32[16,384]{1,0:T(8,128)S(1)}, f32[16,384]{1,0:T(8,128)S(1)}, u32[]{:S(2)}, u32[]{:S(2)}) collective-permute-start(f32[16,384]{1,0:T(8,128)S(1)} %get-tuple-element.44), channel_id=1, source_target_pairs={{0,24},{48,72},{96,120},{144,168},{192,216},{240,264},{288,312},{3... | collective-permute-start | bytes 73736 | tf_op jit(solution)/shard_map/ppermute | solution.py:521
  51.8 1.2 %collective-permute-done.4.far_state = f32[16,384]{1,0:T(8,128)S(1)} collective-permute-done((f32[16,384]{1,0:T(8,128)S(1)}, f32[16,384]{1,0:T(8,128)S(1)}, u32[]{:S(2)}, u32[]{:S(2)}) %collective-permute-start.4) | collective-permute-done | bytes 24608 | tf_op jit(solution)/shard_map/ppermute | solution.py:521
  53.0 0.0 collective-permute-done.5.near_state
  53.0 4.6 %all-to-all-done.got = f32[32,5,2,128]{3,2,1,0:T(2,128)S(1)} async-done(((f32[32,5,2,128]{3,2,1,0:T(2,128)}), f32[32,5,2,128]{3,2,1,0:T(2,128)S(1)}, u32[]{:S(2)}, u32[]{:S(2)}) %all-to-all-start) | async-done | bytes 163872 | tf_op jit(solution)/shard_map/all_to_all | solution.py:579
  57.6 1.9 %shard_map.73 = (f32[5,24,256]{2,1,0:T(8,128)}, f32[5,24,256]{2,1,0:T(8,128)}) custom-call(f32[25,24,384]{2,1,0:T(8,128)S(1)} %get-tuple-element.27.jac_own, f32[5,24,384]{2,1,0:T(8,128)S(1)} %get-tuple-element.28.rhs_own, f32[5,24,384]{2,1,0:T(8,128)S(1)} %get-tuple-element.29.scaled_own, f32[48,128]{1,0:T(8,128)S(1)} %get-tuple-element.32.low, ...), custom_call_target="tpu_custom_call" | custom-call | tf_op jit(solution)/shard_map/pallas_call | solution.py:508
Async XLA Ops:
  0.6 8.8 %copy-start = (f32[5,5,24,256]{3,2,1,0:T(8,128)S(1)}, f32[5,5,24,256]{3,2,1,0:T(8,128)}, u32[]{:S(2)}) copy-start(f32[5,5,24,256]{3,2,1,0:T(8,128)} %jac.1) | copy-start | bytes 1843204
  0.6 8.8 %copy-start.1 = (s32[24,256]{1,0:T(8,128)S(1)}, s32[24,256]{1,0:T(8,128)}, u32[]{:S(2)}) copy-start(s32[24,256]{1,0:T(8,128)} %flags.3) | copy-start | bytes 73732
  3.1 6.5 %collective-permute-start = (f32[2,24,128]{2,1,0:T(8,128)S(1)}, f32[2,24,128]{2,1,0:T(8,128)S(1)}, u32[]{:S(2)}, u32[]{:S(2)}) collective-permute-start(f32[2,24,128]{2,1,0:T(8,128)S(1)} %get-tuple-element.25), channel_id=1, source_target_pairs={{1,2},{3,4},{5,6},{7,8},{9,10},{11,12},{13,14},{15,16},{17,18},{19... | collective-permute-start | bytes 73736 | tf_op jit(solution)/shard_map/ppermute | solution.py:521
  7.5 4.6 %collective-permute-start.1 = (f32[2,24,128]{2,1,0:T(8,128)S(1)}, f32[2,24,128]{2,1,0:T(8,128)S(1)}, u32[]{:S(2)}, u32[]{:S(2)}) collective-permute-start(f32[2,24,128]{2,1,0:T(8,128)S(1)} %get-tuple-element.26), channel_id=1, source_target_pairs={{0,1},{2,3},{4,5},{6,7},{8,9},{10,11},{12,13},{14,15},{16,17},{18,... | collective-permute-start | bytes 73736 | tf_op jit(solution)/shard_map/ppermute | solution.py:521
  9.5 2.6 %copy-start.2 = (f32[5,6,64]{2,1,0:T(8,128)S(1)}, f32[5,6,64]{2,1,0:T(8,128)}, u32[]{:S(2)}) copy-start(f32[5,6,64]{2,1,0:T(8,128)} %coef.1) | copy-start | bytes 23044
  12.3 13.1 %collective-permute-start.2 = (f32[88,256]{1,0:T(8,128)S(1)}, f32[88,256]{1,0:T(8,128)S(1)}, u32[]{:S(2)}, u32[]{:S(2)}) collective-permute-start(f32[88,256]{1,0:T(8,128)S(1)} %get-tuple-element.35), channel_id=1, source_target_pairs={{24,48},{72,96},{120,144},{168,192},{216,240},{264,288},{312,336},... | collective-permute-start | bytes 270344 | tf_op jit(solution)/shard_map/ppermute | solution.py:521
  23.1 3.2 %collective-permute-start.3 = (f32[88,256]{1,0:T(8,128)S(1)}, f32[88,256]{1,0:T(8,128)S(1)}, u32[]{:S(2)}, u32[]{:S(2)}) collective-permute-start(f32[88,256]{1,0:T(8,128)S(1)} %get-tuple-element.36), channel_id=1, source_target_pairs={{0,24},{48,72},{96,120},{144,168},{192,216},{240,264},{288,312},{3... | collective-permute-start | bytes 270344 | tf_op jit(solution)/shard_map/ppermute | solution.py:521
  28.9 28.7 %all-to-all-start = ((f32[32,5,2,128]{3,2,1,0:T(2,128)}), f32[32,5,2,128]{3,2,1,0:T(2,128)S(1)}, u32[]{:S(2)}, u32[]{:S(2)}) async-start(f32[32,5,2,128]{3,2,1,0:T(2,128)} %get-tuple-element.45), calls=%async_computation | async-start | bytes 327680 | tf_op jit(solution)/shard_map/all_to_all | solution.py:579
  43.3 9.7 %collective-permute-start.4 = (f32[16,384]{1,0:T(8,128)S(1)}, f32[16,384]{1,0:T(8,128)S(1)}, u32[]{:S(2)}, u32[]{:S(2)}) collective-permute-start(f32[16,384]{1,0:T(8,128)S(1)} %get-tuple-element.43), channel_id=1, source_target_pairs={{24,48},{72,96},{120,144},{168,192},{216,240},{264,288},{312,336},... | collective-permute-start | bytes 73736 | tf_op jit(solution)/shard_map/ppermute | solution.py:521
  49.8 3.1 %collective-permute-start.5 = (f32[16,384]{1,0:T(8,128)S(1)}, f32[16,384]{1,0:T(8,128)S(1)}, u32[]{:S(2)}, u32[]{:S(2)}) collective-permute-start(f32[16,384]{1,0:T(8,128)S(1)} %get-tuple-element.44), channel_id=1, source_target_pairs={{0,24},{48,72},{96,120},{144,168},{192,216},{240,264},{288,312},{3... | collective-permute-start | bytes 73736 | tf_op jit(solution)/shard_map/ppermute | solution.py:521

commit v6 on v5

--- a/solution.py
+++ b/solution.py
@@ -8,7 +8,7 @@
 F = 5
 TX = 24
 TY = 256
-EX = 40
+EX = 32
 EY = 384
 ROWS = 6
 PLANES = 31
@@ -96,9 +96,9 @@
         gathered.append(total)
     pairs = ((iota((2 * TY, TY), 0) >> 1) == iota((2 * TY, TY), 1)).astype(F32)
     gathered.append(jnp.zeros((8, 2 * TY), F32))
-    summed = select_columns(jnp.concatenate(gathered, axis=0), pairs)
     for copy in late:
         copy.wait()
+    summed = select_columns(jnp.concatenate(gathered, axis=0), pairs)
     planes = [summed[TX * f : TX * (f + 1)] for f in range(F)]
     for f in range(F):
         rhs[f] = planes[f]
@@ -257,7 +257,7 @@
 
 
 def planes_of(own, beyond):
-    return lambda p: jnp.concatenate([beyond[p, 0:8], own[p], beyond[p, 8:16]], axis=0)
+    return lambda p: jnp.concatenate([own[p], beyond[p]], axis=0)
 
 
 def columns(shape, fine_dim, coarse_dim):
@@ -275,19 +275,19 @@
     near_rows, far_rows = near_x[0:ROWS_SENT, :], far_x[0:ROWS_SENT, :]
     sides[0] = jnp.where(odd, near_rows, far_rows)
     sides[1] = jnp.where(odd, far_rows, near_rows)
-    none = jnp.zeros((16, TY), F32)
+    none = jnp.zeros((8, TY), F32)
 
     def put(out, at, rows):
         out[8 - rows : 8, 0:TY] = sides[0, at : at + rows]
-        out[8 : 8 + rows, 0:TY] = sides[1, at : at + rows]
+        out[0:rows, 0:TY] = sides[1, at : at + rows]
 
     for side in range(2):
         at = CORNER_AT + 3 * side
         for a in range(2):
             lanes = slice(128 * a, 128 * (a + 1))
-            beside[side, a] = jnp.zeros((16, 128), F32)
+            beside[side, a] = jnp.zeros((8, 128), F32)
             beside[side, a, 5:8] = sides[0, at : at + 3, lanes]
-            beside[side, a, 8:11] = sides[1, at : at + 3, lanes]
+            beside[side, a, 0:3] = sides[1, at : at + 3, lanes]
     far, near = [[beside[side, a] for a in range(2)] for side in range(2)]
     for p in range(F * F):
         jac[p, :, 0:TY] = none
@@ -295,7 +295,7 @@
         if p % (F + 1) == 0:
             f = p // (F + 1)
             jac[p, 5:6, 0:TY] = sides[0, DIAG_AT + f : DIAG_AT + f + 1]
-            jac[p, 10:11, 0:TY] = sides[1, DIAG_AT + f : DIAG_AT + f + 1]
+            jac[p, 2:3, 0:TY] = sides[1, DIAG_AT + f : DIAG_AT + f + 1]
         jac[p, :, TY:EY] = unpack(near[p // 16], far[p // 16], p)
     for f in range(F):
         rhs[f, :, 0:TY] = none
@@ -315,7 +315,7 @@
     sweep(other, state, scaled_plane, rhs_plane, jac_plane)
     means[...] = jnp.zeros((8 * ROWS, EY), F32)
     for f in range(F):
-        left_over = residual(f, state, rhs_plane, jac_plane)[8 : 8 + TX]
+        left_over = residual(f, state, rhs_plane, jac_plane)[0:TX]
         left_over = left_over + roll(left_over, -1, 0)
         left_over = left_over + roll(left_over, -2, 0)
         for k in range(ROWS):
@@ -358,16 +358,21 @@
     odd_part = jnp.where(pair == 32, x0, jnp.where(pair == 33, roll(x1, 2, 1), odd_part))
     main = jnp.where(lane < 64, x0, roll(x1, 64, 1))
     rest = jnp.where(odd, odd_part, even_part)
-    for f in range(F):
-        block[f, 0:1] = main[f : f + 1]
-        block[f, 1:2] = rest[f : f + 1]
-    copies = [pltpu.make_async_copy(block, sent.at[k], sems.at[k]) for k in range(sent.shape[0])]
+    each = block.shape[0]
+    for f in range(F):
+        both = jnp.concatenate([main[f : f + 1], rest[f : f + 1]], axis=0)
+        for k in range(each):
+            block[k, f] = both
+    copies = [
+        pltpu.make_async_copy(block, sent.at[k * each : (k + 1) * each], sems.at[k])
+        for k in range(sent.shape[0] // each)
+    ]
     for copy in copies:
         copy.start()
     near_state[15:16] = jnp.zeros((1, EY), F32)
     far_state[15:16] = jnp.zeros((1, EY), F32)
     for f in range(F):
-        first, last = state[f, 8:11], state[f, 5 + TX : 8 + TX]
+        first, last = state[f, 0:3], state[f, TX - 3 : TX]
         near_state[3 * f : 3 * f + 3] = jnp.where(odd, first, last)
         far_state[3 * f : 3 * f + 3] = jnp.where(odd, last, first)
     for copy in copies:
@@ -472,26 +477,26 @@
     for f in range(F):
         tiles = []
         for v in range(EX // 8):
-            one = repeated(8 * (2 * v - 1) + f) if v else 0.0
-            two = repeated(8 * (2 * v) + f) if v < EX // 8 - 1 else 0.0
+            groups = (2 * v + 1, (2 * v + 2) % 8)
+            one, two = [repeated(8 * group + f) for group in groups]
             tiles.append(jnp.where(upper, one, two))
         added = jnp.where(scaled_plane(f) != 0.0, jnp.concatenate(tiles, axis=0), 0.0)
         other[f] = state_in[f]
         far, near = far_state[3 * f : 3 * f + 3], near_state[3 * f : 3 * f + 3]
-        other[f, 5:8] = jnp.where(odd, near, far)
-        other[f, 8 + TX : 11 + TX] = jnp.where(odd, far, near)
+        other[f, EX - 3 : EX] = jnp.where(odd, near, far)
+        other[f, TX : TX + 3] = jnp.where(odd, far, near)
         state[f] = other[f] + added
     sweep(state, other, scaled_plane, rhs_plane, jac_plane)
     sweep(other, state, scaled_plane, rhs_plane, jac_plane)
     copies = []
     for f in range(F):
-        correction[f] = state[f, 8 : 8 + TX, 0:TY]
+        correction[f] = state[f, 0:TX, 0:TY]
         copies.append(
             pltpu.make_async_copy(correction.at[f], correction_out.at[f], sems.at[0, f])
         )
         copies[-1].start()
     for f in range(F):
-        level_residual[f] = residual(f, state, rhs_plane, jac_plane)[8 : 8 + TX, 0:TY]
+        level_residual[f] = residual(f, state, rhs_plane, jac_plane)[0:TX, 0:TY]
         copies.append(
             pltpu.make_async_copy(level_residual.at[f], level_residual_out.at[f], sems.at[1, f])
         )
@@ -557,20 +562,20 @@
         own_kernel, [shape_of(F * F, TX, EY), own, own], [], jac, rhs, flags, far_y, near_y
     )
     tile = pltpu.VMEM((F, EX, EY), F32)
-    beyond = shape_of(F, 16, EY)
+    beyond = shape_of(F, 8, EY)
     ends = shape_of(16, EY)
     state, jac_beyond, rhs_beyond, scaled_beyond, value, chip, near_state, far_state, sent = call(
         before_kernel,
         [
-            shape_of(F, EX, EY), shape_of(F * F, 16, EY), beyond, beyond, lines, shape_of(6, 8, 128), ends, ends,
+            shape_of(F, EX, EY), shape_of(F * F, 8, EY), beyond, beyond, lines, shape_of(6, 8, 128), ends, ends,
             shape_of(count, F, 2, 128),
         ],
         [
             tile,
             pltpu.VMEM((2, ROWS_SENT, TY), F32),
-            pltpu.VMEM((2, 2, 16, 128), F32),
+            pltpu.VMEM((2, 2, 8, 128), F32),
             pltpu.VMEM((8 * ROWS, EY), F32),
-            pltpu.VMEM((F, 2, 128), F32),
+            pltpu.VMEM((min(count, 8), F, 2, 128), F32),
             pltpu.SemaphoreType.DMA((count,)),
         ],
         jac_own, rhs_own, scaled_own, low, high, turn, far_x, near_x,

time: 59.9 us -> 59.3 us (0.990)
  Pallas kernels: 7.53 us -> 6.9 us
    pallas_call x6, Pallas kernels: 7.53 us -> 6.9 us  [call(): pl.pallas_call(kernel, out_shape=outs, in_specs=[pl.BlockSpec(memory_spac...]
where the time goes in v6:
time: 59.3 us; the launch traced here: 58.9 us
  starting transfers between devices  41.9 us (71%)
  waiting for transfers between devices  9.31 us (16%)
  Pallas kernels  6.9 us (12%)
  between operations  0.78 us (1%)
    ppermute x6, starting transfers between devices, swap(): lax.ppermute(value, axis, [(i, i + 1) for i in firsts] + [(i + 1, i) for...  27.6 us
    all_to_all x1, starting transfers between devices, local(): got = lax.all_to_all(sent, 'gx', 0, 0, tiled=True)  14.4 us
    pallas_call x6, Pallas kernels, call(): pl.pallas_call(kernel, out_shape=outs, in_specs=[pl.BlockSpec(memory_spac...  6.9 us
    ppermute x6, waiting for transfers between devices, swap(): lax.ppermute(value, axis, [(i, i + 1) for i in firsts] + [(i + 1, i) for...  4.7 us
    all_to_all x1, waiting for transfers between devices, local(): got = lax.all_to_all(sent, 'gx', 0, 0, tiled=True)  4.61 us
  transfers between devices with their start and end apart: 7, of which 4 were waited for; matrix products, arithmetic and copies ran while one was open for 0% of the time, Pallas kernels for 1%

profile of v6, /device:TPU:89, one launch (start us, length us, event | category | flops | bytes accessed | tf_op | source)
XLA Modules:
  0.0 58.9 jit_solution(11695369344598454486)
XLA Ops:
  0.6 0.0 copy-start
  0.6 0.0 copy-start.1
  0.7 2.3 %shard_map.68 = (f32[5,24,256]{2,1,0:T(8,128)S(1)}, f32[2,24,128]{2,1,0:T(8,128)S(1)}, f32[2,24,128]{2,1,0:T(8,128)S(1)}) custom-call(f32[5,48,512]{2,1,0:T(8,128)} %fine_in.1, s32[48,512]{1,0:T(8,128)} %owner_in.1, s32[24,256]{1,0:T(8,128)} %flags.3, f32[5,5,24,256]{3,2,1,0:T(8,128)} %jac.1, f32[5,6,64]{2,1,0:T(8,128)} %coef.1), custom_call_target="tpu_custom_call" | custom-call | tf_op jit(solution)/shard_map/pallas_call | solution.py:513
  2.9 4.4 %collective-permute-start = (f32[2,24,128]{2,1,0:T(8,128)S(1)}, f32[2,24,128]{2,1,0:T(8,128)S(1)}, u32[]{:S(2)}, u32[]{:S(2)}) collective-permute-start(f32[2,24,128]{2,1,0:T(8,128)S(1)} %get-tuple-element.25), channel_id=1, source_target_pairs={{1,2},{3,4},{5,6},{7,8},{9,10},{11,12},{13,14},{15,16},{17,18},{19... | collective-permute-start | bytes 73736 | tf_op jit(solution)/shard_map/ppermute | solution.py:526
  7.3 1.9 %collective-permute-start.1 = (f32[2,24,128]{2,1,0:T(8,128)S(1)}, f32[2,24,128]{2,1,0:T(8,128)S(1)}, u32[]{:S(2)}, u32[]{:S(2)}) collective-permute-start(f32[2,24,128]{2,1,0:T(8,128)S(1)} %get-tuple-element.26), channel_id=1, source_target_pairs={{0,1},{2,3},{4,5},{6,7},{8,9},{10,11},{12,13},{14,15},{16,17},{18,... | collective-permute-start | bytes 73736 | tf_op jit(solution)/shard_map/ppermute | solution.py:526
  9.3 0.0 copy-done
  9.3 0.0 copy-done.1
  9.3 0.0 copy-start.2
  9.3 0.1 shard_map.70
  9.4 0.0 collective-permute-done.far_y
  9.4 2.5 %collective-permute-done.1.near_y = f32[2,24,128]{2,1,0:T(8,128)S(1)} collective-permute-done((f32[2,24,128]{2,1,0:T(8,128)S(1)}, f32[2,24,128]{2,1,0:T(8,128)S(1)}, u32[]{:S(2)}, u32[]{:S(2)}) %collective-permute-start.1) | collective-permute-done | bytes 24608 | tf_op jit(solution)/shard_map/ppermute | solution.py:526
  11.9 0.0 copy-done.2
  11.9 0.2 shard_map.71
  12.1 10.8 %collective-permute-start.2 = (f32[88,256]{1,0:T(8,128)S(1)}, f32[88,256]{1,0:T(8,128)S(1)}, u32[]{:S(2)}, u32[]{:S(2)}) collective-permute-start(f32[88,256]{1,0:T(8,128)S(1)} %get-tuple-element.35), channel_id=1, source_target_pairs={{24,48},{72,96},{120,144},{168,192},{216,240},{264,288},{312,336},... | collective-permute-start | bytes 270344 | tf_op jit(solution)/shard_map/ppermute | solution.py:526
  23.0 1.9 %collective-permute-start.3 = (f32[88,256]{1,0:T(8,128)S(1)}, f32[88,256]{1,0:T(8,128)S(1)}, u32[]{:S(2)}, u32[]{:S(2)}) collective-permute-start(f32[88,256]{1,0:T(8,128)S(1)} %get-tuple-element.36), channel_id=1, source_target_pairs={{0,24},{48,72},{96,120},{144,168},{192,216},{240,264},{288,312},{3... | collective-permute-start | bytes 270344 | tf_op jit(solution)/shard_map/ppermute | solution.py:526
  24.9 0.3 shard_map.69
  25.2 0.0 collective-permute-done.2.far_x
  25.2 1.0 %collective-permute-done.3.near_x = f32[88,256]{1,0:T(8,128)S(1)} collective-permute-done((f32[88,256]{1,0:T(8,128)S(1)}, f32[88,256]{1,0:T(8,128)S(1)}, u32[]{:S(2)}, u32[]{:S(2)}) %collective-permute-start.3) | collective-permute-done | bytes 90144 | tf_op jit(solution)/shard_map/ppermute | solution.py:526
  26.2 2.2 %shard_map.72 = (f32[5,32,384]{2,1,0:T(8,128)S(1)}, f32[25,8,384]{2,1,0:T(8,128)S(1)}, f32[5,8,384]{2,1,0:T(8,128)S(1)}, f32[5,8,384]{2,1,0:T(8,128)S(1)}, f32[4...) custom-call(f32[25,24,384]{2,1,0:T(8,128)S(1)} %get-tuple-element.27, ...), custom_call_target="tpu_custom_call" | custom-call | tf_op jit(solution)/shard_map/pallas_call | solution.py:513
  28.4 14.4 %all-to-all-start = ((f32[32,5,2,128]{3,2,1,0:T(2,128)}), f32[32,5,2,128]{3,2,1,0:T(2,128)S(1)}, u32[]{:S(2)}, u32[]{:S(2)}) async-start(f32[32,5,2,128]{3,2,1,0:T(2,128)} %get-tuple-element.45), calls=%async_computation | async-start | bytes 327680 | tf_op jit(solution)/shard_map/all_to_all | solution.py:584
  42.8 6.5 %collective-permute-start.4 = (f32[16,384]{1,0:T(8,128)S(1)}, f32[16,384]{1,0:T(8,128)S(1)}, u32[]{:S(2)}, u32[]{:S(2)}) collective-permute-start(f32[16,384]{1,0:T(8,128)S(1)} %get-tuple-element.43), channel_id=1, source_target_pairs={{24,48},{72,96},{120,144},{168,192},{216,240},{264,288},{312,336},... | collective-permute-start | bytes 73736 | tf_op jit(solution)/shard_map/ppermute | solution.py:526
  49.3 1.9 %collective-permute-start.5 = (f32[16,384]{1,0:T(8,128)S(1)}, f32[16,384]{1,0:T(8,128)S(1)}, u32[]{:S(2)}, u32[]{:S(2)}) collective-permute-start(f32[16,384]{1,0:T(8,128)S(1)} %get-tuple-element.44), channel_id=1, source_target_pairs={{0,24},{48,72},{96,120},{144,168},{192,216},{240,264},{288,312},{3... | collective-permute-start | bytes 73736 | tf_op jit(solution)/shard_map/ppermute | solution.py:526
  51.3 1.2 %collective-permute-done.4.far_state = f32[16,384]{1,0:T(8,128)S(1)} collective-permute-done((f32[16,384]{1,0:T(8,128)S(1)}, f32[16,384]{1,0:T(8,128)S(1)}, u32[]{:S(2)}, u32[]{:S(2)}) %collective-permute-start.4) | collective-permute-done | bytes 24608 | tf_op jit(solution)/shard_map/ppermute | solution.py:526
  52.5 0.0 collective-permute-done.5.near_state
  52.5 4.6 %all-to-all-done.got = f32[32,5,2,128]{3,2,1,0:T(2,128)S(1)} async-done(((f32[32,5,2,128]{3,2,1,0:T(2,128)}), f32[32,5,2,128]{3,2,1,0:T(2,128)S(1)}, u32[]{:S(2)}, u32[]{:S(2)}) %all-to-all-start) | async-done | bytes 163872 | tf_op jit(solution)/shard_map/all_to_all | solution.py:584
  57.1 1.8 %shard_map.73 = (f32[5,24,256]{2,1,0:T(8,128)}, f32[5,24,256]{2,1,0:T(8,128)}) custom-call(f32[25,24,384]{2,1,0:T(8,128)S(1)} %get-tuple-element.27.jac_own, f32[5,24,384]{2,1,0:T(8,128)S(1)} %get-tuple-element.28.rhs_own, f32[5,24,384]{2,1,0:T(8,128)S(1)} %get-tuple-element.29.scaled_own, f32[48,128]{1,0:T(8,128)S(1)} %get-tuple-element.32.low, ...), custom_call_target="tpu_custom_call" | custom-call | tf_op jit(solution)/shard_map/pallas_call | solution.py:513
Async XLA Ops:
  0.6 8.6 %copy-start = (f32[5,5,24,256]{3,2,1,0:T(8,128)S(1)}, f32[5,5,24,256]{3,2,1,0:T(8,128)}, u32[]{:S(2)}) copy-start(f32[5,5,24,256]{3,2,1,0:T(8,128)} %jac.1) | copy-start | bytes 1843204
  0.6 8.6 %copy-start.1 = (s32[24,256]{1,0:T(8,128)S(1)}, s32[24,256]{1,0:T(8,128)}, u32[]{:S(2)}) copy-start(s32[24,256]{1,0:T(8,128)} %flags.3) | copy-start | bytes 73732
  2.9 6.5 %collective-permute-start = (f32[2,24,128]{2,1,0:T(8,128)S(1)}, f32[2,24,128]{2,1,0:T(8,128)S(1)}, u32[]{:S(2)}, u32[]{:S(2)}) collective-permute-start(f32[2,24,128]{2,1,0:T(8,128)S(1)} %get-tuple-element.25), channel_id=1, source_target_pairs={{1,2},{3,4},{5,6},{7,8},{9,10},{11,12},{13,14},{15,16},{17,18},{19... | collective-permute-start | bytes 73736 | tf_op jit(solution)/shard_map/ppermute | solution.py:526
  7.3 4.6 %collective-permute-start.1 = (f32[2,24,128]{2,1,0:T(8,128)S(1)}, f32[2,24,128]{2,1,0:T(8,128)S(1)}, u32[]{:S(2)}, u32[]{:S(2)}) collective-permute-start(f32[2,24,128]{2,1,0:T(8,128)S(1)} %get-tuple-element.26), channel_id=1, source_target_pairs={{0,1},{2,3},{4,5},{6,7},{8,9},{10,11},{12,13},{14,15},{16,17},{18,... | collective-permute-start | bytes 73736 | tf_op jit(solution)/shard_map/ppermute | solution.py:526
  9.3 2.6 %copy-start.2 = (f32[5,6,64]{2,1,0:T(8,128)S(1)}, f32[5,6,64]{2,1,0:T(8,128)}, u32[]{:S(2)}) copy-start(f32[5,6,64]{2,1,0:T(8,128)} %coef.1) | copy-start | bytes 23044
  12.1 13.1 %collective-permute-start.2 = (f32[88,256]{1,0:T(8,128)S(1)}, f32[88,256]{1,0:T(8,128)S(1)}, u32[]{:S(2)}, u32[]{:S(2)}) collective-permute-start(f32[88,256]{1,0:T(8,128)S(1)} %get-tuple-element.35), channel_id=1, source_target_pairs={{24,48},{72,96},{120,144},{168,192},{216,240},{264,288},{312,336},... | collective-permute-start | bytes 270344 | tf_op jit(solution)/shard_map/ppermute | solution.py:526
  23.0 3.2 %collective-permute-start.3 = (f32[88,256]{1,0:T(8,128)S(1)}, f32[88,256]{1,0:T(8,128)S(1)}, u32[]{:S(2)}, u32[]{:S(2)}) collective-permute-start(f32[88,256]{1,0:T(8,128)S(1)} %get-tuple-element.36), channel_id=1, source_target_pairs={{0,24},{48,72},{96,120},{144,168},{192,216},{240,264},{288,312},{3... | collective-permute-start | bytes 270344 | tf_op jit(solution)/shard_map/ppermute | solution.py:526
  28.4 28.7 %all-to-all-start = ((f32[32,5,2,128]{3,2,1,0:T(2,128)}), f32[32,5,2,128]{3,2,1,0:T(2,128)S(1)}, u32[]{:S(2)}, u32[]{:S(2)}) async-start(f32[32,5,2,128]{3,2,1,0:T(2,128)} %get-tuple-element.45), calls=%async_computation | async-start | bytes 327680 | tf_op jit(solution)/shard_map/all_to_all | solution.py:584
  42.8 9.7 %collective-permute-start.4 = (f32[16,384]{1,0:T(8,128)S(1)}, f32[16,384]{1,0:T(8,128)S(1)}, u32[]{:S(2)}, u32[]{:S(2)}) collective-permute-start(f32[16,384]{1,0:T(8,128)S(1)} %get-tuple-element.43), channel_id=1, source_target_pairs={{24,48},{72,96},{120,144},{168,192},{216,240},{264,288},{312,336},... | collective-permute-start | bytes 73736 | tf_op jit(solution)/shard_map/ppermute | solution.py:526
  49.3 3.2 %collective-permute-start.5 = (f32[16,384]{1,0:T(8,128)S(1)}, f32[16,384]{1,0:T(8,128)S(1)}, u32[]{:S(2)}, u32[]{:S(2)}) collective-permute-start(f32[16,384]{1,0:T(8,128)S(1)} %get-tuple-element.44), channel_id=1, source_target_pairs={{0,24},{48,72},{96,120},{144,168},{192,216},{240,264},{288,312},{3... | collective-permute-start | bytes 73736 | tf_op jit(solution)/shard_map/ppermute | solution.py:526

commit v7 on v6

--- a/solution.py
+++ b/solution.py
@@ -132,7 +132,7 @@
     far[1, 0:ROWS, :] = last
 
 
-JAC_AT, RHS_AT, CODE_AT, DIAG_AT, CORNER_AT, ROWS_SENT = 0, 50, 65, 68, 74, 80
+RHS_AT, STATE_AT, CODE_AT, CORNER_AT, LINE_AT, ROWS_SENT = 50, 60, 65, 68, 74, 80
 
 
 def rows_kernel(jac, rhs, flags, near, far):
@@ -142,12 +142,16 @@
         third = 2 if first else TX - 3
         for p in range(F * F):
             out[2 * p : 2 * p + 2] = jac[p // F, p % F, start : start + 2, :]
+        kinds = flags[third : third + 1, :]
+        interior, wall = kinds == 0, kinds == 2
         for f in range(F):
-            at = RHS_AT + 3 * f
-            out[at : at + 3] = rhs[f, wide : wide + 3, :]
-            out[DIAG_AT + f : DIAG_AT + f + 1] = jac[f, f, third : third + 1, :]
+            at = RHS_AT + 2 * f
+            out[at : at + 2] = rhs[f, start : start + 2, :]
+            kept = interior if f in (1, 2) else interior | wall
+            scaled = jnp.where(kept, 0.8 / jac[f, f, third : third + 1, :], 0.0)
+            out[STATE_AT + f : STATE_AT + f + 1] = scaled * rhs[f, third : third + 1, :]
         out[CODE_AT : CODE_AT + 3] = (flags[wide : wide + 3, :] + 1).astype(F32)
-        out[73:ROWS_SENT] = jnp.zeros((ROWS_SENT - 73, TY), F32)
+        out[CORNER_AT:ROWS_SENT] = jnp.zeros((ROWS_SENT - CORNER_AT, TY), F32)
 
     odd = parity("gx")
 
@@ -162,11 +166,10 @@
         write(far, True)
 
 
-def corners_kernel(near_rows, far_rows, coef, far_y, near_y, near, far, low, high, turn, diag):
+def corners_kernel(near_rows, far_rows, coef, near_y, far_y, near, far, low, high, turn, diag):
     odd = parity("gx")
-    near[0:ROWS_SENT] = near_rows[...]
-    far[0:ROWS_SENT] = far_rows[...]
-    far[ROWS_SENT : ROWS_SENT + 8] = jnp.zeros((8, TY), F32)
+    near[...] = near_rows[...]
+    far[...] = far_rows[...]
     for side, strip in enumerate((far_y, near_y)):
         at = CORNER_AT + 3 * side
         for a in range(2):
@@ -203,8 +206,8 @@
     ends = highs[-1]
     for q, part in enumerate((first_low, lows[-1], highs[-1])):
         ends = jnp.where(lane >> 1 == 33 + q, roll(part, 2 * (q + 1), 1), ends)
-    near[ROWS_SENT : ROWS_SENT + 8, 0:128] = jnp.where(lane < 64, first_low, roll(lows[-1], 64, 1))
-    near[ROWS_SENT : ROWS_SENT + 8, 128:TY] = ends
+    near[LINE_AT : LINE_AT + F, 0:128] = jnp.where(lane < 64, first_low, roll(lows[-1], 64, 1))[0:F]
+    near[LINE_AT : LINE_AT + F, 128:TY] = ends[0:F]
 
 
 def unpack(near, far, p):
@@ -228,7 +231,7 @@
 
 
 def own_kernel(
-    jac_in, rhs_in, flags, far_y, near_y, jac, rhs, scaled
+    jac_in, rhs_in, flags, near_y, far_y, jac, rhs, scaled
 ):
     near, far = [near_y[0], near_y[1]], [far_y[0], far_y[1]]
     for p in range(F * F):
@@ -272,9 +275,8 @@
     state, jac, rhs, scaled, value, chip, near_state, far_state, sent, other, sides, beside, means, block, sems,
 ):
     odd = parity("gx")
-    near_rows, far_rows = near_x[0:ROWS_SENT, :], far_x[0:ROWS_SENT, :]
-    sides[0] = jnp.where(odd, near_rows, far_rows)
-    sides[1] = jnp.where(odd, far_rows, near_rows)
+    sides[0] = jnp.where(odd, near_x[...], far_x[...])
+    sides[1] = jnp.where(odd, far_x[...], near_x[...])
     none = jnp.zeros((8, TY), F32)
 
     def put(out, at, rows):
@@ -293,13 +295,12 @@
         jac[p, :, 0:TY] = none
         put(jac.at[p], 2 * p, 2)
         if p % (F + 1) == 0:
-            f = p // (F + 1)
-            jac[p, 5:6, 0:TY] = sides[0, DIAG_AT + f : DIAG_AT + f + 1]
-            jac[p, 2:3, 0:TY] = sides[1, DIAG_AT + f : DIAG_AT + f + 1]
+            jac[p, 5:6, 0:TY] = jnp.ones((1, TY), F32)
+            jac[p, 2:3, 0:TY] = jnp.ones((1, TY), F32)
         jac[p, :, TY:EY] = unpack(near[p // 16], far[p // 16], p)
     for f in range(F):
         rhs[f, :, 0:TY] = none
-        put(rhs.at[f], RHS_AT + 3 * f, 3)
+        put(rhs.at[f], RHS_AT + 2 * f, 2)
         rhs[f, :, TY:EY] = unpack(near[1], far[1], F * F + f)
     code = scaled.at[F - 1]
     code[:, 0:TY] = none
@@ -311,6 +312,8 @@
     scaled_plane = planes_of(scaled_own, scaled)
     for f in range(F):
         state[f] = scaled_plane(f) * rhs_plane(f)
+        state[f, TX + 5 : TX + 6, 0:TY] = sides[0, STATE_AT + f : STATE_AT + f + 1]
+        state[f, TX + 2 : TX + 3, 0:TY] = sides[1, STATE_AT + f : STATE_AT + f + 1]
     sweep(state, other, scaled_plane, rhs_plane, jac_plane)
     sweep(other, state, scaled_plane, rhs_plane, jac_plane)
     means[...] = jnp.zeros((8 * ROWS, EY), F32)
@@ -332,7 +335,8 @@
         first = values[k] + high[8 * k : 8 * k + 8, :] * first
     lane = iota((8, 128), 1)
 
-    packed = [near_x[ROWS_SENT : ROWS_SENT + 8, 128 * a : 128 * (a + 1)] for a in range(2)]
+    packed = [near_x[ROWS_SENT - 8 :, 128 * a : 128 * (a + 1)] for a in range(2)]
+    packed = [roll(part, ROWS_SENT - 8 - LINE_AT, 0) for part in packed]
     theirs = [packed[0], roll(packed[0], 64, 1), packed[1]]
     theirs = [jnp.where(lane < 64, theirs[q], roll(packed[1], -2 * (q + 1), 1)) for q in range(3)]
     own = [turn[...], low[8 * ROWS - 8 :, :], high[8 * ROWS - 8 :, :]]
@@ -369,12 +373,12 @@
     ]
     for copy in copies:
         copy.start()
-    near_state[15:16] = jnp.zeros((1, EY), F32)
-    far_state[15:16] = jnp.zeros((1, EY), F32)
-    for f in range(F):
-        first, last = state[f, 0:3], state[f, TX - 3 : TX]
-        near_state[3 * f : 3 * f + 3] = jnp.where(odd, first, last)
-        far_state[3 * f : 3 * f + 3] = jnp.where(odd, last, first)
+    for f in range(F):
+        for j in range(EY // 128):
+            lanes = slice(128 * j, 128 * (j + 1))
+            first, last = state[f, 1:3, lanes], state[f, TX - 3 : TX - 1, lanes]
+            near_state[f, j] = jnp.where(odd, first, last)
+            far_state[f, j] = jnp.where(odd, last, first)
     for copy in copies:
         copy.wait()
 
@@ -482,9 +486,11 @@
             tiles.append(jnp.where(upper, one, two))
         added = jnp.where(scaled_plane(f) != 0.0, jnp.concatenate(tiles, axis=0), 0.0)
         other[f] = state_in[f]
-        far, near = far_state[3 * f : 3 * f + 3], near_state[3 * f : 3 * f + 3]
-        other[f, EX - 3 : EX] = jnp.where(odd, near, far)
-        other[f, TX : TX + 3] = jnp.where(odd, far, near)
+        for j in range(EY // 128):
+            lanes = slice(128 * j, 128 * (j + 1))
+            far, near = far_state[f, j], near_state[f, j]
+            other[f, EX - 3 : EX - 1, lanes] = jnp.where(odd, near, far)
+            other[f, TX + 1 : TX + 3, lanes] = jnp.where(odd, far, near)
         state[f] = other[f] + added
     sweep(state, other, scaled_plane, rhs_plane, jac_plane)
     sweep(other, state, scaled_plane, rhs_plane, jac_plane)
@@ -550,20 +556,20 @@
     rows, lines, line = shape_of(ROWS_SENT, TY), shape_of(8 * ROWS, 128), shape_of(8, 128)
     near_rows, far_rows, low, high, turn = call(
         corners_kernel,
-        [shape_of(ROWS_SENT + 8, TY), shape_of(ROWS_SENT + 8, TY), lines, lines, line],
+        [rows, rows, lines, lines, line],
         [pltpu.VMEM((8 * ROWS, 128), F32)],
-        near_rows, far_rows, coef, far_y, near_y,
+        near_rows, far_rows, coef, near_y, far_y,
     )
     far_x = swap(far_rows, "gx", 1)
     near_x = swap(near_rows, "gx", 0)
     count = lax.axis_size("gx")
     own = shape_of(F, TX, EY)
     jac_own, rhs_own, scaled_own = call(
-        own_kernel, [shape_of(F * F, TX, EY), own, own], [], jac, rhs, flags, far_y, near_y
+        own_kernel, [shape_of(F * F, TX, EY), own, own], [], jac, rhs, flags, near_y, far_y
     )
     tile = pltpu.VMEM((F, EX, EY), F32)
     beyond = shape_of(F, 8, EY)
-    ends = shape_of(16, EY)
+    ends = shape_of(F, EY // 128, 2, 128)
     state, jac_beyond, rhs_beyond, scaled_beyond, value, chip, near_state, far_state, sent = call(
         before_kernel,
         [

time: 59.3 us -> 58.5 us (0.987)
  the two profiles are of different devices: /device:TPU:89 before, /device:TPU:57 now
where the time goes in v7:
time: 58.5 us; the launch traced here: 58.2 us
  starting transfers between devices  40.5 us (69%)
  waiting for transfers between devices  10 us (17%)
  Pallas kernels  6.89 us (12%)
  between operations  0.78 us (1%)
    ppermute x6, starting transfers between devices, swap(): lax.ppermute(value, axis, [(i, i + 1) for i in firsts] + [(i + 1, i) for...  26.4 us
    all_to_all x1, starting transfers between devices, local(): got = lax.all_to_all(sent, 'gx', 0, 0, tiled=True)  14 us
    pallas_call x6, Pallas kernels, call(): pl.pallas_call(kernel, out_shape=outs, in_specs=[pl.BlockSpec(memory_spac...  6.89 us
    ppermute x6, waiting for transfers between devices, swap(): lax.ppermute(value, axis, [(i, i + 1) for i in firsts] + [(i + 1, i) for...  5.19 us
    all_to_all x1, waiting for transfers between devices, local(): got = lax.all_to_all(sent, 'gx', 0, 0, tiled=True)  4.85 us
  transfers between devices with their start and end apart: 7, of which 5 were waited for; matrix products, arithmetic and copies ran while one was open for 0% of the time, Pallas kernels for 1%

profile of v7, /device:TPU:57, one launch (start us, length us, event | category | flops | bytes accessed | tf_op | source)
XLA Modules:
  0.0 58.2 jit_solution(11470648371870576212)
XLA Ops:
  0.6 0.0 copy-start
  0.6 0.0 copy-start.1
  0.7 2.3 %shard_map.68 = (f32[5,24,256]{2,1,0:T(8,128)S(1)}, f32[2,24,128]{2,1,0:T(8,128)S(1)}, f32[2,24,128]{2,1,0:T(8,128)S(1)}) custom-call(f32[5,48,512]{2,1,0:T(8,128)} %fine_in.1, s32[48,512]{1,0:T(8,128)} %owner_in.1, s32[24,256]{1,0:T(8,128)} %flags.3, f32[5,5,24,256]{3,2,1,0:T(8,128)} %jac.1, f32[5,6,64]{2,1,0:T(8,128)} %coef.1), custom_call_target="tpu_custom_call" | custom-call | tf_op jit(solution)/shard_map/pallas_call | solution.py:519
  2.9 3.0 %collective-permute-start = (f32[2,24,128]{2,1,0:T(8,128)S(1)}, f32[2,24,128]{2,1,0:T(8,128)S(1)}, u32[]{:S(2)}, u32[]{:S(2)}) collective-permute-start(f32[2,24,128]{2,1,0:T(8,128)S(1)} %get-tuple-element.25), channel_id=1, source_target_pairs={{0,1},{2,3},{4,5},{6,7},{8,9},{10,11},{12,13},{14,15},{16,17},{18,... | collective-permute-start | bytes 73736 | tf_op jit(solution)/shard_map/ppermute | solution.py:532
  5.9 3.4 %collective-permute-start.1 = (f32[2,24,128]{2,1,0:T(8,128)S(1)}, f32[2,24,128]{2,1,0:T(8,128)S(1)}, u32[]{:S(2)}, u32[]{:S(2)}) collective-permute-start(f32[2,24,128]{2,1,0:T(8,128)S(1)} %get-tuple-element.26), channel_id=1, source_target_pairs={{1,2},{3,4},{5,6},{7,8},{9,10},{11,12},{13,14},{15,16},{17,18},{19... | collective-permute-start | bytes 73736 | tf_op jit(solution)/shard_map/ppermute | solution.py:532
  9.4 0.0 copy-done
  9.4 0.0 copy-done.1
  9.4 0.0 copy-start.2
  9.4 0.1 shard_map.70
  9.5 0.0 collective-permute-done.near_y
  9.5 3.1 %collective-permute-done.1.far_y = f32[2,24,128]{2,1,0:T(8,128)S(1)} collective-permute-done((f32[2,24,128]{2,1,0:T(8,128)S(1)}, f32[2,24,128]{2,1,0:T(8,128)S(1)}, u32[]{:S(2)}, u32[]{:S(2)}) %collective-permute-start.1) | collective-permute-done | bytes 24608 | tf_op jit(solution)/shard_map/ppermute | solution.py:532
  12.6 0.0 copy-done.2
  12.6 0.2 shard_map.71
  12.8 10.8 %collective-permute-start.2 = (f32[80,256]{1,0:T(8,128)S(1)}, f32[80,256]{1,0:T(8,128)S(1)}, u32[]{:S(2)}, u32[]{:S(2)}) collective-permute-start(f32[80,256]{1,0:T(8,128)S(1)} %get-tuple-element.35), channel_id=1, source_target_pairs={{24,48},{72,96},{120,144},{168,192},{216,240},{264,288},{312,336},... | collective-permute-start | bytes 245768 | tf_op jit(solution)/shard_map/ppermute | solution.py:532
  23.6 1.9 %collective-permute-start.3 = (f32[80,256]{1,0:T(8,128)S(1)}, f32[80,256]{1,0:T(8,128)S(1)}, u32[]{:S(2)}, u32[]{:S(2)}) collective-permute-start(f32[80,256]{1,0:T(8,128)S(1)} %get-tuple-element.36), channel_id=1, source_target_pairs={{0,24},{48,72},{96,120},{144,168},{192,216},{240,264},{288,312},{3... | collective-permute-start | bytes 245768 | tf_op jit(solution)/shard_map/ppermute | solution.py:532
  25.6 0.3 shard_map.69
  25.8 0.0 collective-permute-done.2.far_x
  25.9 0.9 %collective-permute-done.3.near_x = f32[80,256]{1,0:T(8,128)S(1)} collective-permute-done((f32[80,256]{1,0:T(8,128)S(1)}, f32[80,256]{1,0:T(8,128)S(1)}, u32[]{:S(2)}, u32[]{:S(2)}) %collective-permute-start.3) | collective-permute-done | bytes 81952 | tf_op jit(solution)/shard_map/ppermute | solution.py:532
  26.8 2.2 %shard_map.72 = (f32[5,32,384]{2,1,0:T(8,128)S(1)}, f32[25,8,384]{2,1,0:T(8,128)S(1)}, f32[5,8,384]{2,1,0:T(8,128)S(1)}, f32[5,8,384]{2,1,0:T(8,128)S(1)}, f32[4...) custom-call(f32[25,24,384]{2,1,0:T(8,128)S(1)} %get-tuple-element.27, ...), custom_call_target="tpu_custom_call" | custom-call | tf_op jit(solution)/shard_map/pallas_call | solution.py:519
  29.1 14.0 %all-to-all-start = ((f32[32,5,2,128]{3,2,1,0:T(2,128)}), f32[32,5,2,128]{3,2,1,0:T(2,128)S(1)}, u32[]{:S(2)}, u32[]{:S(2)}) async-start(f32[32,5,2,128]{3,2,1,0:T(2,128)} %get-tuple-element.45), calls=%async_computation | async-start | bytes 327680 | tf_op jit(solution)/shard_map/all_to_all | solution.py:590
  43.1 5.3 %collective-permute-start.4 = (f32[5,3,2,128]{3,2,1,0:T(2,128)S(1)}, f32[5,3,2,128]{3,2,1,0:T(2,128)S(1)}, u32[]{:S(2)}, u32[]{:S(2)}) collective-permute-start(f32[5,3,2,128]{3,2,1,0:T(2,128)S(1)} %get-tuple-element.43), channel_id=1, source_target_pairs={{24,48},{72,96},{120,144},{168,192},{216,240},{264,288},{312,336},... | collective-permute-start | bytes 46088 | tf_op jit(solution)/shard_map/ppermute | solution.py:532
  48.4 1.9 %collective-permute-start.5 = (f32[5,3,2,128]{3,2,1,0:T(2,128)S(1)}, f32[5,3,2,128]{3,2,1,0:T(2,128)S(1)}, u32[]{:S(2)}, u32[]{:S(2)}) collective-permute-start(f32[5,3,2,128]{3,2,1,0:T(2,128)S(1)} %get-tuple-element.44), channel_id=1, source_target_pairs={{0,24},{48,72},{96,120},{144,168},{192,216},{240,264},{288,312},{3... | collective-permute-start | bytes 46088 | tf_op jit(solution)/shard_map/ppermute | solution.py:532
  50.4 0.7 %collective-permute-done.4.far_state = f32[5,3,2,128]{3,2,1,0:T(2,128)S(1)} collective-permute-done((f32[5,3,2,128]{3,2,1,0:T(2,128)S(1)}, f32[5,3,2,128]{3,2,1,0:T(2,128)S(1)}, u32[]{:S(2)}, u32[]{:S(2)}) %collective-permute-start.4) | collective-permute-done | bytes 15392 | tf_op jit(solution)/shard_map/ppermute | solution.py:532
  51.1 0.5 collective-permute-done.5.near_state
  51.5 4.9 %all-to-all-done.got = f32[32,5,2,128]{3,2,1,0:T(2,128)S(1)} async-done(((f32[32,5,2,128]{3,2,1,0:T(2,128)}), f32[32,5,2,128]{3,2,1,0:T(2,128)S(1)}, u32[]{:S(2)}, u32[]{:S(2)}) %all-to-all-start) | async-done | bytes 163872 | tf_op jit(solution)/shard_map/all_to_all | solution.py:590
  56.4 1.8 %shard_map.73 = (f32[5,24,256]{2,1,0:T(8,128)}, f32[5,24,256]{2,1,0:T(8,128)}) custom-call(f32[25,24,384]{2,1,0:T(8,128)S(1)} %get-tuple-element.27.jac_own, f32[5,24,384]{2,1,0:T(8,128)S(1)} %get-tuple-element.28.rhs_own, f32[5,24,384]{2,1,0:T(8,128)S(1)} %get-tuple-element.29.scaled_own, f32[48,128]{1,0:T(8,128)S(1)} %get-tuple-element.32.low, ...), custom_call_target="tpu_custom_call" | custom-call | tf_op jit(solution)/shard_map/pallas_call | solution.py:519
Async XLA Ops:
  0.6 8.7 %copy-start = (f32[5,5,24,256]{3,2,1,0:T(8,128)S(1)}, f32[5,5,24,256]{3,2,1,0:T(8,128)}, u32[]{:S(2)}) copy-start(f32[5,5,24,256]{3,2,1,0:T(8,128)} %jac.1) | copy-start | bytes 1843204
  0.6 8.7 %copy-start.1 = (s32[24,256]{1,0:T(8,128)S(1)}, s32[24,256]{1,0:T(8,128)}, u32[]{:S(2)}) copy-start(s32[24,256]{1,0:T(8,128)} %flags.3) | copy-start | bytes 73732
  2.9 6.6 %collective-permute-start = (f32[2,24,128]{2,1,0:T(8,128)S(1)}, f32[2,24,128]{2,1,0:T(8,128)S(1)}, u32[]{:S(2)}, u32[]{:S(2)}) collective-permute-start(f32[2,24,128]{2,1,0:T(8,128)S(1)} %get-tuple-element.25), channel_id=1, source_target_pairs={{0,1},{2,3},{4,5},{6,7},{8,9},{10,11},{12,13},{14,15},{16,17},{18,... | collective-permute-start | bytes 73736 | tf_op jit(solution)/shard_map/ppermute | solution.py:532
  5.9 6.7 %collective-permute-start.1 = (f32[2,24,128]{2,1,0:T(8,128)S(1)}, f32[2,24,128]{2,1,0:T(8,128)S(1)}, u32[]{:S(2)}, u32[]{:S(2)}) collective-permute-start(f32[2,24,128]{2,1,0:T(8,128)S(1)} %get-tuple-element.26), channel_id=1, source_target_pairs={{1,2},{3,4},{5,6},{7,8},{9,10},{11,12},{13,14},{15,16},{17,18},{19... | collective-permute-start | bytes 73736 | tf_op jit(solution)/shard_map/ppermute | solution.py:532
  9.4 3.2 %copy-start.2 = (f32[5,6,64]{2,1,0:T(8,128)S(1)}, f32[5,6,64]{2,1,0:T(8,128)}, u32[]{:S(2)}) copy-start(f32[5,6,64]{2,1,0:T(8,128)} %coef.1) | copy-start | bytes 23044
  12.8 13.0 %collective-permute-start.2 = (f32[80,256]{1,0:T(8,128)S(1)}, f32[80,256]{1,0:T(8,128)S(1)}, u32[]{:S(2)}, u32[]{:S(2)}) collective-permute-start(f32[80,256]{1,0:T(8,128)S(1)} %get-tuple-element.35), channel_id=1, source_target_pairs={{24,48},{72,96},{120,144},{168,192},{216,240},{264,288},{312,336},... | collective-permute-start | bytes 245768 | tf_op jit(solution)/shard_map/ppermute | solution.py:532
  23.6 3.2 %collective-permute-start.3 = (f32[80,256]{1,0:T(8,128)S(1)}, f32[80,256]{1,0:T(8,128)S(1)}, u32[]{:S(2)}, u32[]{:S(2)}) collective-permute-start(f32[80,256]{1,0:T(8,128)S(1)} %get-tuple-element.36), channel_id=1, source_target_pairs={{0,24},{48,72},{96,120},{144,168},{192,216},{240,264},{288,312},{3... | collective-permute-start | bytes 245768 | tf_op jit(solution)/shard_map/ppermute | solution.py:532
  29.1 27.3 %all-to-all-start = ((f32[32,5,2,128]{3,2,1,0:T(2,128)}), f32[32,5,2,128]{3,2,1,0:T(2,128)S(1)}, u32[]{:S(2)}, u32[]{:S(2)}) async-start(f32[32,5,2,128]{3,2,1,0:T(2,128)} %get-tuple-element.45), calls=%async_computation | async-start | bytes 327680 | tf_op jit(solution)/shard_map/all_to_all | solution.py:590
  43.1 8.0 %collective-permute-start.4 = (f32[5,3,2,128]{3,2,1,0:T(2,128)S(1)}, f32[5,3,2,128]{3,2,1,0:T(2,128)S(1)}, u32[]{:S(2)}, u32[]{:S(2)}) collective-permute-start(f32[5,3,2,128]{3,2,1,0:T(2,128)S(1)} %get-tuple-element.43), channel_id=1, source_target_pairs={{24,48},{72,96},{120,144},{168,192},{216,240},{264,288},{312,336},... | collective-permute-start | bytes 46088 | tf_op jit(solution)/shard_map/ppermute | solution.py:532
  48.4 3.1 %collective-permute-start.5 = (f32[5,3,2,128]{3,2,1,0:T(2,128)S(1)}, f32[5,3,2,128]{3,2,1,0:T(2,128)S(1)}, u32[]{:S(2)}, u32[]{:S(2)}) collective-permute-start(f32[5,3,2,128]{3,2,1,0:T(2,128)S(1)} %get-tuple-element.44), channel_id=1, source_target_pairs={{0,24},{48,72},{96,120},{144,168},{192,216},{240,264},{288,312},{3... | collective-permute-start | bytes 46088 | tf_op jit(solution)/shard_map/ppermute | solution.py:532

commit v8 on v7

--- a/solution.py
+++ b/solution.py
@@ -231,7 +231,7 @@
 
 
 def own_kernel(
-    jac_in, rhs_in, flags, near_y, far_y, jac, rhs, scaled
+    jac_in, rhs_in, flags, near_y, far_y, jac, rhs, scaled, first, second
 ):
     near, far = [near_y[0], near_y[1]], [far_y[0], far_y[1]]
     for p in range(F * F):
@@ -243,6 +243,18 @@
     aside = unpack(near[1], far[1], F * F + F)
     code = jnp.concatenate([(flags[...] + 1).astype(F32), aside], axis=1)
     scale(code, jac, scaled)
+
+    for f in range(F):
+        first[f] = scaled[f] * rhs[f]
+    row = iota((TX, EY), 0)
+    for f in range(F):
+        own = first[f]
+        above = jnp.where(row == 0, 0.0, roll(own, 1, 0))
+        below = jnp.where(row == TX - 1, 0.0, roll(own, -1, 0))
+        total = rhs[f] + above + below + roll(own, 1, 1) + roll(own, -1, 1)
+        for g in range(F):
+            total = total - jac[F * f + g] * first[g]
+        second[f] = own + scaled[f] * total
 
 
 def residual(f, state, rhs, jac):
@@ -271,7 +283,7 @@
 
 
 def before_kernel(
-    jac_own, rhs_own, scaled_own, low, high, turn, far_x, near_x,
+    jac_own, rhs_own, scaled_own, first_own, second_own, low, high, turn, far_x, near_x,
     state, jac, rhs, scaled, value, chip, near_state, far_state, sent, other, sides, beside, means, block, sems,
 ):
     odd = parity("gx")
@@ -311,10 +323,26 @@
     jac_plane, rhs_plane = planes_of(jac_own, jac), planes_of(rhs_own, rhs)
     scaled_plane = planes_of(scaled_own, scaled)
     for f in range(F):
-        state[f] = scaled_plane(f) * rhs_plane(f)
+        state[f, TX:EX] = scaled[f] * rhs[f]
         state[f, TX + 5 : TX + 6, 0:TY] = sides[0, STATE_AT + f : STATE_AT + f + 1]
         state[f, TX + 2 : TX + 3, 0:TY] = sides[1, STATE_AT + f : STATE_AT + f + 1]
-    sweep(state, other, scaled_plane, rhs_plane, jac_plane)
+    row = iota((8, EY), 0)
+    for f in range(F):
+        beyond = state[f, TX:EX]
+        next_up, next_down = roll(beyond, 1, 0), roll(beyond, -1, 0)
+        above = jnp.where(row == 0, first_own[f, TX - 1 : TX, :], next_up)
+        below = jnp.where(row == 7, first_own[f, 0:1, :], next_down)
+        total = rhs[f] + above + below + roll(beyond, 1, 1) + roll(beyond, -1, 1)
+        for g in range(F):
+            total = total - jac[F * f + g] * state[g, TX:EX]
+        other[f, TX:EX] = beyond + scaled[f] * total
+        other[f, 0:8] = second_own[f, 0:8, :] + jnp.where(
+            row == 0, scaled_own[f, 0:8, :] * next_up, 0.0
+        )
+        other[f, 8:16] = second_own[f, 8:16, :]
+        other[f, 16:TX] = second_own[f, 16:TX, :] + jnp.where(
+            row == 7, scaled_own[f, 16:TX, :] * next_down, 0.0
+        )
     sweep(other, state, scaled_plane, rhs_plane, jac_plane)
     means[...] = jnp.zeros((8 * ROWS, EY), F32)
     for f in range(F):
@@ -564,8 +592,8 @@
     near_x = swap(near_rows, "gx", 0)
     count = lax.axis_size("gx")
     own = shape_of(F, TX, EY)
-    jac_own, rhs_own, scaled_own = call(
-        own_kernel, [shape_of(F * F, TX, EY), own, own], [], jac, rhs, flags, near_y, far_y
+    jac_own, rhs_own, scaled_own, first_own, second_own = call(
+        own_kernel, [shape_of(F * F, TX, EY), own, own, own, own], [], jac, rhs, flags, near_y, far_y
     )
     tile = pltpu.VMEM((F, EX, EY), F32)
     beyond = shape_of(F, 8, EY)
@@ -584,7 +612,7 @@
             pltpu.VMEM((min(count, 8), F, 2, 128), F32),
             pltpu.SemaphoreType.DMA((count,)),
         ],
-        jac_own, rhs_own, scaled_own, low, high, turn, far_x, near_x,
+        jac_own, rhs_own, scaled_own, first_own, second_own, low, high, turn, far_x, near_x,
         out_space=[pltpu.VMEM] * 8 + [pl.ANY],
     )
     got = lax.all_to_all(sent, "gx", 0, 0, tiled=True)

time: 58.5 us -> 58.4 us (level)
  no operation moved by 1% of the time
where the time goes in v8:
time: 58.4 us; the launch traced here: 58 us
  starting transfers between devices  40.5 us (69%)
  waiting for transfers between devices  9.78 us (17%)
  Pallas kernels  6.98 us (12%)
  between operations  0.77 us (1%)
    ppermute x6, starting transfers between devices, swap(): lax.ppermute(value, axis, [(i, i + 1) for i in firsts] + [(i + 1, i) for...  26.4 us
    all_to_all x1, starting transfers between devices, local(): got = lax.all_to_all(sent, 'gx', 0, 0, tiled=True)  14 us
    pallas_call x6, Pallas kernels, call(): pl.pallas_call(kernel, out_shape=outs, in_specs=[pl.BlockSpec(memory_spac...  6.98 us
    ppermute x6, waiting for transfers between devices, swap(): lax.ppermute(value, axis, [(i, i + 1) for i in firsts] + [(i + 1, i) for...  4.92 us
    all_to_all x1, waiting for transfers between devices, local(): got = lax.all_to_all(sent, 'gx', 0, 0, tiled=True)  4.86 us
  transfers between devices with their start and end apart: 7, of which 5 were waited for; matrix products, arithmetic and copies ran while one was open for 0% of the time, Pallas kernels for 1%

profile of v8, /device:TPU:57, one launch (start us, length us, event | category | flops | bytes accessed | tf_op | source)
XLA Modules:
  0.0 58.0 jit_solution(5596217841267341013)
XLA Ops:
  0.6 0.0 copy-start
  0.6 0.0 copy-start.1
  0.7 2.3 %shard_map.68 = (f32[5,24,256]{2,1,0:T(8,128)S(1)}, f32[2,24,128]{2,1,0:T(8,128)S(1)}, f32[2,24,128]{2,1,0:T(8,128)S(1)}) custom-call(f32[5,48,512]{2,1,0:T(8,128)} %fine_in.1, s32[48,512]{1,0:T(8,128)} %owner_in.1, s32[24,256]{1,0:T(8,128)} %flags.3, f32[5,5,24,256]{3,2,1,0:T(8,128)} %jac.1, f32[5,6,64]{2,1,0:T(8,128)} %coef.1), custom_call_target="tpu_custom_call" | custom-call | tf_op jit(solution)/shard_map/pallas_call | solution.py:547
  2.9 3.0 %collective-permute-start = (f32[2,24,128]{2,1,0:T(8,128)S(1)}, f32[2,24,128]{2,1,0:T(8,128)S(1)}, u32[]{:S(2)}, u32[]{:S(2)}) collective-permute-start(f32[2,24,128]{2,1,0:T(8,128)S(1)} %get-tuple-element.27), channel_id=1, source_target_pairs={{0,1},{2,3},{4,5},{6,7},{8,9},{10,11},{12,13},{14,15},{16,17},{18,... | collective-permute-start | bytes 73736 | tf_op jit(solution)/shard_map/ppermute | solution.py:560
  5.9 3.4 %collective-permute-start.1 = (f32[2,24,128]{2,1,0:T(8,128)S(1)}, f32[2,24,128]{2,1,0:T(8,128)S(1)}, u32[]{:S(2)}, u32[]{:S(2)}) collective-permute-start(f32[2,24,128]{2,1,0:T(8,128)S(1)} %get-tuple-element.28), channel_id=1, source_target_pairs={{1,2},{3,4},{5,6},{7,8},{9,10},{11,12},{13,14},{15,16},{17,18},{19... | collective-permute-start | bytes 73736 | tf_op jit(solution)/shard_map/ppermute | solution.py:560
  9.4 0.0 copy-done
  9.4 0.0 copy-done.1
  9.4 0.0 copy-start.2
  9.4 0.1 shard_map.70
  9.5 0.0 collective-permute-done.near_y
  9.5 3.1 %collective-permute-done.1.far_y = f32[2,24,128]{2,1,0:T(8,128)S(1)} collective-permute-done((f32[2,24,128]{2,1,0:T(8,128)S(1)}, f32[2,24,128]{2,1,0:T(8,128)S(1)}, u32[]{:S(2)}, u32[]{:S(2)}) %collective-permute-start.1) | collective-permute-done | bytes 24608 | tf_op jit(solution)/shard_map/ppermute | solution.py:560
  12.6 0.0 copy-done.2
  12.6 0.2 shard_map.71
  12.8 10.8 %collective-permute-start.2 = (f32[80,256]{1,0:T(8,128)S(1)}, f32[80,256]{1,0:T(8,128)S(1)}, u32[]{:S(2)}, u32[]{:S(2)}) collective-permute-start(f32[80,256]{1,0:T(8,128)S(1)} %get-tuple-element.39), channel_id=1, source_target_pairs={{24,48},{72,96},{120,144},{168,192},{216,240},{264,288},{312,336},... | collective-permute-start | bytes 245768 | tf_op jit(solution)/shard_map/ppermute | solution.py:560
  23.6 1.9 %collective-permute-start.3 = (f32[80,256]{1,0:T(8,128)S(1)}, f32[80,256]{1,0:T(8,128)S(1)}, u32[]{:S(2)}, u32[]{:S(2)}) collective-permute-start(f32[80,256]{1,0:T(8,128)S(1)} %get-tuple-element.40), channel_id=1, source_target_pairs={{0,24},{48,72},{96,120},{144,168},{192,216},{240,264},{288,312},{3... | collective-permute-start | bytes 245768 | tf_op jit(solution)/shard_map/ppermute | solution.py:560
  25.6 0.5 shard_map.69
  26.1 0.0 collective-permute-done.2.far_x
  26.1 0.7 %collective-permute-done.3.near_x = f32[80,256]{1,0:T(8,128)S(1)} collective-permute-done((f32[80,256]{1,0:T(8,128)S(1)}, f32[80,256]{1,0:T(8,128)S(1)}, u32[]{:S(2)}, u32[]{:S(2)}) %collective-permute-start.3) | collective-permute-done | bytes 81952 | tf_op jit(solution)/shard_map/ppermute | solution.py:560
  26.8 2.1 %shard_map.72 = (f32[5,32,384]{2,1,0:T(8,128)S(1)}, f32[25,8,384]{2,1,0:T(8,128)S(1)}, f32[5,8,384]{2,1,0:T(8,128)S(1)}, f32[5,8,384]{2,1,0:T(8,128)S(1)}, f32[4...) custom-call(f32[25,24,384]{2,1,0:T(8,128)S(1)} %get-tuple-element.29, ...), custom_call_target="tpu_custom_call" | custom-call | tf_op jit(solution)/shard_map/pallas_call | solution.py:547
  28.9 14.0 %all-to-all-start = ((f32[32,5,2,128]{3,2,1,0:T(2,128)}), f32[32,5,2,128]{3,2,1,0:T(2,128)S(1)}, u32[]{:S(2)}, u32[]{:S(2)}) async-start(f32[32,5,2,128]{3,2,1,0:T(2,128)} %get-tuple-element.49), calls=%async_computation | async-start | bytes 327680 | tf_op jit(solution)/shard_map/all_to_all | solution.py:618
  42.9 5.3 %collective-permute-start.4 = (f32[5,3,2,128]{3,2,1,0:T(2,128)S(1)}, f32[5,3,2,128]{3,2,1,0:T(2,128)S(1)}, u32[]{:S(2)}, u32[]{:S(2)}) collective-permute-start(f32[5,3,2,128]{3,2,1,0:T(2,128)S(1)} %get-tuple-element.47), channel_id=1, source_target_pairs={{24,48},{72,96},{120,144},{168,192},{216,240},{264,288},{312,336},... | collective-permute-start | bytes 46088 | tf_op jit(solution)/shard_map/ppermute | solution.py:560
  48.3 1.9 %collective-permute-start.5 = (f32[5,3,2,128]{3,2,1,0:T(2,128)S(1)}, f32[5,3,2,128]{3,2,1,0:T(2,128)S(1)}, u32[]{:S(2)}, u32[]{:S(2)}) collective-permute-start(f32[5,3,2,128]{3,2,1,0:T(2,128)S(1)} %get-tuple-element.48), channel_id=1, source_target_pairs={{0,24},{48,72},{96,120},{144,168},{192,216},{240,264},{288,312},{3... | collective-permute-start | bytes 46088 | tf_op jit(solution)/shard_map/ppermute | solution.py:560
  50.2 0.7 %collective-permute-done.4.far_state = f32[5,3,2,128]{3,2,1,0:T(2,128)S(1)} collective-permute-done((f32[5,3,2,128]{3,2,1,0:T(2,128)S(1)}, f32[5,3,2,128]{3,2,1,0:T(2,128)S(1)}, u32[]{:S(2)}, u32[]{:S(2)}) %collective-permute-start.4) | collective-permute-done | bytes 15392 | tf_op jit(solution)/shard_map/ppermute | solution.py:560
  50.9 0.5 collective-permute-done.5.near_state
  51.3 4.9 %all-to-all-done.got = f32[32,5,2,128]{3,2,1,0:T(2,128)S(1)} async-done(((f32[32,5,2,128]{3,2,1,0:T(2,128)}), f32[32,5,2,128]{3,2,1,0:T(2,128)S(1)}, u32[]{:S(2)}, u32[]{:S(2)}) %all-to-all-start) | async-done | bytes 163872 | tf_op jit(solution)/shard_map/all_to_all | solution.py:618
  56.2 1.8 %shard_map.73 = (f32[5,24,256]{2,1,0:T(8,128)}, f32[5,24,256]{2,1,0:T(8,128)}) custom-call(f32[25,24,384]{2,1,0:T(8,128)S(1)} %get-tuple-element.29.jac_own, f32[5,24,384]{2,1,0:T(8,128)S(1)} %get-tuple-element.30.rhs_own, f32[5,24,384]{2,1,0:T(8,128)S(1)} %get-tuple-element.31.scaled_own, f32[48,128]{1,0:T(8,128)S(1)} %get-tuple-element.34.low, ...), custom_call_target="tpu_custom_call" | custom-call | tf_op jit(solution)/shard_map/pallas_call | solution.py:547
Async XLA Ops:
  0.6 8.7 %copy-start = (f32[5,5,24,256]{3,2,1,0:T(8,128)S(1)}, f32[5,5,24,256]{3,2,1,0:T(8,128)}, u32[]{:S(2)}) copy-start(f32[5,5,24,256]{3,2,1,0:T(8,128)} %jac.1) | copy-start | bytes 1843204
  0.6 8.7 %copy-start.1 = (s32[24,256]{1,0:T(8,128)S(1)}, s32[24,256]{1,0:T(8,128)}, u32[]{:S(2)}) copy-start(s32[24,256]{1,0:T(8,128)} %flags.3) | copy-start | bytes 73732
  2.9 6.6 %collective-permute-start = (f32[2,24,128]{2,1,0:T(8,128)S(1)}, f32[2,24,128]{2,1,0:T(8,128)S(1)}, u32[]{:S(2)}, u32[]{:S(2)}) collective-permute-start(f32[2,24,128]{2,1,0:T(8,128)S(1)} %get-tuple-element.27), channel_id=1, source_target_pairs={{0,1},{2,3},{4,5},{6,7},{8,9},{10,11},{12,13},{14,15},{16,17},{18,... | collective-permute-start | bytes 73736 | tf_op jit(solution)/shard_map/ppermute | solution.py:560
  5.9 6.7 %collective-permute-start.1 = (f32[2,24,128]{2,1,0:T(8,128)S(1)}, f32[2,24,128]{2,1,0:T(8,128)S(1)}, u32[]{:S(2)}, u32[]{:S(2)}) collective-permute-start(f32[2,24,128]{2,1,0:T(8,128)S(1)} %get-tuple-element.28), channel_id=1, source_target_pairs={{1,2},{3,4},{5,6},{7,8},{9,10},{11,12},{13,14},{15,16},{17,18},{19... | collective-permute-start | bytes 73736 | tf_op jit(solution)/shard_map/ppermute | solution.py:560
  9.4 3.2 %copy-start.2 = (f32[5,6,64]{2,1,0:T(8,128)S(1)}, f32[5,6,64]{2,1,0:T(8,128)}, u32[]{:S(2)}) copy-start(f32[5,6,64]{2,1,0:T(8,128)} %coef.1) | copy-start | bytes 23044
  12.8 13.3 %collective-permute-start.2 = (f32[80,256]{1,0:T(8,128)S(1)}, f32[80,256]{1,0:T(8,128)S(1)}, u32[]{:S(2)}, u32[]{:S(2)}) collective-permute-start(f32[80,256]{1,0:T(8,128)S(1)} %get-tuple-element.39), channel_id=1, source_target_pairs={{24,48},{72,96},{120,144},{168,192},{216,240},{264,288},{312,336},... | collective-permute-start | bytes 245768 | tf_op jit(solution)/shard_map/ppermute | solution.py:560
  23.6 3.2 %collective-permute-start.3 = (f32[80,256]{1,0:T(8,128)S(1)}, f32[80,256]{1,0:T(8,128)S(1)}, u32[]{:S(2)}, u32[]{:S(2)}) collective-permute-start(f32[80,256]{1,0:T(8,128)S(1)} %get-tuple-element.40), channel_id=1, source_target_pairs={{0,24},{48,72},{96,120},{144,168},{192,216},{240,264},{288,312},{3... | collective-permute-start | bytes 245768 | tf_op jit(solution)/shard_map/ppermute | solution.py:560
  28.9 27.3 %all-to-all-start = ((f32[32,5,2,128]{3,2,1,0:T(2,128)}), f32[32,5,2,128]{3,2,1,0:T(2,128)S(1)}, u32[]{:S(2)}, u32[]{:S(2)}) async-start(f32[32,5,2,128]{3,2,1,0:T(2,128)} %get-tuple-element.49), calls=%async_computation | async-start | bytes 327680 | tf_op jit(solution)/shard_map/all_to_all | solution.py:618
  42.9 7.9 %collective-permute-start.4 = (f32[5,3,2,128]{3,2,1,0:T(2,128)S(1)}, f32[5,3,2,128]{3,2,1,0:T(2,128)S(1)}, u32[]{:S(2)}, u32[]{:S(2)}) collective-permute-start(f32[5,3,2,128]{3,2,1,0:T(2,128)S(1)} %get-tuple-element.47), channel_id=1, source_target_pairs={{24,48},{72,96},{120,144},{168,192},{216,240},{264,288},{312,336},... | collective-permute-start | bytes 46088 | tf_op jit(solution)/shard_map/ppermute | solution.py:560
  48.3 3.1 %collective-permute-start.5 = (f32[5,3,2,128]{3,2,1,0:T(2,128)S(1)}, f32[5,3,2,128]{3,2,1,0:T(2,128)S(1)}, u32[]{:S(2)}, u32[]{:S(2)}) collective-permute-start(f32[5,3,2,128]{3,2,1,0:T(2,128)S(1)} %get-tuple-element.48), channel_id=1, source_target_pairs={{0,24},{48,72},{96,120},{144,168},{192,216},{240,264},{288,312},{3... | collective-permute-start | bytes 46088 | tf_op jit(solution)/shard_map/ppermute | solution.py:560

commit v9 on v8

--- a/solution.py
+++ b/solution.py
@@ -166,17 +166,23 @@
         write(far, True)
 
 
-def corners_kernel(near_rows, far_rows, coef, near_y, far_y, near, far, low, high, turn, diag):
-    odd = parity("gx")
-    near[...] = near_rows[...]
-    far[...] = far_rows[...]
+def put_corners(out, first_rows, near_y, far_y):
     for side, strip in enumerate((far_y, near_y)):
         at = CORNER_AT + 3 * side
         for a in range(2):
             lanes = slice(128 * a, 128 * (a + 1))
             first, last = strip[a, 0:3, :], strip[a, TX - 3 : TX, :]
-            near[at : at + 3, lanes] = jnp.where(odd, first, last)
-            far[at : at + 3, lanes] = jnp.where(odd, last, first)
+            out[at : at + 3, lanes] = jnp.where(first_rows, first, last)
+
+
+def far_kernel(far_rows, near_y, far_y, far):
+    far[...] = far_rows[...]
+    put_corners(far, jnp.logical_not(parity("gx")), near_y, far_y)
+
+
+def near_kernel(near_rows, coef, near_y, far_y, near, low, high, turn, diag):
+    near[...] = near_rows[...]
+    put_corners(near, parity("gx"), near_y, far_y)
 
     lane = iota((ROWS, 128), 1)
     odd_y = parity("gy")
@@ -582,13 +588,14 @@
     far_y = swap(far, "gy", 1)
     near_y = swap(near, "gy", 0)
     rows, lines, line = shape_of(ROWS_SENT, TY), shape_of(8 * ROWS, 128), shape_of(8, 128)
-    near_rows, far_rows, low, high, turn = call(
-        corners_kernel,
-        [rows, rows, lines, lines, line],
+    (far_rows,) = call(far_kernel, [rows], [], far_rows, near_y, far_y)
+    far_x = swap(far_rows, "gx", 1)
+    near_rows, low, high, turn = call(
+        near_kernel,
+        [rows, lines, lines, line],
         [pltpu.VMEM((8 * ROWS, 128), F32)],
-        near_rows, far_rows, coef, near_y, far_y,
-    )
-    far_x = swap(far_rows, "gx", 1)
+        near_rows, coef, near_y, far_y,
+    )
     near_x = swap(near_rows, "gx", 0)
     count = lax.axis_size("gx")
     own = shape_of(F, TX, EY)

time: 58.4 us -> 58.5 us (level)
    pallas_call x6 -> x7, Pallas kernels: 6.98 us -> 6.97 us  [call(): pl.pallas_call(kernel, out_shape=outs, in_specs=[pl.BlockSpec(memory_spac...]
  transfers between devices with their start and end apart: 7 -> 7, of which waited for: 5 -> 4; matrix products, arithmetic and copies ran while one was open for 0% -> 0% of each run, Pallas kernels for 1% -> 1%
where the time goes in v9:
time: 58.5 us; the launch traced here: 58.1 us
  starting transfers between devices  40.4 us (69%)
  waiting for transfers between devices  9.92 us (17%)
  Pallas kernels  6.97 us (12%)
  between operations  0.79 us (1%)
    ppermute x6, starting transfers between devices, swap(): lax.ppermute(value, axis, [(i, i + 1) for i in firsts] + [(i + 1, i) for...  26.4 us
    all_to_all x1, starting transfers between devices, local(): got = lax.all_to_all(sent, 'gx', 0, 0, tiled=True)  14 us
    pallas_call x7, Pallas kernels, call(): pl.pallas_call(kernel, out_shape=outs, in_specs=[pl.BlockSpec(memory_spac...  6.97 us
    all_to_all x1, waiting for transfers between devices, local(): got = lax.all_to_all(sent, 'gx', 0, 0, tiled=True)  4.97 us
    ppermute x6, waiting for transfers between devices, swap(): lax.ppermute(value, axis, [(i, i + 1) for i in firsts] + [(i + 1, i) for...  4.95 us
  transfers between devices with their start and end apart: 7, of which 4 were waited for; matrix products, arithmetic and copies ran while one was open for 0% of the time, Pallas kernels for 1%

profile of v9, /device:TPU:57, one launch (start us, length us, event | category | flops | bytes accessed | tf_op | source)
XLA Modules:
  0.0 58.1 jit_solution(14415754085169190491)
XLA Ops:
  0.6 0.0 copy-start
  0.6 0.0 copy-start.1
  0.7 2.3 %shard_map.68 = (f32[5,24,256]{2,1,0:T(8,128)S(1)}, f32[2,24,128]{2,1,0:T(8,128)S(1)}, f32[2,24,128]{2,1,0:T(8,128)S(1)}) custom-call(f32[5,48,512]{2,1,0:T(8,128)} %fine_in.1, s32[48,512]{1,0:T(8,128)} %owner_in.1, s32[24,256]{1,0:T(8,128)} %flags.3, f32[5,5,24,256]{3,2,1,0:T(8,128)} %jac.1, f32[5,6,64]{2,1,0:T(8,128)} %coef.1), custom_call_target="tpu_custom_call" | custom-call | tf_op jit(solution)/shard_map/pallas_call | solution.py:553
  2.9 3.0 %collective-permute-start = (f32[2,24,128]{2,1,0:T(8,128)S(1)}, f32[2,24,128]{2,1,0:T(8,128)S(1)}, u32[]{:S(2)}, u32[]{:S(2)}) collective-permute-start(f32[2,24,128]{2,1,0:T(8,128)S(1)} %get-tuple-element.26), channel_id=1, source_target_pairs={{0,1},{2,3},{4,5},{6,7},{8,9},{10,11},{12,13},{14,15},{16,17},{18,... | collective-permute-start | bytes 73736 | tf_op jit(solution)/shard_map/ppermute | solution.py:566
  5.9 3.4 %collective-permute-start.1 = (f32[2,24,128]{2,1,0:T(8,128)S(1)}, f32[2,24,128]{2,1,0:T(8,128)S(1)}, u32[]{:S(2)}, u32[]{:S(2)}) collective-permute-start(f32[2,24,128]{2,1,0:T(8,128)S(1)} %get-tuple-element.27), channel_id=1, source_target_pairs={{1,2},{3,4},{5,6},{7,8},{9,10},{11,12},{13,14},{15,16},{17,18},{19... | collective-permute-start | bytes 73736 | tf_op jit(solution)/shard_map/ppermute | solution.py:566
  9.4 0.0 copy-done
  9.4 0.0 copy-done.1
  9.4 0.1 shard_map.70
  9.5 0.0 collective-permute-done.near_y
  9.5 3.1 %collective-permute-done.1.far_y = f32[2,24,128]{2,1,0:T(8,128)S(1)} collective-permute-done((f32[2,24,128]{2,1,0:T(8,128)S(1)}, f32[2,24,128]{2,1,0:T(8,128)S(1)}, u32[]{:S(2)}, u32[]{:S(2)}) %collective-permute-start.1) | collective-permute-done | bytes 24608 | tf_op jit(solution)/shard_map/ppermute | solution.py:566
  12.6 0.0 copy-start.2
  12.6 10.8 %collective-permute-start.2 = (f32[80,256]{1,0:T(8,128)S(1)}, f32[80,256]{1,0:T(8,128)S(1)}, u32[]{:S(2)}, u32[]{:S(2)}) collective-permute-start(f32[80,256]{1,0:T(8,128)S(1)} %shard_map.72), channel_id=1, source_target_pairs={{24,48},{72,96},{120,144},{168,192},{216,240},{264,288},{312,336},... | collective-permute-start | bytes 245768 | tf_op jit(solution)/shard_map/ppermute | solution.py:566
  23.4 0.0 copy-done.2
  23.5 0.2 shard_map.71
  23.7 1.9 %collective-permute-start.3 = (f32[80,256]{1,0:T(8,128)S(1)}, f32[80,256]{1,0:T(8,128)S(1)}, u32[]{:S(2)}, u32[]{:S(2)}) collective-permute-start(f32[80,256]{1,0:T(8,128)S(1)} %get-tuple-element.38), channel_id=1, source_target_pairs={{0,24},{48,72},{96,120},{144,168},{192,216},{240,264},{288,312},{3... | collective-permute-start | bytes 245768 | tf_op jit(solution)/shard_map/ppermute | solution.py:566
  25.6 0.5 shard_map.69
  26.1 0.0 collective-permute-done.2.far_x
  26.1 0.7 %collective-permute-done.3.near_x = f32[80,256]{1,0:T(8,128)S(1)} collective-permute-done((f32[80,256]{1,0:T(8,128)S(1)}, f32[80,256]{1,0:T(8,128)S(1)}, u32[]{:S(2)}, u32[]{:S(2)}) %collective-permute-start.3) | collective-permute-done | bytes 81952 | tf_op jit(solution)/shard_map/ppermute | solution.py:566
  26.8 2.1 %shard_map.73 = (f32[5,32,384]{2,1,0:T(8,128)S(1)}, f32[25,8,384]{2,1,0:T(8,128)S(1)}, f32[5,8,384]{2,1,0:T(8,128)S(1)}, f32[5,8,384]{2,1,0:T(8,128)S(1)}, f32[4...) custom-call(f32[25,24,384]{2,1,0:T(8,128)S(1)} %get-tuple-element.28, ...), custom_call_target="tpu_custom_call" | custom-call | tf_op jit(solution)/shard_map/pallas_call | solution.py:553
  28.9 14.0 %all-to-all-start = ((f32[32,5,2,128]{3,2,1,0:T(2,128)}), f32[32,5,2,128]{3,2,1,0:T(2,128)S(1)}, u32[]{:S(2)}, u32[]{:S(2)}) async-start(f32[32,5,2,128]{3,2,1,0:T(2,128)} %get-tuple-element.47), calls=%async_computation | async-start | bytes 327680 | tf_op jit(solution)/shard_map/all_to_all | solution.py:625
  42.9 5.3 %collective-permute-start.4 = (f32[5,3,2,128]{3,2,1,0:T(2,128)S(1)}, f32[5,3,2,128]{3,2,1,0:T(2,128)S(1)}, u32[]{:S(2)}, u32[]{:S(2)}) collective-permute-start(f32[5,3,2,128]{3,2,1,0:T(2,128)S(1)} %get-tuple-element.45), channel_id=1, source_target_pairs={{24,48},{72,96},{120,144},{168,192},{216,240},{264,288},{312,336},... | collective-permute-start | bytes 46088 | tf_op jit(solution)/shard_map/ppermute | solution.py:566
  48.3 1.9 %collective-permute-start.5 = (f32[5,3,2,128]{3,2,1,0:T(2,128)S(1)}, f32[5,3,2,128]{3,2,1,0:T(2,128)S(1)}, u32[]{:S(2)}, u32[]{:S(2)}) collective-permute-start(f32[5,3,2,128]{3,2,1,0:T(2,128)S(1)} %get-tuple-element.46), channel_id=1, source_target_pairs={{0,24},{48,72},{96,120},{144,168},{192,216},{240,264},{288,312},{3... | collective-permute-start | bytes 46088 | tf_op jit(solution)/shard_map/ppermute | solution.py:566
  50.2 0.0 collective-permute-done.4.far_state
  50.2 1.1 %collective-permute-done.5.near_state = f32[5,3,2,128]{3,2,1,0:T(2,128)S(1)} collective-permute-done((f32[5,3,2,128]{3,2,1,0:T(2,128)S(1)}, f32[5,3,2,128]{3,2,1,0:T(2,128)S(1)}, u32[]{:S(2)}, u32[]{:S(2)}) %collective-permute-start.5) | collective-permute-done | bytes 15392 | tf_op jit(solution)/shard_map/ppermute | solution.py:566
  51.3 5.0 %all-to-all-done.got = f32[32,5,2,128]{3,2,1,0:T(2,128)S(1)} async-done(((f32[32,5,2,128]{3,2,1,0:T(2,128)}), f32[32,5,2,128]{3,2,1,0:T(2,128)S(1)}, u32[]{:S(2)}, u32[]{:S(2)}) %all-to-all-start) | async-done | bytes 163872 | tf_op jit(solution)/shard_map/all_to_all | solution.py:625
  56.3 1.8 %shard_map.74 = (f32[5,24,256]{2,1,0:T(8,128)}, f32[5,24,256]{2,1,0:T(8,128)}) custom-call(f32[25,24,384]{2,1,0:T(8,128)S(1)} %get-tuple-element.28.jac_own, f32[5,24,384]{2,1,0:T(8,128)S(1)} %get-tuple-element.29.rhs_own, f32[5,24,384]{2,1,0:T(8,128)S(1)} %get-tuple-element.30.scaled_own, f32[48,128]{1,0:T(8,128)S(1)} %get-tuple-element.32.low, ...), custom_call_target="tpu_custom_call" | custom-call | tf_op jit(solution)/shard_map/pallas_call | solution.py:553
  (1 shorter events, 0.0 us)
Async XLA Ops:
  0.6 8.7 %copy-start = (f32[5,5,24,256]{3,2,1,0:T(8,128)S(1)}, f32[5,5,24,256]{3,2,1,0:T(8,128)}, u32[]{:S(2)}) copy-start(f32[5,5,24,256]{3,2,1,0:T(8,128)} %jac.1) | copy-start | bytes 1843204
  0.6 8.7 %copy-start.1 = (s32[24,256]{1,0:T(8,128)S(1)}, s32[24,256]{1,0:T(8,128)}, u32[]{:S(2)}) copy-start(s32[24,256]{1,0:T(8,128)} %flags.3) | copy-start | bytes 73732
  2.9 6.6 %collective-permute-start = (f32[2,24,128]{2,1,0:T(8,128)S(1)}, f32[2,24,128]{2,1,0:T(8,128)S(1)}, u32[]{:S(2)}, u32[]{:S(2)}) collective-permute-start(f32[2,24,128]{2,1,0:T(8,128)S(1)} %get-tuple-element.26), channel_id=1, source_target_pairs={{0,1},{2,3},{4,5},{6,7},{8,9},{10,11},{12,13},{14,15},{16,17},{18,... | collective-permute-start | bytes 73736 | tf_op jit(solution)/shard_map/ppermute | solution.py:566
  5.9 6.7 %collective-permute-start.1 = (f32[2,24,128]{2,1,0:T(8,128)S(1)}, f32[2,24,128]{2,1,0:T(8,128)S(1)}, u32[]{:S(2)}, u32[]{:S(2)}) collective-permute-start(f32[2,24,128]{2,1,0:T(8,128)S(1)} %get-tuple-element.27), channel_id=1, source_target_pairs={{1,2},{3,4},{5,6},{7,8},{9,10},{11,12},{13,14},{15,16},{17,18},{19... | collective-permute-start | bytes 73736 | tf_op jit(solution)/shard_map/ppermute | solution.py:566
  12.6 10.9 %copy-start.2 = (f32[5,6,64]{2,1,0:T(8,128)S(1)}, f32[5,6,64]{2,1,0:T(8,128)}, u32[]{:S(2)}) copy-start(f32[5,6,64]{2,1,0:T(8,128)} %coef.1) | copy-start | bytes 23044
  12.6 13.5 %collective-permute-start.2 = (f32[80,256]{1,0:T(8,128)S(1)}, f32[80,256]{1,0:T(8,128)S(1)}, u32[]{:S(2)}, u32[]{:S(2)}) collective-permute-start(f32[80,256]{1,0:T(8,128)S(1)} %shard_map.72), channel_id=1, source_target_pairs={{24,48},{72,96},{120,144},{168,192},{216,240},{264,288},{312,336},... | collective-permute-start | bytes 245768 | tf_op jit(solution)/shard_map/ppermute | solution.py:566
  23.7 3.2 %collective-permute-start.3 = (f32[80,256]{1,0:T(8,128)S(1)}, f32[80,256]{1,0:T(8,128)S(1)}, u32[]{:S(2)}, u32[]{:S(2)}) collective-permute-start(f32[80,256]{1,0:T(8,128)S(1)} %get-tuple-element.38), channel_id=1, source_target_pairs={{0,24},{48,72},{96,120},{144,168},{192,216},{240,264},{288,312},{3... | collective-permute-start | bytes 245768 | tf_op jit(solution)/shard_map/ppermute | solution.py:566
  28.9 27.4 %all-to-all-start = ((f32[32,5,2,128]{3,2,1,0:T(2,128)}), f32[32,5,2,128]{3,2,1,0:T(2,128)S(1)}, u32[]{:S(2)}, u32[]{:S(2)}) async-start(f32[32,5,2,128]{3,2,1,0:T(2,128)} %get-tuple-element.47), calls=%async_computation | async-start | bytes 327680 | tf_op jit(solution)/shard_map/all_to_all | solution.py:625
  42.9 7.3 %collective-permute-start.4 = (f32[5,3,2,128]{3,2,1,0:T(2,128)S(1)}, f32[5,3,2,128]{3,2,1,0:T(2,128)S(1)}, u32[]{:S(2)}, u32[]{:S(2)}) collective-permute-start(f32[5,3,2,128]{3,2,1,0:T(2,128)S(1)} %get-tuple-element.45), channel_id=1, source_target_pairs={{24,48},{72,96},{120,144},{168,192},{216,240},{264,288},{312,336},... | collective-permute-start | bytes 46088 | tf_op jit(solution)/shard_map/ppermute | solution.py:566
  48.3 3.1 %collective-permute-start.5 = (f32[5,3,2,128]{3,2,1,0:T(2,128)S(1)}, f32[5,3,2,128]{3,2,1,0:T(2,128)S(1)}, u32[]{:S(2)}, u32[]{:S(2)}) collective-permute-start(f32[5,3,2,128]{3,2,1,0:T(2,128)S(1)} %get-tuple-element.46), channel_id=1, source_target_pairs={{0,24},{48,72},{96,120},{144,168},{192,216},{240,264},{288,312},{3... | collective-permute-start | bytes 46088 | tf_op jit(solution)/shard_map/ppermute | solution.py:566
